TPU v7x, 256 devices: a whole 4x4x8 slice. The times are simulated.
256 devices in a mesh: blk: 32 (over z_lo, y, core), tp: 8 (over z_hi, x).
Axes of the slice: x: 4, y: 4, z: 8 (z_hi: 2, z_lo: 4; z = z_hi * 4 + z_lo), core: 2. Of those that a mesh axis runs over, the one named last changes fastest.
Arguments:
- queries: bfloat16 [16384, 8192], P('blk', 'tp'), may hold values from -4.5 to 4.5
- leaf_kv: bfloat16 [2, 16384, 1024], P(None, 'blk', 'tp'), may hold values from -9 to 9
- root_kv: bfloat16 [2, 2048, 1024], P(None, ('blk', 'tp')), may hold values from -4.5 to 4.5
- node_kv: bfloat16 [2, 128, 256, 1024], P(None, 'blk', None, 'tp'), may hold values from -9 to 9
- node_len: int32 [128], replicated, may hold values from 64 to 256, as said below
- node_slot: int32 [128], replicated, may hold values from 0 to 127, each once
- slot_leaf: int32 [32], replicated, may hold values from 0 to 31, each once
- ancestors: int32 [32, 2], replicated, may hold values from 0 to 127, as said below
Outputs:
- attended: bfloat16 [16384, 8192], P('blk', 'tp')
Inputs may be any that keep to these rules, and one draw needn't show every extreme that they name: `node_len`: every node has 64 or more tokens; some node has exactly 256. `ancestors`: column 0 holds a branch node id below 32, column 1 a twig node id of 32 or more; all leaves with one twig name the same branch; leaves per twig vary widely.
All inputs are finite; a program needn't handle non-finite values.
Results may differ from a plain program's by a relative error of at most 0.0065.
Values may be sent and summed in bfloat16 or wider, within the bound.
No kernel may reach another device: no remote copies, remote signals or barrier semaphores. Data moves between devices by JAX's collectives and lax.ppermute only.
A program may use at most 128 MiB of HBM per device.

v0:
```python
import jax
import jax.numpy as jnp
from jax import lax
from jax.sharding import PartitionSpec as P

HD = 128
LEAF_LEN = 512
NODE_LEN = 256


masked_score = -1e30


def attend(carry_state, query_rows, key_rows, value_rows, visible, paired):
    running_max, running_sum, weighted = carry_state
    score_scale = query_rows.shape[-1] ** (-0.5)
    if paired:
        scores = jnp.einsum(
            "lqkgd,lnkd->lqkgn", query_rows, key_rows, preferred_element_type=jnp.float32
        )
    else:
        scores = jnp.einsum(
            "lqkgd,nkd->lqkgn", query_rows, key_rows, preferred_element_type=jnp.float32
        )
    scores = scores * score_scale
    shown = visible[:, :, None, None, :]
    scores = jnp.where(shown, scores, masked_score)
    new_max = jnp.maximum(running_max, jnp.max(scores, -1))
    weights = jnp.where(shown, jnp.exp(scores - new_max[..., None]), 0.0)
    rescale = jnp.exp(running_max - new_max)
    running_sum = running_sum * rescale + jnp.sum(weights, -1)
    rounded = weights.astype(jnp.bfloat16)
    if paired:
        contrib = jnp.einsum(
            "lqkgn,lnkd->lqkgd", rounded, value_rows, preferred_element_type=jnp.float32
        )
    else:
        contrib = jnp.einsum(
            "lqkgn,nkd->lqkgd", rounded, value_rows, preferred_element_type=jnp.float32
        )
    weighted = weighted * rescale[..., None] + contrib
    return (new_max, running_sum, weighted)


def attend_blocks(carry_state, query_rows, key_rows, value_rows, visible, paired):
    key_axis = 1 if paired else 0
    key_count = key_rows.shape[key_axis]
    block = 512
    full_blocks = key_count // block

    def one_block(index, current):
        lower = (index * block).astype(jnp.int32)
        part_keys = lax.dynamic_slice_in_dim(key_rows, lower, block, key_axis)
        part_values = lax.dynamic_slice_in_dim(value_rows, lower, block, key_axis)
        part_visible = lax.dynamic_slice_in_dim(visible, lower, block, 2)
        return attend(current, query_rows, part_keys, part_values, part_visible, paired)

    carry_state = lax.fori_loop(0, full_blocks, one_block, carry_state)
    lower = full_blocks * block
    return carry_state


def per_device(queries, leaf_kv, root_kv, node_kv, node_len, node_slot, slot_leaf, ancestors):
    row_count = queries.shape[0]
    leaf_dev = row_count // LEAF_LEN
    kv_dev = leaf_kv.shape[2] // HD
    head_width = kv_dev * HD
    group = queries.shape[1] // head_width
    query_rows = queries.reshape(leaf_dev, LEAF_LEN, kv_dev, group, HD)
    carry_state = (
        jnp.full((leaf_dev, LEAF_LEN, kv_dev, group), masked_score, jnp.float32),
        jnp.zeros((leaf_dev, LEAF_LEN, kv_dev, group), jnp.float32),
        jnp.zeros((leaf_dev, LEAF_LEN, kv_dev, group, HD), jnp.float32),
    )
    own_cache = leaf_kv.reshape(2, leaf_dev, LEAF_LEN, kv_dev, HD)
    causal = jnp.arange(LEAF_LEN)[:, None] >= jnp.arange(LEAF_LEN)[None, :]
    carry_state = attend_blocks(
        carry_state, query_rows, own_cache[0], own_cache[1], causal[None], True
    )
    tp_index = lax.axis_index("tp")
    my_heads = lax.dynamic_slice_in_dim(
        lax.all_gather(root_kv, ("blk", "tp"), axis=1, tiled=True),
        tp_index * head_width,
        head_width,
        2,
    )
    key_count = my_heads.shape[1]
    key_rows = my_heads[0].reshape(key_count, kv_dev, HD)
    value_rows = my_heads[1].reshape(key_count, kv_dev, HD)
    everywhere = jnp.ones((1, 1, key_count), dtype=bool)
    carry_state = attend_blocks(carry_state, query_rows, key_rows, value_rows, everywhere, False)
    blk_index = lax.axis_index("blk")
    leaf_total = slot_leaf.shape[0]
    positions = jnp.arange(NODE_LEN, dtype=jnp.int32)
    depth = ancestors.shape[1]
    wanted = leaf_dev * depth
    node_total = node_slot.shape[0]
    slots = blk_index * leaf_dev + jnp.arange(leaf_dev, dtype=jnp.int32)
    leaf_range = jnp.arange(leaf_total, dtype=jnp.int32)
    leaf_ids = jnp.sum(jnp.where(slots[:, None] == leaf_range[None, :], slot_leaf[None, :], 0), 1)
    matches = leaf_ids[:, None] == leaf_range[None, :]
    lineage = jnp.sum(jnp.where(matches[:, :, None], ancestors[None, :, :], 0), 1)
    by_node = lineage[:, :, None] == jnp.arange(node_total, dtype=jnp.int32)[None, None, :]
    stored_at = jnp.sum(jnp.where(by_node, node_slot[None, None, :], 0), 2)
    lengths = jnp.sum(jnp.where(by_node, node_len[None, None, :], 0), 2)
    within = positions[None, None, :] < lengths[:, :, None]
    pieces = lax.all_gather(node_kv, "blk", axis=1, tiled=True)
    node_count = pieces.shape[1]
    inside = (stored_at >= 0) & (stored_at < node_count)
    picked_index = jnp.clip(stored_at, 0, node_count - 1).reshape(wanted)
    picked = jnp.take(pieces, picked_index, axis=1)
    picked = picked.reshape(2, leaf_dev, depth * NODE_LEN, kv_dev, HD)
    visible = (inside[:, :, None] & within).reshape(leaf_dev, 1, depth * NODE_LEN)

    def use_nodes(current):
        return attend_blocks(current, query_rows, picked[0], picked[1], visible, True)

    def skip_nodes(current):
        return current

    carry_state = lax.cond(jnp.any(inside), use_nodes, skip_nodes, carry_state)
    running_max, running_sum, weighted = carry_state
    result = weighted / running_sum[..., None]
    return result.reshape(row_count, group * head_width).astype(jnp.bfloat16)


def solution(mesh):
    placed = (
        P("blk", "tp"),
        P(None, "blk", "tp"),
        P(None, ("blk", "tp"), None),
        P(None, "blk", None, "tp"),
        P(),
        P(),
        P(),
        P(),
    )
    return jax.shard_map(
        per_device, mesh=mesh, in_specs=placed, out_specs=P("blk", "tp"), check_vma=False
    )
```

profile of v0, /device:TPU:1, one launch (start us, length us, event | category | flops | bytes accessed | tf_op | source)
XLA Modules:
  0.0 856.7 jit_solution(117036734549285043)
XLA Ops:
  6.5 0.0 all-gather.3.cloned.1.call-start
  6.5 0.7 all-gather.3.cloned.1.call-update
  7.3 0.0 all-gather.5.cloned.1.call-start
  7.3 0.7 all-gather.5.cloned.1.call-update
  8.0 1.3 fusion.55
  9.3 0.6 iota_compare_fusion.2
  10.0 0.8 select_reduce_fusion.2
  10.8 0.8 select_reduce_fusion.1
  11.6 0.6 and_reduce_fusion
  12.9 2.3 copy.27
  15.2 0.1 iota_compare_fusion
  15.2 2.9 fusion.38
  18.1 0.0 copy-start
  18.1 3.2 copy-done
  21.3 0.0 copy-done.1
  21.3 3.9 fusion.45
  25.2 1.9 copy.28
  27.1 1.6 copy.29
  28.7 0.1 iota_compare_fusion.1
  28.8 4.5 fusion.40
  33.3 698.6 %all-gather.3.cloned.1.call-done = bf16[2,2048,1024]{2,1,0:T(8,128)(2,1)} async-done(((bf16[2,8,1024]{2,1,0:T(8,128)(2,1)}), bf16[2,2048,1024]{2,1,0:T(8,128)(2,1)}) %all-gather.3.cloned.1.call-update) | async-done | bytes 8388624 | tf_op jit(solution)/shard_map/all_gather | solution.py:82
  731.9 2.4 dynamic-slice_bitcast_fusion
  734.2 26.7 %while.4 = (s32[]{:T(128)}, f32[1,512,1,8]{1,3,2,0:T(8,128)S(1)}, f32[1,512,1,8]{1,3,2,0:T(8,128)S(1)}, f32[1,512,1,8,128]{1,4,3,0,2:T(8,128)S(1)}, bf16[2048,1,...) while((s32[]{:T(128)}, f32[1,512,1,8]{1,3,2,0:T(8,128)S(1)}, ...), condition=%wide.region_9.10_spmd, body=%wide.region_6.9_spmd.sunk | while | flops 1091579904 | bytes 30933164 | solution.py:58
  734.2 2.2 bitcast_reduce_fusion.3
  736.4 1.4 fusion.68
  737.9 3.0 bitcast_add_fusion.9
  740.9 2.2 bitcast_reduce_fusion.3
  743.1 1.4 fusion.68
  744.5 3.1 bitcast_add_fusion.9
  747.6 2.2 bitcast_reduce_fusion.3
  749.8 1.4 fusion.68
  751.2 3.0 bitcast_add_fusion.9
  754.3 2.2 bitcast_reduce_fusion.3
  756.5 1.4 fusion.68
  757.9 3.0 bitcast_add_fusion.9
  760.9 72.5 %all-gather.5.cloned.1.call-done = bf16[2,128,256,128]{3,2,1,0:T(8,128)(2,1)} async-done(((bf16[2,4,256,128]{3,2,1,0:T(8,128)(2,1)}), bf16[2,128,256,128]{3,2,1,0:T(8,128)(2,1)}) %all-gather.5.cloned.1.call-update) | async-done | bytes 16777232 | tf_op jit(solution)/shard_map/all_gather | solution.py:107
  833.4 14.8 %conditional.1 = (f32[1,512,1,8]{1,3,2,0:T(8,128)S(1)}, f32[1,512,1,8,128]{1,4,3,2,0:T(8,128)S(1)}) conditional(s32[]{:T(128)} %convert_element_type.28, (f32[1,512,1,8]{1,3,2,0:T(8,128)S(1)}, f32[1,512,1,8,128]{1,4,3,0,2:T(8,128)S(1)}) %tuple.99, (s32[2]{0:T(128)S(1)}, s32[2,256]{1,0:T(2,128)S(1)}, s32[128]{0:T(128)S(1)}, ...), branch_computations={%region_10.11_spmd, %region_11.15_spmd} | conditional | flops 1102203392 | bytes 32495960 | solution.py:121
  833.6 0.1 and.47
  833.7 0.1 select_reduce_fusion
  833.8 0.1 lt.82
  833.9 6.4 gather_fusion
  840.4 0.1 broadcast_in_dim.154
  840.4 0.1 broadcast_select_fusion
  840.6 2.6 bitcast_reduce_fusion.1
  843.2 2.4 fusion.23
  845.6 2.6 bitcast_add_fusion.2
  848.2 0.3 divide_convert_fusion
  848.5 1.3 copy.40
  (30 shorter events, 0.3 us)
Async XLA Ops:
  6.5 14.8 %copy-start.1 = (bf16[2,512,128]{2,1,0:T(8,128)(2,1)S(1)}, bf16[2,512,128]{2,1,0:T(8,128)(2,1)}, u32[]{:S(2)}) copy-start(bf16[2,512,128]{2,1,0:T(8,128)(2,1)} %param.13) | copy-start | bytes 786436
  6.5 725.3 %all-gather.3.cloned.1.call-start = ((), (), s32[]{:S(2)}) async-start(), calls=%async_computation | async-start | bytes 8421376 | tf_op jit(solution)/shard_map/all_gather | solution.py:82
  7.3 826.1 %all-gather.5.cloned.1.call-start = ((), (), s32[]{:S(2)}) async-start(), calls=%async_computation.1 | async-start | bytes 17301504 | tf_op jit(solution)/shard_map/all_gather | solution.py:107
  18.1 3.2 copy-start
  734.2 99.2 %copy-start.2 = (s32[128]{0:T(128)S(1)}, s32[128]{0:T(128)}, u32[]{:S(2)}) copy-start(s32[128]{0:T(128)} %param.16) | copy-start | bytes 1540
Sparse Core Ops, SparseCore 0:
  9.2 722.5 all-gather.2
  733.8 99.6 all-gather.4
where the time goes:
time: 857 us
  waiting for transfers between devices  772 us (90%)
  matrix products  32.6 us (4%)
  local copies, waits for them, and re-layouts  19.3 us (2%)
  other arithmetic  17.5 us (2%)
  between operations  14.2 us (2%)
    all_gather x1, waiting for transfers between devices, per_device(): lax.all_gather(root_kv, ('blk', 'tp'), axis=1, tiled=True)  699 us
    all_gather x1, waiting for transfers between devices, per_device(): pieces = lax.all_gather(node_kv, 'blk', axis=1, tiled=True)  72.5 us
  transfers between devices with their start and end apart: 2, of which 2 were waited for; matrix products, arithmetic and copies ran while one was open for 6% of the time, Pallas kernels for 0%

commit v1 on v0

v1 whole, which is shorter than its diff:
```python
import jax
import jax.numpy as jnp
from jax import lax
from jax.experimental import pallas as pl
from jax.experimental.pallas import tpu as pltpu
from jax.sharding import PartitionSpec as P

HD = 128
HEADS_DEV = 8
LEAF_LEN = 512
NODE_LEN = 256
DEPTH = 2
ROOT = 2048
Z, Y, CORES = 4, 4, 2
CHIPS = Z * Y
PIECE = NODE_LEN // CHIPS
NODES_DEV = 4
NODE_ROWS = DEPTH * NODE_LEN

SCORE_SCALE = HD**-0.5
LOG_SCALE = SCORE_SCALE * 1.4426950408889634
MASKED = -1e30
TOTAL_MIN, TOTAL_MAX = 2.0**-60, 2.0**100

bf16, f32 = jnp.bfloat16, jnp.float32


def device_at(z, y, core):
    return (z * Y + y) * CORES + core


def shifted(dz, dy, dcore):
    return [
        (device_at(z, y, c), device_at((z + dz) % Z, (y + dy) % Y, c ^ dcore))
        for z in range(Z)
        for y in range(Y)
        for c in range(CORES)
    ]


SAME_CORE = [[device_at(z, y, c) for z in range(Z) for y in range(Y)] for c in range(CORES)]


def dot(a, b):
    return jnp.dot(a, b, preferred_element_type=f32)


def dot_t(a, b):
    return lax.dot_general(a, b, (((1,), (1,)), ((), ())), preferred_element_type=f32)


def scaled_query(q):
    scaled = q.astype(f32) * LOG_SCALE
    high = scaled.astype(bf16)
    low = (scaled - high.astype(f32)).astype(bf16)
    return jnp.concatenate([high, low], 1)


def store_keys(keys_ref, first, keys):
    count = keys.shape[0]
    turned = keys.T
    keys_ref[0:HD, first : first + count] = turned
    keys_ref[HD : 2 * HD, first : first + count] = turned


def leaf_kernel(q_ref, leaf_ref, out_ref, keys, values):
    @pl.when(pl.program_id(0) == 0)
    def _():
        store_keys(keys, 0, leaf_ref[0])
        values[:, 0:HD] = leaf_ref[1]
        values[:, HD : 2 * HD] = jnp.ones((LEAF_LEN, HD), bf16)

    half = LEAF_LEN // 2
    row = lax.broadcasted_iota(jnp.int32, (half, half), 0)
    column = lax.broadcasted_iota(jnp.int32, (half, half), 1)
    causal = row >= column
    query = scaled_query(q_ref[...])
    upper, lower = query[:half], query[half:]
    weights = jnp.exp2(jnp.where(causal, dot(upper, keys[:, :half]), MASKED)).astype(bf16)
    out_ref[0, :half, :] = dot(weights, values[:half])
    weights = jnp.exp2(dot(lower, keys[:, :half])).astype(bf16)
    own = jnp.exp2(jnp.where(causal, dot(lower, keys[:, half:]), MASKED)).astype(bf16)
    out_ref[0, half:, :] = dot(weights, values[:half]) + dot(own, values[half:])


def root_kernel(q_ref, mine_ref, other_ref, acc_ref, out_ref, keys, values):
    @pl.when(pl.program_id(0) == 0)
    def _():
        count = ROOT // CORES
        for part, ref in enumerate((mine_ref, other_ref)):
            first = part * count
            store_keys(keys, first, ref[:, 0].reshape(count, HD))
            values[first : first + count, 0:HD] = ref[:, 1].reshape(count, HD)
            values[first : first + count, HD : 2 * HD] = jnp.ones((count, HD), bf16)

    scores = dot(scaled_query(q_ref[...]), keys[...])
    out_ref[0] = acc_ref[0] + dot(jnp.exp2(scores).astype(bf16), values[...])


def select_kernel(
    blk_ref, slot_leaf_ref, ancestors_ref, node_slot_ref, mine_ref, other_ref, out_ref
):
    core = lax.rem(blk_ref[0], CORES)
    for chip in range(CHIPS):
        leaf = slot_leaf_ref[chip * CORES + core]
        for level in range(DEPTH):
            slot = node_slot_ref[ancestors_ref[leaf * DEPTH + level]]
            owner = slot // NODES_DEV
            place = lax.rem(slot, NODES_DEV)
            source = owner // CORES
            same = lax.rem(owner, CORES) == core

            @pl.when(same)
            def _():
                out_ref[chip, :, level] = mine_ref[source, :, place]

            @pl.when(jnp.logical_not(same))
            def _():
                out_ref[chip, :, level] = other_ref[source, :, place]


def node_kernel(
    blk_ref,
    slot_leaf_ref,
    ancestors_ref,
    node_len_ref,
    q_ref,
    node_ref,
    acc_ref,
    mine_ref,
    other_ref,
    leaf_ref,
    out_ref,
    keys,
    values,
    root_vmem,
    leaf_vmem,
):
    leaf = slot_leaf_ref[blk_ref[0]]
    first_len = node_len_ref[ancestors_ref[leaf * DEPTH]]
    second_len = node_len_ref[ancestors_ref[leaf * DEPTH + 1]]

    def visible(shape, dim):
        r = lax.broadcasted_iota(jnp.int32, shape, dim)
        token = (r >> 5) * PIECE + (r & (PIECE - 1))
        return token < jnp.where((r & PIECE) == 0, first_len, second_len)

    @pl.when(pl.program_id(0) == 0)
    def _():
        shown = visible((NODE_ROWS, HD), 0)
        node_keys = node_ref[:, 0].reshape(NODE_ROWS, HD).astype(f32)
        node_values = node_ref[:, 1].reshape(NODE_ROWS, HD).astype(f32)
        store_keys(keys, 0, jnp.where(shown, node_keys, 0.0).astype(bf16))
        values[:, 0:HD] = jnp.where(shown, node_values, 0.0).astype(bf16)
        values[:, HD : 2 * HD] = jnp.where(shown, 1.0, 0.0).astype(bf16)

    scores = dot(scaled_query(q_ref[...]), keys[...])
    acc = acc_ref[0] + dot(jnp.exp2(scores).astype(bf16), values[...])
    total = acc[:, HD:]
    out_ref[...] = (acc[:, :HD] / total).astype(bf16)
    inside = (total >= TOTAL_MIN) & (total <= TOTAL_MAX)
    outside = jnp.max(jnp.where(inside, 0.0, 1.0)) > 0.5

    @pl.when(outside)
    def _():
        pltpu.sync_copy(mine_ref, root_vmem.at[0])
        pltpu.sync_copy(other_ref, root_vmem.at[1])
        pltpu.sync_copy(leaf_ref, leaf_vmem)
        root_keys = root_vmem[:, :, 0].reshape(ROOT, HD)
        root_values = root_vmem[:, :, 1].reshape(ROOT, HD)
        rows = 128

        def some_rows(step, carry):
            start = pl.multiple_of(step * rows, rows)
            query = q_ref[pl.ds(start, rows), :]
            root_scores = dot_t(query, root_keys) * SCORE_SCALE
            node_scores = dot(query, keys[0:HD, :]) * SCORE_SCALE
            leaf_scores = dot_t(query, leaf_vmem[0]) * SCORE_SCALE
            node_shown = visible((rows, NODE_ROWS), 1)
            position = start + lax.broadcasted_iota(jnp.int32, (rows, LEAF_LEN), 0)
            leaf_shown = position >= lax.broadcasted_iota(jnp.int32, (rows, LEAF_LEN), 1)
            node_scores = jnp.where(node_shown, node_scores, MASKED)
            leaf_scores = jnp.where(leaf_shown, leaf_scores, MASKED)
            top = jnp.maximum(
                jnp.max(root_scores, 1, keepdims=True),
                jnp.maximum(
                    jnp.max(node_scores, 1, keepdims=True), jnp.max(leaf_scores, 1, keepdims=True)
                ),
            )
            root_weights = jnp.exp(root_scores - top)
            node_weights = jnp.where(node_shown, jnp.exp(node_scores - top), 0.0)
            leaf_weights = jnp.where(leaf_shown, jnp.exp(leaf_scores - top), 0.0)
            sums = (
                jnp.sum(root_weights, 1, keepdims=True)
                + jnp.sum(node_weights, 1, keepdims=True)
                + jnp.sum(leaf_weights, 1, keepdims=True)
            )
            mixed = (
                dot(root_weights.astype(bf16), root_values)
                + dot(node_weights.astype(bf16), values[:, 0:HD])
                + dot(leaf_weights.astype(bf16), leaf_vmem[1])
            )
            out_ref[pl.ds(start, rows), :] = (mixed / sums).astype(bf16)
            return carry

        lax.fori_loop(0, LEAF_LEN // rows, some_rows, 0)


def whole(shape):
    return pl.BlockSpec(shape, lambda h, *_: (0,) * len(shape))


q_spec = pl.BlockSpec((LEAF_LEN, HD), lambda h, *_: (0, h))
acc_spec = pl.BlockSpec((1, LEAF_LEN, 2 * HD), lambda h, *_: (h, 0, 0))
acc_shape = jax.ShapeDtypeStruct((HEADS_DEV, LEAF_LEN, 2 * HD), f32)
root_part = (CHIPS, 2, ROOT // (CHIPS * CORES), HD)


def cost(keys):
    rows = HEADS_DEV * LEAF_LEN
    return pl.CostEstimate(
        flops=rows * keys * HD * 8, bytes_accessed=2**22, transcendentals=rows * keys
    )


def attend_leaf(queries, leaf_kv):
    return pl.pallas_call(
        leaf_kernel,
        grid=(HEADS_DEV,),
        in_specs=[q_spec, whole((2, LEAF_LEN, HD))],
        out_specs=acc_spec,
        out_shape=acc_shape,
        scratch_shapes=[pltpu.VMEM((2 * HD, LEAF_LEN), bf16), pltpu.VMEM((LEAF_LEN, 2 * HD), bf16)],
        compiler_params=pltpu.CompilerParams(vmem_limit_bytes=32 * 2**20),
        cost_estimate=cost(LEAF_LEN * 3 // 4),
        name="attend_leaf",
    )(queries, leaf_kv)


def attend_root(queries, mine, other, acc):
    return pl.pallas_call(
        root_kernel,
        grid=(HEADS_DEV,),
        in_specs=[q_spec, whole(root_part), whole(root_part), acc_spec],
        out_specs=acc_spec,
        out_shape=acc_shape,
        scratch_shapes=[pltpu.VMEM((2 * HD, ROOT), bf16), pltpu.VMEM((ROOT, 2 * HD), bf16)],
        compiler_params=pltpu.CompilerParams(vmem_limit_bytes=40 * 2**20),
        cost_estimate=cost(ROOT),
        name="attend_root",
    )(queries, mine, other, acc)


def select_pieces(scalars, mine, other):
    shape = (CHIPS, 2, DEPTH, PIECE, HD)
    part = (CHIPS, 2, NODES_DEV, PIECE, HD)
    return pl.pallas_call(
        select_kernel,
        grid_spec=pltpu.PrefetchScalarGridSpec(
            num_scalar_prefetch=4,
            grid=(1,),
            in_specs=[whole(part), whole(part)],
            out_specs=whole(shape),
        ),
        out_shape=jax.ShapeDtypeStruct(shape, bf16),
        compiler_params=pltpu.CompilerParams(vmem_limit_bytes=16 * 2**20),
        name="select_pieces",
    )(*scalars, mine, other)


def attend_nodes(scalars, queries, nodes, acc, mine, other, leaf_kv):
    anywhere = pl.BlockSpec(memory_space=pl.ANY)
    return pl.pallas_call(
        node_kernel,
        grid_spec=pltpu.PrefetchScalarGridSpec(
            num_scalar_prefetch=4,
            grid=(HEADS_DEV,),
            in_specs=[
                q_spec,
                whole((CHIPS, 2, DEPTH, PIECE, HD)),
                acc_spec,
                anywhere,
                anywhere,
                anywhere,
            ],
            out_specs=q_spec,
            scratch_shapes=[
                pltpu.VMEM((2 * HD, NODE_ROWS), bf16),
                pltpu.VMEM((NODE_ROWS, 2 * HD), bf16),
                pltpu.VMEM((CORES,) + root_part, bf16),
                pltpu.VMEM((2, LEAF_LEN, HD), bf16),
            ],
        ),
        out_shape=jax.ShapeDtypeStruct((LEAF_LEN, HEADS_DEV * HD), bf16),
        compiler_params=pltpu.CompilerParams(vmem_limit_bytes=40 * 2**20),
        cost_estimate=cost(NODE_ROWS),
        name="attend_nodes",
    )(*scalars, queries, nodes, acc, mine, other, leaf_kv)


def per_device(queries, leaf_kv, root_kv, node_kv, node_len, node_slot, slot_leaf, ancestors):
    blk = lax.axis_index("blk").astype(jnp.int32).reshape(1)
    paths = ancestors.reshape(-1)

    pieces = node_kv.reshape(2, NODES_DEV, CHIPS, PIECE, HD).transpose(2, 0, 1, 3, 4)
    mine = lax.all_to_all(pieces, "blk", 0, 0, tiled=True, axis_index_groups=SAME_CORE)
    other = lax.ppermute(mine, "blk", shifted(0, 0, 1))
    chosen = select_pieces((blk, slot_leaf, paths, node_slot), mine, other)
    nodes = lax.all_to_all(chosen, "blk", 0, 0, tiled=True, axis_index_groups=SAME_CORE)

    heads = root_kv.reshape(2, -1, HEADS_DEV, HD).transpose(2, 0, 1, 3)
    heads = lax.all_to_all(heads, "tp", 0, 0, tiled=True)
    root = heads.transpose(1, 0, 2, 3).reshape(1, 2, -1, HD)
    root = jnp.concatenate([root] + [lax.ppermute(root, "blk", shifted(d, 0, 0)) for d in range(1, Z)])
    root = jnp.concatenate([root] + [lax.ppermute(root, "blk", shifted(0, d, 0)) for d in range(1, Y)])
    root_other = lax.ppermute(root, "blk", shifted(0, 0, 1))

    acc = attend_leaf(queries, leaf_kv)
    acc = attend_root(queries, root, root_other, acc)
    scalars = (blk, slot_leaf, paths, node_len)
    return attend_nodes(scalars, queries, nodes, acc, root, root_other, leaf_kv)


def solution(mesh):
    placed = (
        P("blk", "tp"),
        P(None, "blk", "tp"),
        P(None, ("blk", "tp"), None),
        P(None, "blk", None, "tp"),
        P(),
        P(),
        P(),
        P(),
    )
    return jax.shard_map(
        per_device, mesh=mesh, in_specs=placed, out_specs=P("blk", "tp"), check_vma=False
    )
```

time: 857 us -> 132 us (0.15)
  waiting for transfers between devices: 772 us -> 20.6 us
  Pallas kernels: 0 us -> 60.1 us
  starting transfers between devices: 0.04 us -> 36 us
  matrix products: 32.6 us -> 0 us
  other arithmetic: 17.5 us -> 0.02 us
  between operations: 14.2 us -> 0.17 us
    all_gather x2 -> x0, waiting for transfers between devices: 771 us -> none  [the longest x1 699 us: per_device(): lax.all_gather(root_kv, ('blk', 'tp'), axis=1, tiled=True)]
    pallas_call x0 -> x4, Pallas kernels: none -> 60.1 us  [the longest x1 41 us: attend_nodes(): pl.pallas_call(node_kernel, grid_spec=pltpu.PrefetchScalarGridSpec(num_sc...]
    dot_general x12 -> x0, matrix products: 32.6 us -> none  [the longest x4 12.1 us: attend(): jnp.einsum('lqkgn,nkd->lqkgd', rounded, value_rows, preferred_element_typ...]
    all_to_all x0 -> x3, starting transfers between devices: none -> 22.5 us  [the longest x1 11.5 us: per_device(): heads = lax.all_to_all(heads, 'tp', 0, 0, tiled=True)]
    reduce_sum x10 -> x0, other arithmetic: 15.5 us -> none  [the longest x6 12.4 us: attend(): running_sum = running_sum * rescale + jnp.sum(weights, -1)]
    ppermute x0 -> x8, starting transfers between devices: none -> 13.6 us  [the longest x3 4.7 us: per_device(): lax.ppermute(root, 'blk', shifted(d, 0, 0))]
    ppermute x0 -> x8, waiting for transfers between devices: none -> 13.4 us  [the longest x3 10.9 us: per_device(): lax.ppermute(root, 'blk', shifted(d, 0, 0))]
  transfers between devices with their start and end apart: 2 -> 11, of which waited for: 2 -> 5; matrix products, arithmetic and copies ran while one was open for 6% -> 2% of each run, Pallas kernels for 0% -> 15%
where the time goes in v1:
time: 132 us
  Pallas kernels  60.1 us (46%)
  starting transfers between devices  36 us (27%)
  waiting for transfers between devices  20.6 us (16%)
  local copies, waits for them, and re-layouts  14.7 us (11%)
    pallas_call x1, Pallas kernels, attend_nodes(): pl.pallas_call(node_kernel, grid_spec=pltpu.PrefetchScalarGridSpec(num_sc...  41 us
    unnamed x30, local copies, waits for them, and re-layouts  12.1 us
    pallas_call x1, Pallas kernels, attend_root(): pl.pallas_call(root_kernel, grid=(HEADS_DEV,), in_specs=[q_spec, whole(ro...  11.7 us
    all_to_all x1, starting transfers between devices, per_device(): heads = lax.all_to_all(heads, 'tp', 0, 0, tiled=True)  11.5 us
    ppermute x3, waiting for transfers between devices, per_device(): lax.ppermute(root, 'blk', shifted(d, 0, 0))  10.9 us
    all_to_all x1, waiting for transfers between devices, per_device(): heads = lax.all_to_all(heads, 'tp', 0, 0, tiled=True)  7.12 us
    all_to_all x1, starting transfers between devices, per_device(): lax.all_to_all(pieces, 'blk', 0, 0, tiled=True, axis_index_groups=SAME_CORE)  5.79 us
    pallas_call x1, Pallas kernels, attend_leaf(): pl.pallas_call(leaf_kernel, grid=(HEADS_DEV,), in_specs=[q_spec, whole((2...  5.33 us
  transfers between devices with their start and end apart: 11, of which 5 were waited for; matrix products, arithmetic and copies ran while one was open for 2% of the time, Pallas kernels for 15%

profile of v1, /device:TPU:1, one launch (start us, length us, event | category | flops | bytes accessed | tf_op | source)
XLA Modules:
  0.0 131.7 jit_solution(12932660791795183195)
XLA Ops:
  0.0 0.8 copy.26
  0.8 0.6 copy.17
  1.4 11.5 %all-to-all-start.2 = ((bf16[8,2,8,128]{3,2,1,0:T(8,128)(2,1)}), bf16[8,2,8,128]{3,2,1,0:T(8,128)(2,1)S(1)}, u32[]{:S(2)}, u32[]{:S(2)}) async-start(bf16[8,2,8,128]{3,2,1,0:T(8,128)(2,1)} %copy.17), calls=%async_computation.2 | async-start | bytes 65536 | tf_op jit(solution)/shard_map/all_to_all | solution.py:312
  12.9 1.9 %copy.25 = bf16[2,4,16,16,128]{4,3,1,0,2:T(8,128)(2,1)} copy(bf16[2,4,16,16,128]{4,3,2,1,0:T(8,128)(2,1)} %bitcast.23) | data formatting | bytes 1048576 | tf_op jit(solution)/shard_map/reshape | solution.py:305
  14.8 7.1 %all-to-all-done.2 = bf16[8,2,8,128]{3,2,1,0:T(8,128)(2,1)S(1)} async-done(((bf16[8,2,8,128]{3,2,1,0:T(8,128)(2,1)}), bf16[8,2,8,128]{3,2,1,0:T(8,128)(2,1)S(1)}, u32[]{:S(2)}, u32[]{:S(2)}) %all-to-all-start.2) | async-done | bytes 32800 | tf_op jit(solution)/shard_map/all_to_all | solution.py:312
  21.9 5.8 %all-to-all-start = ((bf16[16,2,4,16,128]{4,3,2,1,0:T(8,128)(2,1)}), bf16[16,2,4,16,128]{4,3,2,1,0:T(8,128)(2,1)S(1)}, u32[]{:S(2)}, u32[]{:S(2)}) async-start(bf16[16,2,4,16,128]{4,3,2,1,0:T(8,128)(2,1)} %bitcast.20), calls=%async_computation | async-start | bytes 1048576 | tf_op jit(solution)/shard_map/all_to_all | solution.py:306
  27.7 1.4 %collective-permute-start.1 = (bf16[1,2,64,128]{3,2,1,0:T(8,128)(2,1)S(1)}, bf16[1,2,64,128]{3,2,1,0:T(8,128)(2,1)S(1)}, u32[]{:S(2)}, u32[]{:S(2)}) collective-permute-start(bf16[1,2,64,128]{3,2,1,0:T(8,128)(2,1)S(1)} %copy_bitcast_fusion.1), channel_id=1, source_target_pairs={{0,64},{8,72},{16,80},{24,88},{32,96},{40,104},{48,112},{56,120},{... | collective-permute-start | bytes 98312 | tf_op jit(solution)/shard_map/ppermute | solution.py:314
  29.1 2.1 %collective-permute-start.2 = (bf16[1,2,64,128]{3,2,1,0:T(8,128)(2,1)S(1)}, bf16[1,2,64,128]{3,2,1,0:T(8,128)(2,1)S(1)}, u32[]{:S(2)}, u32[]{:S(2)}) collective-permute-start(bf16[1,2,64,128]{3,2,1,0:T(8,128)(2,1)S(1)} %copy_bitcast_fusion.1), channel_id=1, source_target_pairs={{0,128},{8,136},{16,144},{24,152},{32,160},{40,168},{48,176},{56,1... | collective-permute-start | bytes 98312 | tf_op jit(solution)/shard_map/ppermute | solution.py:314
  31.2 1.2 collective-permute-start.3
  32.4 6.3 %collective-permute-done.1 = bf16[1,2,64,128]{3,2,1,0:T(8,128)(2,1)S(1)} collective-permute-done((bf16[1,2,64,128]{3,2,1,0:T(8,128)(2,1)S(1)}, bf16[1,2,64,128]{3,2,1,0:T(8,128)(2,1)S(1)}, u32[]{:S(2)}, u32[]{:S(2)}) %collective-permute-start.1) | collective-permute-done | bytes 32800 | tf_op jit(solution)/shard_map/ppermute | solution.py:314
  38.7 4.6 %collective-permute-done.2 = bf16[1,2,64,128]{3,2,1,0:T(8,128)(2,1)S(1)} collective-permute-done((bf16[1,2,64,128]{3,2,1,0:T(8,128)(2,1)S(1)}, bf16[1,2,64,128]{3,2,1,0:T(8,128)(2,1)S(1)}, u32[]{:S(2)}, u32[]{:S(2)}) %collective-permute-start.2) | collective-permute-done | bytes 32800 | tf_op jit(solution)/shard_map/ppermute | solution.py:314
  43.3 0.0 collective-permute-done.3
  43.3 1.3 collective-permute-start.4
  44.6 1.8 %collective-permute-start.5 = (bf16[4,2,64,128]{3,2,1,0:T(8,128)(2,1)S(1)}, bf16[4,2,64,128]{3,2,1,0:T(8,128)(2,1)S(1)}, u32[]{:S(2)}, u32[]{:S(2)}) collective-permute-start(bf16[4,2,64,128]{3,2,1,0:T(8,128)(2,1)S(1)} %pad_maximum_fusion), channel_id=1, source_target_pairs={{0,32},{8,40},{16,48},{24,56},{32,0},{40,8},{48,16},{56,24},{64,96... | collective-permute-start | bytes 393224 | tf_op jit(solution)/shard_map/ppermute | solution.py:315
  46.4 1.2 collective-permute-start.6
  47.6 0.8 collective-permute-done.4
  48.4 1.7 %collective-permute-done.5 = bf16[4,2,64,128]{3,2,1,0:T(8,128)(2,1)S(1)} collective-permute-done((bf16[4,2,64,128]{3,2,1,0:T(8,128)(2,1)S(1)}, bf16[4,2,64,128]{3,2,1,0:T(8,128)(2,1)S(1)}, u32[]{:S(2)}, u32[]{:S(2)}) %collective-permute-start.5) | collective-permute-done | bytes 131104 | tf_op jit(solution)/shard_map/ppermute | solution.py:315
  50.2 0.0 all-to-all-done.mine_ref
  50.2 4.1 %collective-permute-start = (bf16[16,2,4,16,128]{4,3,2,1,0:T(8,128)(2,1)S(1)}, bf16[16,2,4,16,128]{4,3,2,1,0:T(8,128)(2,1)S(1)}, u32[]{:S(2)}, u32[]{:S(2)}) collective-permute-start(bf16[16,2,4,16,128]{4,3,2,1,0:T(8,128)(2,1)S(1)} %all-to-all-done.mine_ref), channel_id=1, source_target_pairs={{0,8},{8,0},{16,24},{24,16},{32,40},{40,32},{48,56},{56,48},{64,72... | collective-permute-start | bytes 1572872 | tf_op jit(solution)/shard_map/ppermute | solution.py:307
  54.3 0.0 collective-permute-done.6
  54.3 0.6 collective-permute-start.7
  54.9 0.8 copy.15
  55.6 0.1 reshape.16.ancestors_ref
  55.7 0.0 copy-start.2
  55.7 1.2 copy-done.2
  57.0 0.9 copy-done.4
  57.9 5.3 %attend_leaf.1.acc_ref = f32[8,512,256]{2,1,0:T(8,128)S(1)} custom-call(bf16[512,1024]{1,0:T(8,128)(2,1)S(1)} %copy-done.2, bf16[2,512,128]{2,1,0:T(8,128)(2,1)S(1)} %copy-done.4), custom_call_target="tpu_custom_call" | custom-call | flops 1610612736 | bytes 4194304 | tf_op jit(solution)/shard_map/attend_leaf/pallas_call | solution.py:227
  63.2 0.0 copy-start.9
  63.3 1.9 %copy-done.9 = f32[8,512,256]{2,1,0:T(8,128)} copy-done((f32[8,512,256]{2,1,0:T(8,128)}, f32[8,512,256]{2,1,0:T(8,128)S(1)}, u32[]{:S(2)}) %copy-start.9) | copy-done | bytes 4194328
  65.2 0.0 collective-permute-done.other_ref
  65.2 0.0 copy-done
  65.2 0.0 copy-done.1
  65.2 2.2 %select_pieces.1 = bf16[16,2,2,16,128]{4,3,2,1,0:T(8,128)(2,1)} custom-call(s32[1]{0:T(128)} %bitcast.blk_ref, s32[32]{0:T(128)S(1)} %copy-done.1, s32[64]{0:T(128)S(1)} %reshape.16.ancestors_ref, s32[128]{0:T(128)S(1)} %copy-done, bf16[16,2,4,16,128]{4,3,2,1,0:T(8,128)(2,1)S(1)} %all-to-all-done.mine_ref, ...), custom_call_target="tpu_custom_call" | custom-call | tf_op jit(solution)/shard_map/select_pieces/pallas_call | solution.py:257
  67.4 5.2 %all-to-all-start.1 = ((bf16[16,2,2,16,128]{4,3,2,1,0:T(8,128)(2,1)}), bf16[16,2,2,16,128]{4,3,2,1,0:T(8,128)(2,1)S(1)}, u32[]{:S(2)}, u32[]{:S(2)}) async-start(bf16[16,2,2,16,128]{4,3,2,1,0:T(8,128)(2,1)} %select_pieces.1), calls=%async_computation.1 | async-start | bytes 524288 | tf_op jit(solution)/shard_map/all_to_all | solution.py:309
  72.6 0.0 copy-start.5
  72.6 0.0 copy-start.6
  72.6 0.0 collective-permute-done.7.other_ref
  72.6 0.0 copy-done.3
  72.6 0.0 copy-start.10
  72.7 2.2 %copy-done.10 = f32[8,512,256]{2,1,0:T(8,128)S(1)} copy-done((f32[8,512,256]{2,1,0:T(8,128)S(1)}, f32[8,512,256]{2,1,0:T(8,128)}, u32[]{:S(2)}) %copy-start.10) | copy-done | bytes 4194328
  74.9 11.7 %attend_root.1.acc_ref = f32[8,512,256]{2,1,0:T(8,128)S(1)} custom-call(bf16[512,1024]{1,0:T(8,128)(2,1)S(1)} %copy-done.3, bf16[16,2,64,128]{3,2,1,0:T(8,128)(2,1)S(1)} %constant_dynamic-update-slice_fusion.mine_ref, bf16[16,2,64,128]{3,2,1,0:T(8,128)(2,1)S(1)} %collective-permute-done.7.other_ref, f32[8,512,256]{2,1,0:T(8,128)S(1)} %copy-done.10), custom_call_target="tpu_custom_call" | custom-call | flops 8589934592 | bytes 4194304 | tf_op jit(solution)/shard_map/attend_root/pallas_call | solution.py:241
  86.5 0.0 copy-start.7
  86.5 1.9 %copy-done.7 = f32[8,512,256]{2,1,0:T(8,128)} copy-done((f32[8,512,256]{2,1,0:T(8,128)}, f32[8,512,256]{2,1,0:T(8,128)S(1)}, u32[]{:S(2)}) %copy-start.7) | copy-done | bytes 4194328
  88.5 0.0 all-to-all-done.1.node_ref
  88.5 0.0 copy-done.5
  88.5 0.0 copy-done.6
  88.5 2.2 %copy-done.8 = f32[8,512,256]{2,1,0:T(8,128)S(1)} copy-done((f32[8,512,256]{2,1,0:T(8,128)S(1)}, f32[8,512,256]{2,1,0:T(8,128)}, u32[]{:S(2)}) %copy-start.8) | copy-done | bytes 4194328
  90.7 41.0 %attend_nodes.1 = bf16[512,1024]{1,0:T(8,128)(2,1)} custom-call(s32[1]{0:T(128)} %bitcast.blk_ref, s32[32]{0:T(128)S(1)} %copy-done.1, s32[64]{0:T(128)S(1)} %reshape.16.ancestors_ref, s32[128]{0:T(128)S(1)} %copy-done.6, bf16[512,1024]{1,0:T(8,128)(2,1)S(1)} %copy-done.3, bf16[16,2,2,16,128]{4,3,2,1,0:T(8,128)(2,1)S(1)} %all-to-all-done.1.node_ref, ...), custom_call_target="tpu_custom_call" | custom-call | flops 2147483648 | bytes 4194304 | tf_op jit(solution)/shard_map/attend_nodes/pallas_call | solution.py:273
  (14 shorter events, 0.1 us)
Async XLA Ops:
  1.4 20.5 %all-to-all-start.2 = ((bf16[8,2,8,128]{3,2,1,0:T(8,128)(2,1)}), bf16[8,2,8,128]{3,2,1,0:T(8,128)(2,1)S(1)}, u32[]{:S(2)}, u32[]{:S(2)}) async-start(bf16[8,2,8,128]{3,2,1,0:T(8,128)(2,1)} %copy.17), calls=%async_computation.2 | async-start | bytes 65536 | tf_op jit(solution)/shard_map/all_to_all | solution.py:312
  21.9 43.3 %copy-start = (s32[128]{0:T(128)S(1)}, s32[128]{0:T(128)}, u32[]{:S(2)}) copy-start(s32[128]{0:T(128)} %node_slot_ref.1) | copy-start | bytes 1540
  21.9 43.3 %copy-start.1 = (s32[32]{0:T(128)S(1)}, s32[32]{0:T(128)}, u32[]{:S(2)}) copy-start(s32[32]{0:T(128)} %slot_leaf_ref.3) | copy-start | bytes 388
  21.9 28.3 %all-to-all-start = ((bf16[16,2,4,16,128]{4,3,2,1,0:T(8,128)(2,1)}), bf16[16,2,4,16,128]{4,3,2,1,0:T(8,128)(2,1)S(1)}, u32[]{:S(2)}, u32[]{:S(2)}) async-start(bf16[16,2,4,16,128]{4,3,2,1,0:T(8,128)(2,1)} %bitcast.20), calls=%async_computation | async-start | bytes 1048576 | tf_op jit(solution)/shard_map/all_to_all | solution.py:306
  27.7 11.0 %collective-permute-start.1 = (bf16[1,2,64,128]{3,2,1,0:T(8,128)(2,1)S(1)}, bf16[1,2,64,128]{3,2,1,0:T(8,128)(2,1)S(1)}, u32[]{:S(2)}, u32[]{:S(2)}) collective-permute-start(bf16[1,2,64,128]{3,2,1,0:T(8,128)(2,1)S(1)} %copy_bitcast_fusion.1), channel_id=1, source_target_pairs={{0,64},{8,72},{16,80},{24,88},{32,96},{40,104},{48,112},{56,120},{... | collective-permute-start | bytes 98312 | tf_op jit(solution)/shard_map/ppermute | solution.py:314
  29.1 14.1 %collective-permute-start.2 = (bf16[1,2,64,128]{3,2,1,0:T(8,128)(2,1)S(1)}, bf16[1,2,64,128]{3,2,1,0:T(8,128)(2,1)S(1)}, u32[]{:S(2)}, u32[]{:S(2)}) collective-permute-start(bf16[1,2,64,128]{3,2,1,0:T(8,128)(2,1)S(1)} %copy_bitcast_fusion.1), channel_id=1, source_target_pairs={{0,128},{8,136},{16,144},{24,152},{32,160},{40,168},{48,176},{56,1... | collective-permute-start | bytes 98312 | tf_op jit(solution)/shard_map/ppermute | solution.py:314
  31.2 12.1 %collective-permute-start.3 = (bf16[1,2,64,128]{3,2,1,0:T(8,128)(2,1)S(1)}, bf16[1,2,64,128]{3,2,1,0:T(8,128)(2,1)S(1)}, u32[]{:S(2)}, u32[]{:S(2)}) collective-permute-start(bf16[1,2,64,128]{3,2,1,0:T(8,128)(2,1)S(1)} %copy_bitcast_fusion.1), channel_id=1, source_target_pairs={{0,192},{8,200},{16,208},{24,216},{32,224},{40,232},{48,240},{56,2... | collective-permute-start | bytes 98312 | tf_op jit(solution)/shard_map/ppermute | solution.py:314
  43.3 29.3 %copy-start.3 = (bf16[512,1024]{1,0:T(8,128)(2,1)S(1)}, bf16[512,1024]{1,0:T(8,128)(2,1)}, u32[]{:S(2)}) copy-start(bf16[512,1024]{1,0:T(8,128)(2,1)} %q_ref.5) | copy-start | bytes 3145732
  43.3 5.1 %collective-permute-start.4 = (bf16[4,2,64,128]{3,2,1,0:T(8,128)(2,1)S(1)}, bf16[4,2,64,128]{3,2,1,0:T(8,128)(2,1)S(1)}, u32[]{:S(2)}, u32[]{:S(2)}) collective-permute-start(bf16[4,2,64,128]{3,2,1,0:T(8,128)(2,1)S(1)} %pad_maximum_fusion), channel_id=1, source_target_pairs={{0,16},{8,24},{16,32},{24,40},{32,48},{40,56},{48,0},{56,8},{64,80... | collective-permute-start | bytes 393224 | tf_op jit(solution)/shard_map/ppermute | solution.py:315
  44.6 5.6 %collective-permute-start.5 = (bf16[4,2,64,128]{3,2,1,0:T(8,128)(2,1)S(1)}, bf16[4,2,64,128]{3,2,1,0:T(8,128)(2,1)S(1)}, u32[]{:S(2)}, u32[]{:S(2)}) collective-permute-start(bf16[4,2,64,128]{3,2,1,0:T(8,128)(2,1)S(1)} %pad_maximum_fusion), channel_id=1, source_target_pairs={{0,32},{8,40},{16,48},{24,56},{32,0},{40,8},{48,16},{56,24},{64,96... | collective-permute-start | bytes 393224 | tf_op jit(solution)/shard_map/ppermute | solution.py:315
  46.4 7.9 %collective-permute-start.6 = (bf16[4,2,64,128]{3,2,1,0:T(8,128)(2,1)S(1)}, bf16[4,2,64,128]{3,2,1,0:T(8,128)(2,1)S(1)}, u32[]{:S(2)}, u32[]{:S(2)}) collective-permute-start(bf16[4,2,64,128]{3,2,1,0:T(8,128)(2,1)S(1)} %pad_maximum_fusion), channel_id=1, source_target_pairs={{0,48},{8,56},{16,0},{24,8},{32,16},{40,24},{48,32},{56,40},{64,11... | collective-permute-start | bytes 393224 | tf_op jit(solution)/shard_map/ppermute | solution.py:315
  50.2 15.0 %collective-permute-start = (bf16[16,2,4,16,128]{4,3,2,1,0:T(8,128)(2,1)S(1)}, bf16[16,2,4,16,128]{4,3,2,1,0:T(8,128)(2,1)S(1)}, u32[]{:S(2)}, u32[]{:S(2)}) collective-permute-start(bf16[16,2,4,16,128]{4,3,2,1,0:T(8,128)(2,1)S(1)} %all-to-all-done.mine_ref), channel_id=1, source_target_pairs={{0,8},{8,0},{16,24},{24,16},{32,40},{40,32},{48,56},{56,48},{64,72... | collective-permute-start | bytes 1572872 | tf_op jit(solution)/shard_map/ppermute | solution.py:307
  54.3 18.3 %collective-permute-start.7 = (bf16[16,2,64,128]{3,2,1,0:T(8,128)(2,1)S(1)}, bf16[16,2,64,128]{3,2,1,0:T(8,128)(2,1)S(1)}, u32[]{:S(2)}, u32[]{:S(2)}) collective-permute-start(bf16[16,2,64,128]{3,2,1,0:T(8,128)(2,1)S(1)} %constant_dynamic-update-slice_fusion.mine_ref), channel_id=1, source_target_pairs={{0,8},{8,0},{16,24},{24,16},{32,40},{40,32},{48,56},{56,48},{64,72... | collective-permute-start | bytes 1572872 | tf_op jit(solution)/shard_map/ppermute | solution.py:316
  55.7 1.2 copy-start.2
  57.0 0.9 copy-start.4
  63.2 1.9 %copy-start.9 = (f32[8,512,256]{2,1,0:T(8,128)}, f32[8,512,256]{2,1,0:T(8,128)S(1)}, u32[]{:S(2)}) copy-start(f32[8,512,256]{2,1,0:T(8,128)S(1)} %attend_leaf.1.acc_ref) | copy-start | bytes 12582916
  67.4 21.1 %all-to-all-start.1 = ((bf16[16,2,2,16,128]{4,3,2,1,0:T(8,128)(2,1)}), bf16[16,2,2,16,128]{4,3,2,1,0:T(8,128)(2,1)S(1)}, u32[]{:S(2)}, u32[]{:S(2)}) async-start(bf16[16,2,2,16,128]{4,3,2,1,0:T(8,128)(2,1)} %select_pieces.1), calls=%async_computation.1 | async-start | bytes 524288 | tf_op jit(solution)/shard_map/all_to_all | solution.py:309
  72.6 15.9 %copy-start.5 = (bf16[2,512,128]{2,1,0:T(8,128)(2,1)S(1)}, bf16[2,512,128]{2,1,0:T(8,128)(2,1)}, u32[]{:S(2)}) copy-start(bf16[2,512,128]{2,1,0:T(8,128)(2,1)} %leaf_ref.3) | copy-start | bytes 786436
  72.6 15.9 %copy-start.6 = (s32[128]{0:T(128)S(1)}, s32[128]{0:T(128)}, u32[]{:S(2)}) copy-start(s32[128]{0:T(128)} %node_len_ref.1) | copy-start | bytes 1540
  72.6 2.2 %copy-start.10 = (f32[8,512,256]{2,1,0:T(8,128)S(1)}, f32[8,512,256]{2,1,0:T(8,128)}, u32[]{:S(2)}) copy-start(f32[8,512,256]{2,1,0:T(8,128)} %copy-done.9) | copy-start | bytes 12582916
  86.5 1.9 %copy-start.7 = (f32[8,512,256]{2,1,0:T(8,128)}, f32[8,512,256]{2,1,0:T(8,128)S(1)}, u32[]{:S(2)}) copy-start(f32[8,512,256]{2,1,0:T(8,128)S(1)} %attend_root.1.acc_ref) | copy-start | bytes 12582916
  88.5 2.2 %copy-start.8 = (f32[8,512,256]{2,1,0:T(8,128)S(1)}, f32[8,512,256]{2,1,0:T(8,128)}, u32[]{:S(2)}) copy-start(f32[8,512,256]{2,1,0:T(8,128)} %copy-done.7) | copy-start | bytes 12582916

commit v2 on v1

v2 whole, which is shorter than its diff:
```python
import jax
import jax.numpy as jnp
from jax import lax
from jax.experimental import pallas as pl
from jax.experimental.pallas import tpu as pltpu
from jax.sharding import PartitionSpec as P

HD = 128
HEADS_DEV = 8
LEAF_LEN = 512
NODE_LEN = 256
DEPTH = 2
ROOT = 2048
X, Y, Z, CORES = 4, 4, 4, 2
CHIPS = Z * Y
PIECE = NODE_LEN // CHIPS
NODES_DEV = 4
NODE_ROWS = DEPTH * NODE_LEN
LEAVES, NODES = 32, 128
SLOT_LEAF, ANCESTORS, NODE_SLOT, NODE_LENS, BLK = 0, 32, 96, 224, 352
SPREAD = 4
GROUP, ROOT_BLOCK = 4, 1024
SCORE_SCALE = HD**-0.5
LOG_SCALE = SCORE_SCALE * 1.4426950408889634
MASKED = -1e30
TOTAL_MIN, TOTAL_MAX = 2.0**-60, 2.0**100

bf16, f32 = jnp.bfloat16, jnp.float32


def device_at(z, y, core):
    return (z * Y + y) * CORES + core


def shifted(dz, dy, dcore):
    return [
        (device_at(z, y, c), device_at((z + dz) % Z, (y + dy) % Y, c ^ dcore))
        for z in range(Z)
        for y in range(Y)
        for c in range(CORES)
    ]


SAME_CORE = [[device_at(z, y, c) for z in range(Z) for y in range(Y)] for c in range(CORES)]


def dot(a, b):
    return jnp.dot(a, b, preferred_element_type=f32)


def dot_t(a, b):
    return lax.dot_general(a, b, (((1,), (1,)), ((), ())), preferred_element_type=f32)


def scaled_query(q):
    scaled = q.astype(f32) * LOG_SCALE
    high = scaled.astype(bf16)
    low = (scaled - high.astype(f32)).astype(bf16)
    return jnp.concatenate([high, low], 1)


def store_keys(keys_ref, first, keys):
    count = keys.shape[0]
    turned = keys.T
    keys_ref[0:HD, first : first + count] = turned
    keys_ref[HD : 2 * HD, first : first + count] = turned


def spread_kernel(node_ref, out_ref):
    for chip in range(SPREAD):
        out_ref[chip] = node_ref[:, :, chip * PIECE : (chip + 1) * PIECE]


def node_at(table_ref, blk, level):
    leaf = table_ref[SLOT_LEAF + blk]
    return table_ref[ANCESTORS + level * LEAVES + leaf]


def select_kernel(table_ref, mine_ref, other_ref, out_ref):
    core = lax.rem(table_ref[BLK], CORES)
    for chip in range(CHIPS):
        for level in range(DEPTH):
            slot = table_ref[NODE_SLOT + node_at(table_ref, chip * CORES + core, level)]
            owner = slot // NODES_DEV
            place = lax.rem(slot, NODES_DEV)
            source = owner // CORES
            out_ref[chip, :, level] = jnp.where(
                lax.rem(owner, CORES) == core,
                mine_ref[source, :, place],
                other_ref[source, :, place],
            )


def store_values(values_ref, first, rows):
    count = rows.shape[0]
    values_ref[first : first + count, 0:HD] = rows
    values_ref[first : first + count, HD : 2 * HD] = jnp.ones((count, HD), bf16)


def weigh(query, keys, values, shown=None):
    scores = dot(query, keys)
    if shown is not None:
        scores = jnp.where(shown, scores, MASKED)
    return dot(jnp.exp2(scores).astype(bf16), values)


def leaf_kernel(leaf_ref, q_ref, out_ref, keys, values):
    @pl.when(pl.program_id(0) == 0)
    def _():
        store_keys(keys, 0, leaf_ref[0])
        store_values(values, 0, leaf_ref[1])

    half = LEAF_LEN // 2
    row = lax.broadcasted_iota(jnp.int32, (half, half), 0)
    column = lax.broadcasted_iota(jnp.int32, (half, half), 1)
    causal = row >= column
    for head in range(GROUP):
        query = scaled_query(q_ref[:, head * HD : (head + 1) * HD])
        upper, lower = query[:half], query[half:]
        out_ref[head, :half] = weigh(upper, keys[:, :half], values[:half], causal)
        out_ref[head, half:] = weigh(lower, keys[:, :half], values[:half]) + weigh(
            lower, keys[:, half:], values[half:], causal
        )


def root_kernel(mine_ref, other_ref, q_ref, acc_ref, out_ref, keys, values):
    @pl.when(pl.program_id(0) == 0)
    def _():
        count = ROOT // CORES
        for part, ref in enumerate((mine_ref, other_ref)):
            store_keys(keys, part * count, ref[:, 0].reshape(count, HD))
            store_values(values, part * count, ref[:, 1].reshape(count, HD))

    for head in range(GROUP):
        query = scaled_query(q_ref[:, head * HD : (head + 1) * HD])
        acc = acc_ref[head]
        for first in range(0, ROOT, ROOT_BLOCK):
            block = slice(first, first + ROOT_BLOCK)
            acc += weigh(query, keys[:, block], values[block])
        out_ref[head] = acc


def node_kernel(
    table_ref,
    node_ref,
    mine_ref,
    other_ref,
    leaf_ref,
    q_ref,
    acc_ref,
    out_ref,
    _,
    keys,
    values,
    root_vmem,
    leaf_vmem,
):
    blk = table_ref[BLK]
    first_len = table_ref[NODE_LENS + node_at(table_ref, blk, 0)]
    second_len = table_ref[NODE_LENS + node_at(table_ref, blk, 1)]

    def visible(shape, dim):
        r = lax.broadcasted_iota(jnp.int32, shape, dim)
        token = (r >> 5) * PIECE + (r & (PIECE - 1))
        return token < jnp.where((r & PIECE) == 0, first_len, second_len)

    @pl.when(pl.program_id(0) == 0)
    def _():
        shown = visible((NODE_ROWS, HD), 0)
        node_keys = node_ref[:, 0].reshape(NODE_ROWS, HD).astype(f32)
        node_values = node_ref[:, 1].reshape(NODE_ROWS, HD).astype(f32)
        store_keys(keys, 0, jnp.where(shown, node_keys, 0.0).astype(bf16))
        values[:, 0:HD] = jnp.where(shown, node_values, 0.0).astype(bf16)
        values[:, HD : 2 * HD] = jnp.where(shown, 1.0, 0.0).astype(bf16)

    outside = jnp.zeros((LEAF_LEN, HD), f32)
    for head in range(GROUP):
        columns = slice(head * HD, (head + 1) * HD)
        acc = acc_ref[head] + weigh(scaled_query(q_ref[:, columns]), keys[...], values[...])
        total = acc[:, HD:]
        outside = jnp.where((total >= TOTAL_MIN) & (total <= TOTAL_MAX), outside, 1.0)
        out_ref[:, columns] = (acc[:, :HD] / total).astype(bf16)

    @pl.when(jnp.max(outside) > 0.5)
    def _():
        pltpu.sync_copy(mine_ref, root_vmem.at[0])
        pltpu.sync_copy(other_ref, root_vmem.at[1])
        pltpu.sync_copy(leaf_ref, leaf_vmem)
        rows = 128
        blocks = LEAF_LEN // rows

        def some_rows(step, carry):
            start = pl.multiple_of(lax.rem(step, blocks) * rows, rows)
            place = (pl.ds(start, rows), pl.ds(pl.multiple_of(step // blocks * HD, HD), HD))
            query = q_ref[place]
            root_keys = root_vmem[:, :, 0].reshape(ROOT, HD)
            root_values = root_vmem[:, :, 1].reshape(ROOT, HD)
            root_scores = dot_t(query, root_keys) * SCORE_SCALE
            node_scores = dot(query, keys[0:HD, :]) * SCORE_SCALE
            leaf_scores = dot_t(query, leaf_vmem[0]) * SCORE_SCALE
            node_shown = visible((rows, NODE_ROWS), 1)
            position = start + lax.broadcasted_iota(jnp.int32, (rows, LEAF_LEN), 0)
            leaf_shown = position >= lax.broadcasted_iota(jnp.int32, (rows, LEAF_LEN), 1)
            node_scores = jnp.where(node_shown, node_scores, MASKED)
            leaf_scores = jnp.where(leaf_shown, leaf_scores, MASKED)
            top = jnp.maximum(
                jnp.max(root_scores, 1, keepdims=True),
                jnp.maximum(
                    jnp.max(node_scores, 1, keepdims=True), jnp.max(leaf_scores, 1, keepdims=True)
                ),
            )
            root_weights = jnp.exp(root_scores - top)
            node_weights = jnp.where(node_shown, jnp.exp(node_scores - top), 0.0)
            leaf_weights = jnp.where(leaf_shown, jnp.exp(leaf_scores - top), 0.0)
            total = (
                jnp.sum(root_weights, 1, keepdims=True)
                + jnp.sum(node_weights, 1, keepdims=True)
                + jnp.sum(leaf_weights, 1, keepdims=True)
            )
            attended = (
                dot(root_weights.astype(bf16), root_values)
                + dot(node_weights.astype(bf16), values[:, 0:HD])
                + dot(leaf_weights.astype(bf16), leaf_vmem[1])
            )
            out_ref[place] = (attended / total).astype(bf16)
            return carry

        lax.fori_loop(0, GROUP * blocks, some_rows, 0)


vmem = pl.BlockSpec(memory_space=pltpu.VMEM)
smem = pl.BlockSpec(memory_space=pltpu.SMEM)
anywhere = pl.BlockSpec(memory_space=pl.ANY)
head_spec = pl.BlockSpec((LEAF_LEN, GROUP * HD), lambda step: (0, step))
acc_spec = pl.BlockSpec((GROUP, LEAF_LEN, 2 * HD), lambda step: (step, 0, 0))
root_part = (CHIPS, 2, ROOT // (CHIPS * CORES), HD)


def cost(keys):
    rows = HEADS_DEV * LEAF_LEN
    return pl.CostEstimate(
        flops=rows * keys * HD * 8, bytes_accessed=2**22, transcendentals=rows * keys
    )


def limit(mib):
    return pltpu.CompilerParams(vmem_limit_bytes=mib * 2**20)


def spread(node_kv):
    return pl.pallas_call(
        spread_kernel,
        grid=(CHIPS // SPREAD,),
        in_specs=[
            pl.BlockSpec((2, NODES_DEV, SPREAD * PIECE, HD), lambda step: (0, 0, step, 0))
        ],
        out_specs=pl.BlockSpec((SPREAD, 2, NODES_DEV, PIECE, HD), lambda step: (step, 0, 0, 0, 0)),
        out_shape=pltpu.HBM((CHIPS, 2, NODES_DEV, PIECE, HD), bf16),
        compiler_params=limit(4),
        name="spread",
    )(node_kv)


def select_pieces(table, mine, other):
    return pl.pallas_call(
        select_kernel,
        in_specs=[smem, vmem, vmem],
        out_specs=vmem,
        out_shape=jax.ShapeDtypeStruct((CHIPS, 2, DEPTH, PIECE, HD), bf16),
        compiler_params=limit(8),
        name="select_pieces",
    )(table, mine, other)


def attend_leaf(leaf_kv, queries):
    return pl.pallas_call(
        leaf_kernel,
        grid=(HEADS_DEV // GROUP,),
        in_specs=[pl.BlockSpec((2, LEAF_LEN, HD), lambda step: (0, 0, 0)), head_spec],
        out_specs=acc_spec,
        out_shape=pltpu.HBM((HEADS_DEV, LEAF_LEN, 2 * HD), f32),
        scratch_shapes=[pltpu.VMEM((2 * HD, LEAF_LEN), bf16), pltpu.VMEM((LEAF_LEN, 2 * HD), bf16)],
        compiler_params=limit(24),
        cost_estimate=cost(LEAF_LEN),
        name="attend_leaf",
    )(leaf_kv, queries)


def attend_root(mine, other, queries, acc):
    return pl.pallas_call(
        root_kernel,
        grid=(HEADS_DEV // GROUP,),
        in_specs=[vmem, vmem, head_spec, acc_spec],
        out_specs=acc_spec,
        out_shape=pltpu.HBM((HEADS_DEV, LEAF_LEN, 2 * HD), f32),
        scratch_shapes=[pltpu.VMEM((2 * HD, ROOT), bf16), pltpu.VMEM((ROOT, 2 * HD), bf16)],
        input_output_aliases={3: 0},
        compiler_params=limit(32),
        name="attend_root",
    )(mine, other, queries, acc)


def attend_nodes(table, nodes, mine, other, leaf_kv, queries, acc):
    return pl.pallas_call(
        node_kernel,
        grid=(HEADS_DEV // GROUP,),
        in_specs=[smem, vmem] + [anywhere] * 3 + [head_spec, acc_spec],
        out_specs=[head_spec, anywhere],
        out_shape=[
            jax.ShapeDtypeStruct((LEAF_LEN, HEADS_DEV * HD), bf16),
            pltpu.HBM((HEADS_DEV, LEAF_LEN, 2 * HD), f32),
        ],
        input_output_aliases={6: 1},
        scratch_shapes=[
            pltpu.VMEM((2 * HD, NODE_ROWS), bf16),
            pltpu.VMEM((NODE_ROWS, 2 * HD), bf16),
            pltpu.VMEM((CORES,) + root_part, bf16),
            pltpu.VMEM((2, LEAF_LEN, HD), bf16),
        ],
        compiler_params=limit(32),
        name="attend_nodes",
    )(table, nodes, mine, other, leaf_kv, queries, acc)[0]


def columns_of(rows, place, width):
    return lax.dynamic_slice_in_dim(rows, place * width, width, 2)


def per_device(queries, leaf_kv, root_kv, node_kv, node_len, node_slot, slot_leaf, ancestors):
    blk = lax.axis_index("blk").astype(jnp.int32).reshape(1)
    table = jnp.concatenate([slot_leaf, ancestors.T.reshape(-1), node_slot, node_len, blk])

    tp = lax.axis_index("tp").astype(jnp.int32)
    z_half, x = tp // X, tp % X
    width = X * HD
    swap = [(i, (i + X) % (2 * X)) for i in range(2 * X)]
    away = lax.ppermute(columns_of(root_kv, 1 - z_half, width), "tp", swap)
    root = jnp.concatenate([columns_of(root_kv, z_half, width), away], 1)
    parts = [columns_of(root, x, HD)]
    for d in range(1, X):
        ring = [(h * X + i, h * X + (i + d) % X) for h in range(2) for i in range(X)]
        parts.append(lax.ppermute(columns_of(root, (x + d) % X, HD), "tp", ring))
    root = jnp.concatenate(parts, 1)[None]

    root = jnp.concatenate([root] + [lax.ppermute(root, "blk", shifted(d, 0, 0)) for d in range(1, Z)])

    pieces = spread(node_kv)
    root, pieces = lax.optimization_barrier((root, pieces))
    mine = lax.all_to_all(pieces, "blk", 0, 0, tiled=True, axis_index_groups=SAME_CORE)

    acc = attend_leaf(leaf_kv, queries)
    root = jnp.concatenate([root] + [lax.ppermute(root, "blk", shifted(0, d, 0)) for d in range(1, Y)])
    root, mine, acc = lax.optimization_barrier((root, mine, acc))
    root_other = lax.ppermute(root, "blk", shifted(0, 0, 1))
    other = lax.ppermute(mine, "blk", shifted(0, 0, 1))
    chosen = select_pieces(table, mine, other)
    nodes = lax.all_to_all(chosen, "blk", 0, 0, tiled=True, axis_index_groups=SAME_CORE)

    acc = attend_root(root, root_other, queries, acc)
    return attend_nodes(table, nodes, root, root_other, leaf_kv, queries, acc)


def solution(mesh):
    placed = (
        P("blk", "tp"),
        P(None, "blk", "tp"),
        P(None, ("blk", "tp"), None),
        P(None, "blk", None, "tp"),
        P(),
        P(),
        P(),
        P(),
    )
    return jax.shard_map(
        per_device, mesh=mesh, in_specs=placed, out_specs=P("blk", "tp"), check_vma=False
    )
```

time: 132 us -> 105 us (0.80)
  waiting for transfers between devices: 20.6 us -> 7.7 us
  local copies, waits for them, and re-layouts: 14.7 us -> 4.14 us
  Pallas kernels: 60.1 us -> 57.9 us
    ppermute x0 -> x4, starting transfers between devices: none -> 12.6 us  [the longest x1 7.74 us: per_device(): away = lax.ppermute(columns_of(root_kv, 1 - z_half, width), 'tp', swap)]
    all_to_all x1 -> x0, starting transfers between devices: 11.5 us -> none  [per_device(): heads = lax.all_to_all(heads, 'tp', 0, 0, tiled=True)]
    ppermute x3, waiting for transfers between devices: 10.9 us -> 1.82 us  [per_device(): lax.ppermute(root, 'blk', shifted(d, 0, 0))]
    unnamed x30 -> x18, local copies, waits for them, and re-layouts: 12.1 us -> 3.24 us
    all_to_all x1 -> x0, waiting for transfers between devices: 7.12 us -> none  [per_device(): heads = lax.all_to_all(heads, 'tp', 0, 0, tiled=True)]
    ppermute x0 -> x4, waiting for transfers between devices: none -> 2.77 us  [the longest x3 1.64 us: per_device(): parts.append(lax.ppermute(columns_of(root, (x + d) % X, HD), 'tp', ring))]
    pallas_call x4 -> x5, Pallas kernels: 60.1 us -> 57.9 us  [the longest x1 37.9 us: attend_nodes(): pl.pallas_call(node_kernel, grid=(HEADS_DEV // GROUP,), in_specs=[smem, v...]
    reshape x3 -> x1, local copies, waits for them, and re-layouts: 2.01 us -> 0.08 us  [per_device(): ancestors.T.reshape(-1)]
  transfers between devices with their start and end apart: 11 -> 14, of which waited for: 5 -> 7; matrix products, arithmetic and copies ran while one was open for 2% -> 0% of each run, Pallas kernels for 15% -> 19%
where the time goes in v2:
time: 105 us
  Pallas kernels  57.9 us (55%)
  starting transfers between devices  35.1 us (33%)
  waiting for transfers between devices  7.7 us (7%)
  local copies, waits for them, and re-layouts  4.14 us (4%)
    pallas_call x1, Pallas kernels, attend_nodes(): pl.pallas_call(node_kernel, grid=(HEADS_DEV // GROUP,), in_specs=[smem, v...  37.9 us
    pallas_call x1, Pallas kernels, attend_root(): pl.pallas_call(root_kernel, grid=(HEADS_DEV // GROUP,), in_specs=[vmem, v...  12.6 us
    ppermute x1, starting transfers between devices, per_device(): away = lax.ppermute(columns_of(root_kv, 1 - z_half, width), 'tp', swap)  7.74 us
    all_to_all x1, starting transfers between devices, per_device(): lax.all_to_all(pieces, 'blk', 0, 0, tiled=True, axis_index_groups=SAME_CORE)  5.36 us
    all_to_all x1, starting transfers between devices, per_device(): lax.all_to_all(chosen, 'blk', 0, 0, tiled=True, axis_index_groups=SAME_CORE)  5.3 us
    ppermute x1, starting transfers between devices, per_device(): other = lax.ppermute(mine, 'blk', shifted(0, 0, 1))  5.11 us
    ppermute x3, starting transfers between devices, per_device(): parts.append(lax.ppermute(columns_of(root, (x + d) % X, HD), 'tp', ring))  4.89 us
    pallas_call x1, Pallas kernels, attend_leaf(): pl.pallas_call(leaf_kernel, grid=(HEADS_DEV // GROUP,), in_specs=[pl.Bloc...  4.28 us
  transfers between devices with their start and end apart: 14, of which 7 were waited for; matrix products, arithmetic and copies ran while one was open for 0% of the time, Pallas kernels for 19%

profile of v2, /device:TPU:1, one launch (start us, length us, event | category | flops | bytes accessed | tf_op | source)
XLA Modules:
  0.0 105.0 jit_solution(15704335635003508612)
XLA Ops:
  0.0 0.7 constant_dynamic-slice_fusion
  0.7 7.7 %collective-permute-start = (bf16[2,8,512]{2,1,0:T(8,128)(2,1)S(1)}, bf16[2,8,512]{2,1,0:T(8,128)(2,1)S(1)}, u32[]{:S(2)}, u32[]{:S(2)}) collective-permute-start(bf16[2,8,512]{2,1,0:T(8,128)(2,1)S(1)} %get-tuple-element.21), channel_id=1, source_target_pairs={{0,4},{1,5},{2,6},{3,7},{4,0},{5,1},{6,2},{7,3},{8,12},{9,13},{10,... | collective-permute-start | bytes 49160 | tf_op jit(solution)/shard_map/ppermute | solution.py:337
  8.5 1.1 %collective-permute-done = bf16[2,8,512]{2,1,0:T(8,128)(2,1)S(1)} collective-permute-done((bf16[2,8,512]{2,1,0:T(8,128)(2,1)S(1)}, bf16[2,8,512]{2,1,0:T(8,128)(2,1)S(1)}, u32[]{:S(2)}, u32[]{:S(2)}) %collective-permute-start) | collective-permute-done | bytes 16416 | tf_op jit(solution)/shard_map/ppermute | solution.py:337
  9.6 1.3 %collective-permute-start.1 = (bf16[2,16,128]{2,1,0:T(8,128)(2,1)S(1)}, bf16[2,16,128]{2,1,0:T(8,128)(2,1)S(1)}, u32[]{:S(2)}, u32[]{:S(2)}) collective-permute-start(bf16[2,16,128]{2,1,0:T(8,128)(2,1)S(1)} %get-tuple-element.18), channel_id=1, source_target_pairs={{0,1},{1,2},{2,3},{3,0},{4,5},{5,6},{6,7},{7,4},{8,9},{9,10},{10,1... | collective-permute-start | bytes 24584 | tf_op jit(solution)/shard_map/ppermute | solution.py:342
  10.9 2.5 %collective-permute-start.2 = (bf16[2,16,128]{2,1,0:T(8,128)(2,1)S(1)}, bf16[2,16,128]{2,1,0:T(8,128)(2,1)S(1)}, u32[]{:S(2)}, u32[]{:S(2)}) collective-permute-start(bf16[2,16,128]{2,1,0:T(8,128)(2,1)S(1)} %get-tuple-element.19), channel_id=1, source_target_pairs={{0,2},{1,3},{2,0},{3,1},{4,6},{5,7},{6,4},{7,5},{8,10},{9,11},{10,... | collective-permute-start | bytes 24584 | tf_op jit(solution)/shard_map/ppermute | solution.py:342
  13.3 1.2 %collective-permute-start.3 = (bf16[2,16,128]{2,1,0:T(8,128)(2,1)S(1)}, bf16[2,16,128]{2,1,0:T(8,128)(2,1)S(1)}, u32[]{:S(2)}, u32[]{:S(2)}) collective-permute-start(bf16[2,16,128]{2,1,0:T(8,128)(2,1)S(1)} %get-tuple-element.20), channel_id=1, source_target_pairs={{0,3},{1,0},{2,1},{3,2},{4,7},{5,4},{6,5},{7,6},{8,11},{9,8},{10,9... | collective-permute-start | bytes 24584 | tf_op jit(solution)/shard_map/ppermute | solution.py:342
  14.5 0.0 collective-permute-done.1
  14.5 0.4 collective-permute-done.2
  14.9 1.2 %collective-permute-done.3 = bf16[2,16,128]{2,1,0:T(8,128)(2,1)S(1)} collective-permute-done((bf16[2,16,128]{2,1,0:T(8,128)(2,1)S(1)}, bf16[2,16,128]{2,1,0:T(8,128)(2,1)S(1)}, u32[]{:S(2)}, u32[]{:S(2)}) %collective-permute-start.3) | collective-permute-done | bytes 8224 | tf_op jit(solution)/shard_map/ppermute | solution.py:342
  16.1 2.6 %collective-permute-start.6 = (bf16[1,2,64,128]{3,2,1,0:T(8,128)(2,1)S(1)}, bf16[1,2,64,128]{3,2,1,0:T(8,128)(2,1)S(1)}, u32[]{:S(2)}, u32[]{:S(2)}) collective-permute-start(bf16[1,2,64,128]{3,2,1,0:T(8,128)(2,1)S(1)} %maximum_bitcast_fusion), channel_id=1, source_target_pairs={{0,192},{8,200},{16,208},{24,216},{32,224},{40,232},{48,240},{56,2... | collective-permute-start | bytes 98312 | tf_op jit(solution)/shard_map/ppermute | solution.py:345
  18.8 0.0 collective-permute-start.5
  18.8 0.3 collective-permute-start.4
  19.1 1.0 copy-done.2
  20.1 1.4 %spread.1 = bf16[16,2,4,16,128]{4,3,2,1,0:T(8,128)(2,1)} custom-call(bf16[2,4,256,128]{3,2,1,0:T(8,128)(2,1)S(1)} %copy-done.2), custom_call_target="tpu_custom_call" | custom-call | tf_op jit(solution)/shard_map/spread/pallas_call | solution.py:251
  21.5 0.0 collective-permute-done.6
  21.5 1.0 collective-permute-done.5
  22.6 0.8 collective-permute-done.4
  23.4 0.0 copy-start.1
  23.4 5.4 %all-to-all-start = ((bf16[16,2,4,16,128]{4,3,2,1,0:T(8,128)(2,1)}), bf16[16,2,4,16,128]{4,3,2,1,0:T(8,128)(2,1)S(1)}, u32[]{:S(2)}, u32[]{:S(2)}) async-start(bf16[16,2,4,16,128]{4,3,2,1,0:T(8,128)(2,1)} %spread.1), calls=%async_computation | async-start | bytes 1048576 | tf_op jit(solution)/shard_map/all_to_all | solution.py:349
  28.8 2.6 %collective-permute-start.9 = (bf16[4,2,64,128]{3,2,1,0:T(8,128)(2,1)S(1)}, bf16[4,2,64,128]{3,2,1,0:T(8,128)(2,1)S(1)}, u32[]{:S(2)}, u32[]{:S(2)}) collective-permute-start(bf16[4,2,64,128]{3,2,1,0:T(8,128)(2,1)S(1)} %pad_maximum_fusion.1), channel_id=1, source_target_pairs={{0,48},{8,56},{16,0},{24,8},{32,16},{40,24},{48,32},{56,40},{64,11... | collective-permute-start | bytes 393224 | tf_op jit(solution)/shard_map/ppermute | solution.py:352
  31.4 0.6 collective-permute-start.8
  31.9 0.6 collective-permute-start.7
  32.5 1.2 %copy-done = bf16[512,1024]{1,0:T(8,128)(2,1)S(1)} copy-done((bf16[512,1024]{1,0:T(8,128)(2,1)S(1)}, bf16[512,1024]{1,0:T(8,128)(2,1)}, u32[]{:S(2)}) %copy-start) | copy-done | bytes 1048600
  33.7 0.9 copy-done.3
  34.7 4.3 %attend_leaf.1.acc_ref = f32[8,512,256]{2,1,0:T(8,128)} custom-call(bf16[2,512,128]{2,1,0:T(8,128)(2,1)S(1)} %copy-done.3, bf16[512,1024]{1,0:T(8,128)(2,1)S(1)} %copy-done), custom_call_target="tpu_custom_call" | custom-call | flops 2147483648 | bytes 4194304 | tf_op jit(solution)/shard_map/attend_leaf/pallas_call | solution.py:276
  39.0 0.0 collective-permute-done.9
  39.0 0.0 collective-permute-done.8
  39.0 1.7 %collective-permute-done.7 = bf16[4,2,64,128]{3,2,1,0:T(8,128)(2,1)S(1)} collective-permute-done((bf16[4,2,64,128]{3,2,1,0:T(8,128)(2,1)S(1)}, bf16[4,2,64,128]{3,2,1,0:T(8,128)(2,1)S(1)}, u32[]{:S(2)}, u32[]{:S(2)}) %collective-permute-start.7) | collective-permute-done | bytes 131104 | tf_op jit(solution)/shard_map/ppermute | solution.py:352
  40.7 0.1 pad_maximum_fusion.mine_ref
  40.8 0.0 all-to-all-done.mine_ref
  40.8 5.1 %collective-permute-start.10 = (bf16[16,2,4,16,128]{4,3,2,1,0:T(8,128)(2,1)S(1)}, bf16[16,2,4,16,128]{4,3,2,1,0:T(8,128)(2,1)S(1)}, u32[]{:S(2)}, u32[]{:S(2)}) collective-permute-start(bf16[16,2,4,16,128]{4,3,2,1,0:T(8,128)(2,1)S(1)} %all-to-all-done.mine_ref), channel_id=1, source_target_pairs={{0,8},{8,0},{16,24},{24,16},{32,40},{40,32},{48,56},{56,48},{64,72... | collective-permute-start | bytes 1572872 | tf_op jit(solution)/shard_map/ppermute | solution.py:355
  45.9 0.0 collective-permute-start.11
  45.9 0.0 copy-done.8
  45.9 0.1 reshape.6
  46.0 0.0 copy-done.5
  46.0 0.0 copy-done.6
  46.0 0.0 copy-done.7
  46.0 0.1 concatenate.15.table_ref
  46.1 1.4 %collective-permute-done.10.other_ref = bf16[16,2,4,16,128]{4,3,2,1,0:T(8,128)(2,1)S(1)} collective-permute-done((bf16[16,2,4,16,128]{4,3,2,1,0:T(8,128)(2,1)S(1)}, bf16[16,2,4,16,128]{4,3,2,1,0:T(8,128)(2,1)S(1)}, u32[]{:S(2)}, u32[]{:S(2)}) %collective-permute-start.10) | collective-permute-done | bytes 524320 | tf_op jit(solution)/shard_map/ppermute | solution.py:355
  47.4 1.7 %select_pieces.1 = bf16[16,2,2,16,128]{4,3,2,1,0:T(8,128)(2,1)} custom-call(s32[353]{0:T(512)S(1)} %concatenate.15.table_ref, bf16[16,2,4,16,128]{4,3,2,1,0:T(8,128)(2,1)S(1)} %all-to-all-done.mine_ref, bf16[16,2,4,16,128]{4,3,2,1,0:T(8,128)(2,1)S(1)} %collective-permute-done.10.other_ref), custom_call_target="tpu_custom_call" | custom-call | tf_op jit(solution)/shard_map/select_pieces/pallas_call | solution.py:265
  49.1 5.3 %all-to-all-start.1 = ((bf16[16,2,2,16,128]{4,3,2,1,0:T(8,128)(2,1)}), bf16[16,2,2,16,128]{4,3,2,1,0:T(8,128)(2,1)S(1)}, u32[]{:S(2)}, u32[]{:S(2)}) async-start(bf16[16,2,2,16,128]{4,3,2,1,0:T(8,128)(2,1)} %select_pieces.1), calls=%async_computation.1 | async-start | bytes 524288 | tf_op jit(solution)/shard_map/all_to_all | solution.py:357
  54.4 0.0 copy-start.4
  54.4 0.0 collective-permute-done.11.other_ref
  54.5 0.0 copy-done.1
  54.5 12.6 %attend_root.1.acc_ref = f32[8,512,256]{2,1,0:T(8,128)} custom-call(bf16[16,2,64,128]{3,2,1,0:T(8,128)(2,1)S(1)} %pad_maximum_fusion.mine_ref, bf16[16,2,64,128]{3,2,1,0:T(8,128)(2,1)S(1)} %collective-permute-done.11.other_ref, bf16[512,1024]{1,0:T(8,128)(2,1)S(1)} %copy-done.1, f32[8,512,256]{2,1,0:T(8,128)} %attend_leaf.1.acc_ref), custom_call_target="tpu_custom_call", output_to_operand_aliasing={{}: (3, {})} | custom-call | tf_op jit(solution)/shard_map/attend_root/pallas_call | solution.py:290
  67.0 0.0 all-to-all-done.1.node_ref
  67.0 0.0 copy-done.4
  67.0 37.9 %attend_nodes.1 = (bf16[512,1024]{1,0:T(8,128)(2,1)}, f32[8,512,256]{2,1,0:T(8,128)}) custom-call(s32[353]{0:T(512)S(1)} %concatenate.15.table_ref, bf16[16,2,2,16,128]{4,3,2,1,0:T(8,128)(2,1)S(1)} %all-to-all-done.1.node_ref, bf16[16,2,64,128]{3,2,1,0:T(8,128)(2,1)S(1)} %pad_maximum_fusion.mine_ref, ...), custom_call_target="tpu_custom_call", output_to_operand_aliasing={{1}: (6, {})} | custom-call | tf_op jit(solution)/shard_map/attend_nodes/pallas_call | solution.py:304
  (10 shorter events, 0.0 us)
Async XLA Ops:
  0.7 8.9 %collective-permute-start = (bf16[2,8,512]{2,1,0:T(8,128)(2,1)S(1)}, bf16[2,8,512]{2,1,0:T(8,128)(2,1)S(1)}, u32[]{:S(2)}, u32[]{:S(2)}) collective-permute-start(bf16[2,8,512]{2,1,0:T(8,128)(2,1)S(1)} %get-tuple-element.21), channel_id=1, source_target_pairs={{0,4},{1,5},{2,6},{3,7},{4,0},{5,1},{6,2},{7,3},{8,12},{9,13},{10,... | collective-permute-start | bytes 49160 | tf_op jit(solution)/shard_map/ppermute | solution.py:337
  9.6 4.9 %collective-permute-start.1 = (bf16[2,16,128]{2,1,0:T(8,128)(2,1)S(1)}, bf16[2,16,128]{2,1,0:T(8,128)(2,1)S(1)}, u32[]{:S(2)}, u32[]{:S(2)}) collective-permute-start(bf16[2,16,128]{2,1,0:T(8,128)(2,1)S(1)} %get-tuple-element.18), channel_id=1, source_target_pairs={{0,1},{1,2},{2,3},{3,0},{4,5},{5,6},{6,7},{7,4},{8,9},{9,10},{10,1... | collective-permute-start | bytes 24584 | tf_op jit(solution)/shard_map/ppermute | solution.py:342
  10.9 4.0 %collective-permute-start.2 = (bf16[2,16,128]{2,1,0:T(8,128)(2,1)S(1)}, bf16[2,16,128]{2,1,0:T(8,128)(2,1)S(1)}, u32[]{:S(2)}, u32[]{:S(2)}) collective-permute-start(bf16[2,16,128]{2,1,0:T(8,128)(2,1)S(1)} %get-tuple-element.19), channel_id=1, source_target_pairs={{0,2},{1,3},{2,0},{3,1},{4,6},{5,7},{6,4},{7,5},{8,10},{9,11},{10,... | collective-permute-start | bytes 24584 | tf_op jit(solution)/shard_map/ppermute | solution.py:342
  13.3 2.8 %collective-permute-start.3 = (bf16[2,16,128]{2,1,0:T(8,128)(2,1)S(1)}, bf16[2,16,128]{2,1,0:T(8,128)(2,1)S(1)}, u32[]{:S(2)}, u32[]{:S(2)}) collective-permute-start(bf16[2,16,128]{2,1,0:T(8,128)(2,1)S(1)} %get-tuple-element.20), channel_id=1, source_target_pairs={{0,3},{1,0},{2,1},{3,2},{4,7},{5,4},{6,5},{7,6},{8,11},{9,8},{10,9... | collective-permute-start | bytes 24584 | tf_op jit(solution)/shard_map/ppermute | solution.py:342
  16.1 5.4 %collective-permute-start.6 = (bf16[1,2,64,128]{3,2,1,0:T(8,128)(2,1)S(1)}, bf16[1,2,64,128]{3,2,1,0:T(8,128)(2,1)S(1)}, u32[]{:S(2)}, u32[]{:S(2)}) collective-permute-start(bf16[1,2,64,128]{3,2,1,0:T(8,128)(2,1)S(1)} %maximum_bitcast_fusion), channel_id=1, source_target_pairs={{0,192},{8,200},{16,208},{24,216},{32,224},{40,232},{48,240},{56,2... | collective-permute-start | bytes 98312 | tf_op jit(solution)/shard_map/ppermute | solution.py:345
  18.8 3.8 %collective-permute-start.5 = (bf16[1,2,64,128]{3,2,1,0:T(8,128)(2,1)S(1)}, bf16[1,2,64,128]{3,2,1,0:T(8,128)(2,1)S(1)}, u32[]{:S(2)}, u32[]{:S(2)}) collective-permute-start(bf16[1,2,64,128]{3,2,1,0:T(8,128)(2,1)S(1)} %maximum_bitcast_fusion), channel_id=1, source_target_pairs={{0,128},{8,136},{16,144},{24,152},{32,160},{40,168},{48,176},{56,1... | collective-permute-start | bytes 98312 | tf_op jit(solution)/shard_map/ppermute | solution.py:345
  18.8 4.6 %collective-permute-start.4 = (bf16[1,2,64,128]{3,2,1,0:T(8,128)(2,1)S(1)}, bf16[1,2,64,128]{3,2,1,0:T(8,128)(2,1)S(1)}, u32[]{:S(2)}, u32[]{:S(2)}) collective-permute-start(bf16[1,2,64,128]{3,2,1,0:T(8,128)(2,1)S(1)} %maximum_bitcast_fusion), channel_id=1, source_target_pairs={{0,64},{8,72},{16,80},{24,88},{32,96},{40,104},{48,112},{56,120},{... | collective-permute-start | bytes 98312 | tf_op jit(solution)/shard_map/ppermute | solution.py:345
  19.1 1.0 copy-start.2
  23.4 22.6 %copy-start.8 = (s32[32,2]{0,1:T(2,128)S(1)}, s32[32,2]{0,1:T(2,128)}, u32[]{:S(2)}) copy-start(s32[32,2]{0,1:T(2,128)} %param.15) | copy-start | bytes 772
  23.4 22.6 %copy-start.5 = (s32[32]{0:T(128)S(1)}, s32[32]{0:T(128)}, u32[]{:S(2)}) copy-start(s32[32]{0:T(128)} %param.14) | copy-start | bytes 388
  23.4 22.6 %copy-start.6 = (s32[128]{0:T(128)S(1)}, s32[128]{0:T(128)}, u32[]{:S(2)}) copy-start(s32[128]{0:T(128)} %param.13) | copy-start | bytes 1540
  23.4 22.6 %copy-start.7 = (s32[128]{0:T(128)S(1)}, s32[128]{0:T(128)}, u32[]{:S(2)}) copy-start(s32[128]{0:T(128)} %param.12) | copy-start | bytes 1540
  23.4 31.1 %copy-start.1 = (bf16[512,1024]{1,0:T(8,128)(2,1)S(1)}, bf16[512,1024]{1,0:T(8,128)(2,1)}, u32[]{:S(2)}) copy-start(bf16[512,1024]{1,0:T(8,128)(2,1)} %q_ref.5) | copy-start | bytes 3145732
  23.4 17.4 %all-to-all-start = ((bf16[16,2,4,16,128]{4,3,2,1,0:T(8,128)(2,1)}), bf16[16,2,4,16,128]{4,3,2,1,0:T(8,128)(2,1)S(1)}, u32[]{:S(2)}, u32[]{:S(2)}) async-start(bf16[16,2,4,16,128]{4,3,2,1,0:T(8,128)(2,1)} %spread.1), calls=%async_computation | async-start | bytes 1048576 | tf_op jit(solution)/shard_map/all_to_all | solution.py:349
  28.8 10.2 %collective-permute-start.9 = (bf16[4,2,64,128]{3,2,1,0:T(8,128)(2,1)S(1)}, bf16[4,2,64,128]{3,2,1,0:T(8,128)(2,1)S(1)}, u32[]{:S(2)}, u32[]{:S(2)}) collective-permute-start(bf16[4,2,64,128]{3,2,1,0:T(8,128)(2,1)S(1)} %pad_maximum_fusion.1), channel_id=1, source_target_pairs={{0,48},{8,56},{16,0},{24,8},{32,16},{40,24},{48,32},{56,40},{64,11... | collective-permute-start | bytes 393224 | tf_op jit(solution)/shard_map/ppermute | solution.py:352
  31.4 7.6 %collective-permute-start.8 = (bf16[4,2,64,128]{3,2,1,0:T(8,128)(2,1)S(1)}, bf16[4,2,64,128]{3,2,1,0:T(8,128)(2,1)S(1)}, u32[]{:S(2)}, u32[]{:S(2)}) collective-permute-start(bf16[4,2,64,128]{3,2,1,0:T(8,128)(2,1)S(1)} %pad_maximum_fusion.1), channel_id=1, source_target_pairs={{0,32},{8,40},{16,48},{24,56},{32,0},{40,8},{48,16},{56,24},{64,96... | collective-permute-start | bytes 393224 | tf_op jit(solution)/shard_map/ppermute | solution.py:352
  31.9 8.8 %collective-permute-start.7 = (bf16[4,2,64,128]{3,2,1,0:T(8,128)(2,1)S(1)}, bf16[4,2,64,128]{3,2,1,0:T(8,128)(2,1)S(1)}, u32[]{:S(2)}, u32[]{:S(2)}) collective-permute-start(bf16[4,2,64,128]{3,2,1,0:T(8,128)(2,1)S(1)} %pad_maximum_fusion.1), channel_id=1, source_target_pairs={{0,16},{8,24},{16,32},{24,40},{32,48},{40,56},{48,0},{56,8},{64,80... | collective-permute-start | bytes 393224 | tf_op jit(solution)/shard_map/ppermute | solution.py:352
  32.5 1.2 %copy-start = (bf16[512,1024]{1,0:T(8,128)(2,1)S(1)}, bf16[512,1024]{1,0:T(8,128)(2,1)}, u32[]{:S(2)}) copy-start(bf16[512,1024]{1,0:T(8,128)(2,1)} %q_ref.5) | copy-start | bytes 3145732
  33.7 0.9 copy-start.3
  40.8 6.6 %collective-permute-start.10 = (bf16[16,2,4,16,128]{4,3,2,1,0:T(8,128)(2,1)S(1)}, bf16[16,2,4,16,128]{4,3,2,1,0:T(8,128)(2,1)S(1)}, u32[]{:S(2)}, u32[]{:S(2)}) collective-permute-start(bf16[16,2,4,16,128]{4,3,2,1,0:T(8,128)(2,1)S(1)} %all-to-all-done.mine_ref), channel_id=1, source_target_pairs={{0,8},{8,0},{16,24},{24,16},{32,40},{40,32},{48,56},{56,48},{64,72... | collective-permute-start | bytes 1572872 | tf_op jit(solution)/shard_map/ppermute | solution.py:355
  45.9 8.5 %collective-permute-start.11 = (bf16[16,2,64,128]{3,2,1,0:T(8,128)(2,1)S(1)}, bf16[16,2,64,128]{3,2,1,0:T(8,128)(2,1)S(1)}, u32[]{:S(2)}, u32[]{:S(2)}) collective-permute-start(bf16[16,2,64,128]{3,2,1,0:T(8,128)(2,1)S(1)} %pad_maximum_fusion.mine_ref), channel_id=1, source_target_pairs={{0,8},{8,0},{16,24},{24,16},{32,40},{40,32},{48,56},{56,48},{64,72... | collective-permute-start | bytes 1572872 | tf_op jit(solution)/shard_map/ppermute | solution.py:354
  49.1 17.9 %all-to-all-start.1 = ((bf16[16,2,2,16,128]{4,3,2,1,0:T(8,128)(2,1)}), bf16[16,2,2,16,128]{4,3,2,1,0:T(8,128)(2,1)S(1)}, u32[]{:S(2)}, u32[]{:S(2)}) async-start(bf16[16,2,2,16,128]{4,3,2,1,0:T(8,128)(2,1)} %select_pieces.1), calls=%async_computation.1 | async-start | bytes 524288 | tf_op jit(solution)/shard_map/all_to_all | solution.py:357
  54.4 12.6 %copy-start.4 = (bf16[2,512,128]{2,1,0:T(8,128)(2,1)S(1)}, bf16[2,512,128]{2,1,0:T(8,128)(2,1)}, u32[]{:S(2)}) copy-start(bf16[2,512,128]{2,1,0:T(8,128)(2,1)} %leaf_ref.3) | copy-start | bytes 786436

commit v3 on v2

v3 whole, which is shorter than its diff:
```python
import jax
import jax.numpy as jnp
from jax import lax
from jax.experimental import pallas as pl
from jax.experimental.pallas import tpu as pltpu
from jax.sharding import PartitionSpec as P

HD = 128
HEADS_DEV = 8
LEAF_LEN = 512
NODE_LEN = 256
DEPTH = 2
ROOT = 2048
X, Y, Z, CORES = 4, 4, 4, 2
CHIPS = Z * Y
PIECE = NODE_LEN // CHIPS
NODES_DEV = 4
NODE_ROWS = DEPTH * NODE_LEN
SHARED = ROOT + NODE_ROWS
KEYS = SHARED + LEAF_LEN
LEAVES = 32
SLOT_LEAF, ANCESTORS, NODE_SLOT, NODE_LENS, BLK = 0, 32, 96, 224, 352
SPREAD = 4
GROUP = 4
NODE_GROUPS = ((0, 1, 2, 3, 4, 5), (6, 7))
SCORE_SCALE = HD**-0.5
LOG_SCALE = SCORE_SCALE * 1.4426950408889634
MASKED = -1e30
TOTAL_MIN, TOTAL_MAX = 2.0**-60, 2.0**100

bf16, f32 = jnp.bfloat16, jnp.float32


def device_at(z, y, core):
    return (z * Y + y) * CORES + core


def shifted(dz, dy, dcore):
    return [
        (device_at(z, y, c), device_at((z + dz) % Z, (y + dy) % Y, c ^ dcore))
        for z in range(Z)
        for y in range(Y)
        for c in range(CORES)
    ]


SAME_CORE = [[device_at(z, y, c) for z in range(Z) for y in range(Y)] for c in range(CORES)]


def dot(a, b):
    return jnp.dot(a, b, preferred_element_type=f32)


def dot_t(a, b):
    return lax.dot_general(a, b, (((1,), (1,)), ((), ())), preferred_element_type=f32)


def scaled_query(q):
    scaled = q.astype(f32) * LOG_SCALE
    high = scaled.astype(bf16)
    low = (scaled - high.astype(f32)).astype(bf16)
    return jnp.concatenate([high, low], 1)


def store_keys(keys_ref, first, keys):
    count = keys.shape[0]
    turned = keys.T
    keys_ref[0:HD, first : first + count] = turned
    keys_ref[HD : 2 * HD, first : first + count] = turned


def spread_kernel(node_ref, out_ref):
    for chip in range(SPREAD):
        out_ref[chip] = node_ref[:, :, chip * PIECE : (chip + 1) * PIECE]


def node_at(table_ref, blk, level):
    leaf = table_ref[SLOT_LEAF + blk]
    return table_ref[ANCESTORS + level * LEAVES + leaf]


def select_kernel(table_ref, mine_ref, other_ref, out_ref):
    core = lax.rem(table_ref[BLK], CORES)
    for chip in range(CHIPS):
        for level in range(DEPTH):
            slot = table_ref[NODE_SLOT + node_at(table_ref, chip * CORES + core, level)]
            owner = slot // NODES_DEV
            place = lax.rem(slot, NODES_DEV)
            source = owner // CORES
            out_ref[chip, :, level] = jnp.where(
                lax.rem(owner, CORES) == core,
                mine_ref[source, :, place],
                other_ref[source, :, place],
            )


def store_values(values_ref, first, rows):
    count = rows.shape[0]
    values_ref[first : first + count, 0:HD] = rows
    values_ref[first : first + count, HD : 2 * HD] = jnp.ones((count, HD), bf16)


def weigh(query, keys, values, shown=None):
    scores = dot(query, keys)
    if shown is not None:
        scores = jnp.where(shown, scores, MASKED)
    return dot(jnp.exp2(scores).astype(bf16), values)


def columns_at(step, width):
    return pl.ds(pl.multiple_of(step * width, width), width)


def total_column(head):
    return head * (HD // HEADS_DEV)


def store_total(totals_ref, head, total):
    if head:
        lane = lax.broadcasted_iota(jnp.int32, (LEAF_LEN, HD), 1)
        total = jnp.where(lane >= total_column(head), total, totals_ref[...])
    totals_ref[...] = total


def store_group(copies, sums, sums_hbm, sems, head):
    if (head + 1) % GROUP == 0:
        part = slice((head + 1 - GROUP) * HD, (head + 1) * HD)
        copy = pltpu.make_async_copy(
            sums.at[:, part], sums_hbm.at[:, part], sems.at[head // GROUP]
        )
        copy.start()
        copies.append(copy)


def leaf_kernel(leaf_ref, q_ref, sums_hbm, totals_ref, keys, values, sums, sems):
    store_keys(keys, 0, leaf_ref[0])
    store_values(values, 0, leaf_ref[1])
    half = LEAF_LEN // 2
    row = lax.broadcasted_iota(jnp.int32, (half, half), 0)
    column = lax.broadcasted_iota(jnp.int32, (half, half), 1)
    causal = row >= column
    copies = []
    for head in range(HEADS_DEV):
        columns = slice(head * HD, (head + 1) * HD)
        query = scaled_query(q_ref[:, columns])
        upper, lower = query[:half], query[half:]
        acc_upper = weigh(upper, keys[:, :half], values[:half], causal)
        acc_lower = weigh(lower, keys[:, :half], values[:half]) + weigh(
            lower, keys[:, half:], values[half:], causal
        )
        sums[:half, columns] = acc_upper[:, :HD]
        sums[half:, columns] = acc_lower[:, :HD]
        store_total(totals_ref, head, jnp.concatenate([acc_upper[:, HD:], acc_lower[:, HD:]]))
        store_group(copies, sums, sums_hbm, sems, head)
    for copy in copies:
        copy.wait()


def root_kernel(mine_ref, other_ref, q_ref, sums_hbm, totals_ref, keys, values, sums, sems):
    count = ROOT // CORES
    for part, ref in enumerate((mine_ref, other_ref)):
        store_keys(keys, part * count, ref[:, 0].reshape(count, HD))
        store_values(values, part * count, ref[:, 1].reshape(count, HD))
    copies = []
    for head in range(HEADS_DEV):
        columns = slice(head * HD, (head + 1) * HD)
        acc = weigh(scaled_query(q_ref[:, columns]), keys[...], values[...])
        sums[:, columns] = acc[:, :HD]
        store_total(totals_ref, head, acc[:, HD:])
        store_group(copies, sums, sums_hbm, sems, head)
    for copy in copies:
        copy.wait()


def node_kernel(
    table_ref,
    node_ref,
    leaf_totals_ref,
    root_totals_ref,
    q_ref,
    mine_ref,
    other_ref,
    leaf_ref,
    leaf_sums_hbm,
    root_sums_hbm,
    out_ref,
    _,
    __,
    keys,
    values,
    root_vmem,
    all_keys,
    leaf_sums,
    root_sums,
    result,
    sems,
):
    arrivals = (
        pltpu.make_async_copy(leaf_sums_hbm, leaf_sums, sems.at[0]),
        pltpu.make_async_copy(root_sums_hbm, root_sums, sems.at[1]),
    )
    for arrival in arrivals:
        arrival.start()
    blk = table_ref[BLK]
    first_len = table_ref[NODE_LENS + node_at(table_ref, blk, 0)]
    second_len = table_ref[NODE_LENS + node_at(table_ref, blk, 1)]

    def visible(shape, dim):
        r = lax.broadcasted_iota(jnp.int32, shape, dim)
        token = (r >> 5) * PIECE + (r & (PIECE - 1))
        return token < jnp.where((r & PIECE) == 0, first_len, second_len)

    shown = visible((NODE_ROWS, HD), 0)
    node_keys = node_ref[:, 0].reshape(NODE_ROWS, HD).astype(f32)
    node_values = node_ref[:, 1].reshape(NODE_ROWS, HD).astype(f32)
    store_keys(keys, 0, jnp.where(shown, node_keys, 0.0).astype(bf16))
    values[:, 0:HD] = jnp.where(shown, node_values, 0.0).astype(bf16)
    values[:, HD : 2 * HD] = jnp.where(shown, 1.0, 0.0).astype(bf16)

    outside = jnp.zeros((LEAF_LEN, HD), f32)
    copies = []
    for heads in NODE_GROUPS:
        mixed = [
            weigh(scaled_query(q_ref[:, head * HD : (head + 1) * HD]), keys[...], values[...])
            for head in heads
        ]
        if not copies:
            for arrival in arrivals:
                arrival.wait()
        for head, acc in zip(heads, mixed):
            columns = slice(head * HD, (head + 1) * HD)
            place = total_column(head)
            earlier = leaf_totals_ref[...] + root_totals_ref[...]
            total = acc[:, HD:] + earlier[:, place : place + 1]
            outside = jnp.where((total >= TOTAL_MIN) & (total <= TOTAL_MAX), outside, 1.0)
            sums = acc[:, :HD] + (leaf_sums[:, columns] + root_sums[:, columns])
            result[:, columns] = (sums / total).astype(bf16)
        part = slice(heads[0] * HD, (heads[-1] + 1) * HD)
        copy = pltpu.make_async_copy(
            result.at[:, part], out_ref.at[:, part], sems.at[2 + len(copies)]
        )
        copy.start()
        copies.append(copy)
    for copy in copies:
        copy.wait()

    @pl.when(jnp.max(outside) > 0.5)
    def _():
        pltpu.sync_copy(mine_ref, root_vmem.at[0])
        pltpu.sync_copy(other_ref, root_vmem.at[1])
        pltpu.sync_copy(leaf_ref, all_keys.at[:, pl.ds(SHARED, LEAF_LEN)])
        for kind in range(2):
            all_keys[kind, 0:ROOT] = root_vmem[:, :, kind].reshape(ROOT, HD)
            all_keys[kind, ROOT:SHARED] = node_ref[:, kind].reshape(NODE_ROWS, HD)
        rows = 128
        blocks = LEAF_LEN // rows

        def some_rows(step, carry):
            start = pl.multiple_of(lax.rem(step, blocks) * rows, rows)
            place = (pl.ds(start, rows), columns_at(step // blocks, HD))
            query = q_ref[place]
            row = start + lax.broadcasted_iota(jnp.int32, (rows, NODE_ROWS), 0)
            column = lax.broadcasted_iota(jnp.int32, (rows, NODE_ROWS), 1)

            def scores_of(block):
                keys_here = all_keys[0, pl.ds(pl.multiple_of(block * NODE_ROWS, NODE_ROWS), NODE_ROWS)]
                scores = dot_t(query, keys_here) * SCORE_SCALE
                first = ROOT // NODE_ROWS
                seen = jnp.where(visible((rows, NODE_ROWS), 1), 1, 0)
                seen = jnp.where(block < first, 1, jnp.where(block == first, seen, row >= column))
                return jnp.where(seen > 0, scores, MASKED), seen > 0

            def take_top(block, top):
                return jnp.maximum(top, jnp.max(scores_of(block)[0], 1, keepdims=True))

            top = lax.fori_loop(
                0, KEYS // NODE_ROWS, take_top, jnp.full((rows, 1), MASKED, f32)
            )

            def add_block(block, carry):
                total, attended = carry
                scores, seen = scores_of(block)
                weights = jnp.where(seen, jnp.exp(scores - top), 0.0)
                here = pl.ds(pl.multiple_of(block * NODE_ROWS, NODE_ROWS), NODE_ROWS)
                total += jnp.sum(weights, 1, keepdims=True)
                return total, attended + dot(weights.astype(bf16), all_keys[1, here])

            total, attended = lax.fori_loop(
                0,
                KEYS // NODE_ROWS,
                add_block,
                (jnp.zeros((rows, 1), f32), jnp.zeros((rows, HD), f32)),
            )
            result[place] = (attended / total).astype(bf16)
            return carry

        lax.fori_loop(0, HEADS_DEV * blocks, some_rows, 0)
        pltpu.sync_copy(result, out_ref)


vmem = pl.BlockSpec(memory_space=pltpu.VMEM)
smem = pl.BlockSpec(memory_space=pltpu.SMEM)
anywhere = pl.BlockSpec(memory_space=pl.ANY)


def limit(mib):
    return pltpu.CompilerParams(vmem_limit_bytes=mib * 2**20)


def spread(node_kv):
    return pl.pallas_call(
        spread_kernel,
        grid=(CHIPS // SPREAD,),
        in_specs=[
            pl.BlockSpec((2, NODES_DEV, SPREAD * PIECE, HD), lambda step: (0, 0, step, 0))
        ],
        out_specs=pl.BlockSpec((SPREAD, 2, NODES_DEV, PIECE, HD), lambda step: (step, 0, 0, 0, 0)),
        out_shape=pltpu.HBM((CHIPS, 2, NODES_DEV, PIECE, HD), bf16),
        compiler_params=limit(4),
        name="spread",
    )(node_kv)


def select_pieces(table, mine, other):
    return pl.pallas_call(
        select_kernel,
        in_specs=[smem, vmem, vmem],
        out_specs=vmem,
        out_shape=jax.ShapeDtypeStruct((CHIPS, 2, DEPTH, PIECE, HD), bf16),
        compiler_params=limit(8),
        name="select_pieces",
    )(table, mine, other)


sums_shape = (LEAF_LEN, HEADS_DEV * HD)
totals_shape = (LEAF_LEN, HD)


sums_out = [pltpu.HBM(sums_shape, f32), jax.ShapeDtypeStruct(totals_shape, f32)]


def attend_leaf(leaf_kv, queries):
    return pl.pallas_call(
        leaf_kernel,
        in_specs=[vmem] * 2,
        out_specs=[anywhere, vmem],
        out_shape=sums_out,
        scratch_shapes=[
            pltpu.VMEM((2 * HD, LEAF_LEN), bf16),
            pltpu.VMEM((LEAF_LEN, 2 * HD), bf16),
            pltpu.VMEM(sums_shape, f32),
            pltpu.SemaphoreType.DMA((HEADS_DEV // GROUP,)),
        ],
        compiler_params=limit(16),
        name="attend_leaf",
    )(leaf_kv, queries)


def attend_root(mine, other, queries):
    return pl.pallas_call(
        root_kernel,
        in_specs=[vmem] * 3,
        out_specs=[anywhere, vmem],
        out_shape=sums_out,
        scratch_shapes=[
            pltpu.VMEM((2 * HD, ROOT), bf16),
            pltpu.VMEM((ROOT, 2 * HD), bf16),
            pltpu.VMEM(sums_shape, f32),
            pltpu.SemaphoreType.DMA((HEADS_DEV // GROUP,)),
        ],
        compiler_params=limit(32),
        name="attend_root",
    )(mine, other, queries)


def attend_nodes(table, nodes, leaf_part, root_part, queries, mine, other, leaf_kv):
    (leaf_sums, leaf_totals), (root_sums, root_totals) = leaf_part, root_part
    return pl.pallas_call(
        node_kernel,
        in_specs=[smem] + [vmem] * 4 + [anywhere] * 5,
        out_specs=[anywhere] * 3,
        out_shape=[
            jax.ShapeDtypeStruct((LEAF_LEN, HEADS_DEV * HD), bf16),
            pltpu.HBM(sums_shape, f32),
            pltpu.HBM(sums_shape, f32),
        ],
        input_output_aliases={8: 1, 9: 2},
        scratch_shapes=[
            pltpu.VMEM((2 * HD, NODE_ROWS), bf16),
            pltpu.VMEM((NODE_ROWS, 2 * HD), bf16),
            pltpu.VMEM((CORES,) + mine.shape, bf16),
            pltpu.VMEM((2, KEYS, HD), bf16),
            pltpu.VMEM(sums_shape, f32),
            pltpu.VMEM(sums_shape, f32),
            pltpu.VMEM((LEAF_LEN, HEADS_DEV * HD), bf16),
            pltpu.SemaphoreType.DMA((2 + len(NODE_GROUPS),)),
        ],
        compiler_params=limit(32),
        name="attend_nodes",
    )(
        table,
        nodes,
        leaf_totals,
        root_totals,
        queries,
        mine,
        other,
        leaf_kv,
        leaf_sums,
        root_sums,
    )[0]


def columns_of(rows, place, width):
    return lax.dynamic_slice_in_dim(rows, place * width, width, 2)


def per_device(queries, leaf_kv, root_kv, node_kv, node_len, node_slot, slot_leaf, ancestors):
    blk = lax.axis_index("blk").astype(jnp.int32).reshape(1)
    table = jnp.concatenate([slot_leaf, ancestors.T.reshape(-1), node_slot, node_len, blk])

    tp = lax.axis_index("tp").astype(jnp.int32)
    z_half, x = tp // X, tp % X
    width = X * HD
    swap = [(i, (i + X) % (2 * X)) for i in range(2 * X)]
    away = lax.ppermute(root_kv, "tp", swap)
    root = columns_of(jnp.concatenate([root_kv, away], 1), z_half, width)
    parts = [columns_of(root, x, HD)]
    for d in range(1, X):
        ring = [(h * X + i, h * X + (i + d) % X) for h in range(2) for i in range(X)]
        parts.append(lax.ppermute(columns_of(root, (x + d) % X, HD), "tp", ring))
    root = jnp.concatenate(parts, 1)[None]

    root = jnp.concatenate([root] + [lax.ppermute(root, "blk", shifted(d, 0, 0)) for d in range(1, Z)])

    pieces = spread(node_kv)
    root, pieces = lax.optimization_barrier((root, pieces))
    mine = lax.all_to_all(pieces, "blk", 0, 0, tiled=True, axis_index_groups=SAME_CORE)

    root = jnp.concatenate([root] + [lax.ppermute(root, "blk", shifted(0, d, 0)) for d in range(1, Y)])
    leaf_sums, leaf_totals = attend_leaf(leaf_kv, queries)
    root, mine, leaf_totals = lax.optimization_barrier((root, mine, leaf_totals))
    root_other = lax.ppermute(root, "blk", shifted(0, 0, 1))
    other = lax.ppermute(mine, "blk", shifted(0, 0, 1))
    chosen = select_pieces(table, mine, other)
    nodes = lax.all_to_all(chosen, "blk", 0, 0, tiled=True, axis_index_groups=SAME_CORE)

    leaf_part = leaf_sums, leaf_totals
    root_part = attend_root(root, root_other, queries)
    return attend_nodes(table, nodes, leaf_part, root_part, queries, root, root_other, leaf_kv)


def solution(mesh):
    placed = (
        P("blk", "tp"),
        P(None, "blk", "tp"),
        P(None, ("blk", "tp"), None),
        P(None, "blk", None, "tp"),
        P(),
        P(),
        P(),
        P(),
    )
    return jax.shard_map(
        per_device, mesh=mesh, in_specs=placed, out_specs=P("blk", "tp"), check_vma=False
    )
```

time: 105 us -> 196 us (1.87)
  Pallas kernels: 57.9 us -> 148 us
  waiting for transfers between devices: 7.7 us -> 10.9 us
    pallas_call x3, Pallas kernels: 54.8 us -> 145 us  [the longest x1 131 us: attend_nodes(): pl.pallas_call(node_kernel, in_specs=[smem] + [vmem] * 4 + [anywhere] * 5...]
    ppermute x3, waiting for transfers between devices: 1.75 us -> 3.89 us  [per_device(): lax.ppermute(root, 'blk', shifted(0, d, 0))]
  transfers between devices with their start and end apart: 14 -> 14, of which waited for: 7 -> 8; matrix products, arithmetic and copies ran while one was open for 0% -> 1% of each run, Pallas kernels for 19% -> 9%
where the time goes in v3:
time: 196 us
  Pallas kernels  148 us (76%)
  starting transfers between devices  33.7 us (17%)
  waiting for transfers between devices  10.9 us (6%)
  local copies, waits for them, and re-layouts  2.83 us (1%)
    pallas_call x1, Pallas kernels, attend_nodes(): pl.pallas_call(node_kernel, in_specs=[smem] + [vmem] * 4 + [anywhere] * 5...  131 us
    pallas_call x1, Pallas kernels, attend_root(): pl.pallas_call(root_kernel, in_specs=[vmem] * 3, out_specs=[anywhere, vme...  10.2 us
    ppermute x1, starting transfers between devices, per_device(): away = lax.ppermute(root_kv, 'tp', swap)  7.74 us
    all_to_all x1, starting transfers between devices, per_device(): lax.all_to_all(pieces, 'blk', 0, 0, tiled=True, axis_index_groups=SAME_CORE)  5.23 us
    ppermute x1, starting transfers between devices, per_device(): other = lax.ppermute(mine, 'blk', shifted(0, 0, 1))  5.2 us
    all_to_all x1, starting transfers between devices, per_device(): lax.all_to_all(chosen, 'blk', 0, 0, tiled=True, axis_index_groups=SAME_CORE)  5.02 us
  transfers between devices with their start and end apart: 14, of which 8 were waited for; matrix products, arithmetic and copies ran while one was open for 1% of the time, Pallas kernels for 9%

profile of v3, /device:TPU:1, one launch (start us, length us, event | category | flops | bytes accessed | tf_op | source)
XLA Modules:
  0.0 195.5 jit_solution(2438514058015667483)
XLA Ops:
  0.0 7.7 %collective-permute-start = (bf16[2,8,1024]{2,1,0:T(8,128)(2,1)}, bf16[2,8,1024]{2,1,0:T(8,128)(2,1)S(1)}, u32[]{:S(2)}, u32[]{:S(2)}) collective-permute-start(bf16[2,8,1024]{2,1,0:T(8,128)(2,1)} %param.10), channel_id=1, source_target_pairs={{0,4},{1,5},{2,6},{3,7},{4,0},{5,1},{6,2},{7,3},{8,12},{9,13},{10,... | collective-permute-start | bytes 98312 | tf_op jit(solution)/shard_map/ppermute | solution.py:426
  7.7 0.8 constant_dynamic-update-slice_fusion.1
  8.5 0.7 collective-permute-done
  9.3 0.1 constant_dynamic-slice_fusion.3
  9.4 2.6 %collective-permute-start.3 = (bf16[2,16,128]{2,1,0:T(8,128)(2,1)S(1)}, bf16[2,16,128]{2,1,0:T(8,128)(2,1)S(1)}, u32[]{:S(2)}, u32[]{:S(2)}) collective-permute-start(bf16[2,16,128]{2,1,0:T(8,128)(2,1)S(1)} %get-tuple-element.26), channel_id=1, source_target_pairs={{0,3},{1,0},{2,1},{3,2},{4,7},{5,4},{6,5},{7,6},{8,11},{9,8},{10,9... | collective-permute-start | bytes 24584 | tf_op jit(solution)/shard_map/ppermute | solution.py:431
  11.9 0.5 collective-permute-start.2
  12.4 0.6 collective-permute-start.1
  13.0 0.0 collective-permute-done.3
  13.0 2.9 %collective-permute-done.2 = bf16[2,16,128]{2,1,0:T(8,128)(2,1)S(1)} collective-permute-done((bf16[2,16,128]{2,1,0:T(8,128)(2,1)S(1)}, bf16[2,16,128]{2,1,0:T(8,128)(2,1)S(1)}, u32[]{:S(2)}, u32[]{:S(2)}) %collective-permute-start.2) | collective-permute-done | bytes 8224 | tf_op jit(solution)/shard_map/ppermute | solution.py:431
  15.9 0.2 collective-permute-done.1
  16.2 2.8 %collective-permute-start.6 = (bf16[1,2,64,128]{3,2,1,0:T(8,128)(2,1)S(1)}, bf16[1,2,64,128]{3,2,1,0:T(8,128)(2,1)S(1)}, u32[]{:S(2)}, u32[]{:S(2)}) collective-permute-start(bf16[1,2,64,128]{3,2,1,0:T(8,128)(2,1)S(1)} %maximum_bitcast_fusion), channel_id=1, source_target_pairs={{0,192},{8,200},{16,208},{24,216},{32,224},{40,232},{48,240},{56,2... | collective-permute-start | bytes 98312 | tf_op jit(solution)/shard_map/ppermute | solution.py:434
  19.0 0.0 collective-permute-start.5
  19.0 0.3 collective-permute-start.4
  19.3 1.0 copy-done.2
  20.3 1.4 spread.1
  21.7 0.0 collective-permute-done.6
  21.8 0.9 collective-permute-done.5
  22.7 0.9 collective-permute-done.4
  23.5 5.2 %all-to-all-start = ((bf16[16,2,4,16,128]{4,3,2,1,0:T(8,128)(2,1)}), bf16[16,2,4,16,128]{4,3,2,1,0:T(8,128)(2,1)S(1)}, u32[]{:S(2)}, u32[]{:S(2)}) async-start(bf16[16,2,4,16,128]{4,3,2,1,0:T(8,128)(2,1)} %spread.1), calls=%async_computation | async-start | bytes 1048576 | tf_op jit(solution)/shard_map/all_to_all | solution.py:438
  28.8 2.6 %collective-permute-start.9 = (bf16[4,2,64,128]{3,2,1,0:T(8,128)(2,1)S(1)}, bf16[4,2,64,128]{3,2,1,0:T(8,128)(2,1)S(1)}, u32[]{:S(2)}, u32[]{:S(2)}) collective-permute-start(bf16[4,2,64,128]{3,2,1,0:T(8,128)(2,1)S(1)} %pad_maximum_fusion.1), channel_id=1, source_target_pairs={{0,48},{8,56},{16,0},{24,8},{32,16},{40,24},{48,32},{56,40},{64,11... | collective-permute-start | bytes 393224 | tf_op jit(solution)/shard_map/ppermute | solution.py:440
  31.4 0.6 collective-permute-start.8
  31.9 0.6 collective-permute-start.7
  32.5 0.0 copy-done
  32.5 0.0 copy-done.1
  32.5 3.6 %attend_leaf.1 = (f32[512,1024]{1,0:T(8,128)}, f32[512,128]{1,0:T(8,128)S(1)}) custom-call(bf16[2,512,128]{2,1,0:T(8,128)(2,1)S(1)} %copy-done.1, bf16[512,1024]{1,0:T(8,128)(2,1)S(1)} %copy-done), custom_call_target="tpu_custom_call" | custom-call | tf_op jit(solution)/shard_map/attend_leaf/pallas_call | solution.py:343
  36.1 0.0 copy-start.3
  36.1 0.7 copy-done.3
  36.8 0.6 collective-permute-done.9
  37.4 0.0 collective-permute-done.8
  37.4 3.2 %collective-permute-done.7 = bf16[4,2,64,128]{3,2,1,0:T(8,128)(2,1)S(1)} collective-permute-done((bf16[4,2,64,128]{3,2,1,0:T(8,128)(2,1)S(1)}, bf16[4,2,64,128]{3,2,1,0:T(8,128)(2,1)S(1)}, u32[]{:S(2)}, u32[]{:S(2)}) %collective-permute-start.7) | collective-permute-done | bytes 131104 | tf_op jit(solution)/shard_map/ppermute | solution.py:440
  40.7 0.1 pad_maximum_fusion.mine_ref
  40.8 0.0 all-to-all-done.mine_ref
  40.8 5.2 %collective-permute-start.10 = (bf16[16,2,4,16,128]{4,3,2,1,0:T(8,128)(2,1)S(1)}, bf16[16,2,4,16,128]{4,3,2,1,0:T(8,128)(2,1)S(1)}, u32[]{:S(2)}, u32[]{:S(2)}) collective-permute-start(bf16[16,2,4,16,128]{4,3,2,1,0:T(8,128)(2,1)S(1)} %all-to-all-done.mine_ref), channel_id=1, source_target_pairs={{0,8},{8,0},{16,24},{24,16},{32,40},{40,32},{48,56},{56,48},{64,72... | collective-permute-start | bytes 1572872 | tf_op jit(solution)/shard_map/ppermute | solution.py:444
  46.0 0.0 collective-permute-start.11
  46.0 0.0 copy-done.8
  46.0 0.1 reshape.6
  46.1 0.0 copy-done.5
  46.1 0.0 copy-done.6
  46.1 0.0 copy-done.7
  46.1 0.1 concatenate.15.table_ref
  46.2 1.4 collective-permute-done.10.other_ref
  47.5 1.7 select_pieces.1
  49.2 5.0 %all-to-all-start.1 = ((bf16[16,2,2,16,128]{4,3,2,1,0:T(8,128)(2,1)}), bf16[16,2,2,16,128]{4,3,2,1,0:T(8,128)(2,1)S(1)}, u32[]{:S(2)}, u32[]{:S(2)}) async-start(bf16[16,2,2,16,128]{4,3,2,1,0:T(8,128)(2,1)} %select_pieces.1), calls=%async_computation.1 | async-start | bytes 524288 | tf_op jit(solution)/shard_map/all_to_all | solution.py:446
  54.2 0.0 collective-permute-done.11.other_ref
  54.2 10.2 %attend_root.1 = (f32[512,1024]{1,0:T(8,128)}, f32[512,128]{1,0:T(8,128)S(1)}) custom-call(bf16[16,2,64,128]{3,2,1,0:T(8,128)(2,1)S(1)} %pad_maximum_fusion.mine_ref, bf16[16,2,64,128]{3,2,1,0:T(8,128)(2,1)S(1)} %collective-permute-done.11.other_ref, bf16[512,1024]{1,0:T(8,128)(2,1)S(1)} %copy-done), custom_call_target="tpu_custom_call" | custom-call | tf_op jit(solution)/shard_map/attend_root/pallas_call | solution.py:360
  64.4 0.0 all-to-all-done.1.node_ref
  64.4 0.0 copy-done.4
  64.4 131.0 %attend_nodes.1 = (bf16[512,1024]{1,0:T(8,128)(2,1)}, f32[512,1024]{1,0:T(8,128)}, f32[512,1024]{1,0:T(8,128)}) custom-call(s32[353]{0:T(512)S(1)} %concatenate.15.table_ref, bf16[16,2,2,16,128]{4,3,2,1,0:T(8,128)(2,1)S(1)} %all-to-all-done.1.node_ref, f32[512,128]{1,0:T(8,128)S(1)} %copy-done.4, ...), custom_call_target="tpu_custom_call", output_to_operand_aliasing={{1}: (8, {}), {2}: (9, {})} | custom-call | tf_op jit(solution)/shard_map/attend_nodes/pallas_call | solution.py:378
  (11 shorter events, 0.0 us)
Async XLA Ops:
  0.0 32.5 %copy-start = (bf16[512,1024]{1,0:T(8,128)(2,1)S(1)}, bf16[512,1024]{1,0:T(8,128)(2,1)}, u32[]{:S(2)}) copy-start(bf16[512,1024]{1,0:T(8,128)(2,1)} %q_ref.5) | copy-start | bytes 3145732
  0.0 32.5 %copy-start.1 = (bf16[2,512,128]{2,1,0:T(8,128)(2,1)S(1)}, bf16[2,512,128]{2,1,0:T(8,128)(2,1)}, u32[]{:S(2)}) copy-start(bf16[2,512,128]{2,1,0:T(8,128)(2,1)} %leaf_ref.3) | copy-start | bytes 786436
  0.0 9.3 %collective-permute-start = (bf16[2,8,1024]{2,1,0:T(8,128)(2,1)}, bf16[2,8,1024]{2,1,0:T(8,128)(2,1)S(1)}, u32[]{:S(2)}, u32[]{:S(2)}) collective-permute-start(bf16[2,8,1024]{2,1,0:T(8,128)(2,1)} %param.10), channel_id=1, source_target_pairs={{0,4},{1,5},{2,6},{3,7},{4,0},{5,1},{6,2},{7,3},{8,12},{9,13},{10,... | collective-permute-start | bytes 98312 | tf_op jit(solution)/shard_map/ppermute | solution.py:426
  9.4 3.7 %collective-permute-start.3 = (bf16[2,16,128]{2,1,0:T(8,128)(2,1)S(1)}, bf16[2,16,128]{2,1,0:T(8,128)(2,1)S(1)}, u32[]{:S(2)}, u32[]{:S(2)}) collective-permute-start(bf16[2,16,128]{2,1,0:T(8,128)(2,1)S(1)} %get-tuple-element.26), channel_id=1, source_target_pairs={{0,3},{1,0},{2,1},{3,2},{4,7},{5,4},{6,5},{7,6},{8,11},{9,8},{10,9... | collective-permute-start | bytes 24584 | tf_op jit(solution)/shard_map/ppermute | solution.py:431
  11.9 4.0 %collective-permute-start.2 = (bf16[2,16,128]{2,1,0:T(8,128)(2,1)S(1)}, bf16[2,16,128]{2,1,0:T(8,128)(2,1)S(1)}, u32[]{:S(2)}, u32[]{:S(2)}) collective-permute-start(bf16[2,16,128]{2,1,0:T(8,128)(2,1)S(1)} %get-tuple-element.27), channel_id=1, source_target_pairs={{0,2},{1,3},{2,0},{3,1},{4,6},{5,7},{6,4},{7,5},{8,10},{9,11},{10,... | collective-permute-start | bytes 24584 | tf_op jit(solution)/shard_map/ppermute | solution.py:431
  12.4 3.7 %collective-permute-start.1 = (bf16[2,16,128]{2,1,0:T(8,128)(2,1)S(1)}, bf16[2,16,128]{2,1,0:T(8,128)(2,1)S(1)}, u32[]{:S(2)}, u32[]{:S(2)}) collective-permute-start(bf16[2,16,128]{2,1,0:T(8,128)(2,1)S(1)} %get-tuple-element.28), channel_id=1, source_target_pairs={{0,1},{1,2},{2,3},{3,0},{4,5},{5,6},{6,7},{7,4},{8,9},{9,10},{10,1... | collective-permute-start | bytes 24584 | tf_op jit(solution)/shard_map/ppermute | solution.py:431
  16.2 5.6 %collective-permute-start.6 = (bf16[1,2,64,128]{3,2,1,0:T(8,128)(2,1)S(1)}, bf16[1,2,64,128]{3,2,1,0:T(8,128)(2,1)S(1)}, u32[]{:S(2)}, u32[]{:S(2)}) collective-permute-start(bf16[1,2,64,128]{3,2,1,0:T(8,128)(2,1)S(1)} %maximum_bitcast_fusion), channel_id=1, source_target_pairs={{0,192},{8,200},{16,208},{24,216},{32,224},{40,232},{48,240},{56,2... | collective-permute-start | bytes 98312 | tf_op jit(solution)/shard_map/ppermute | solution.py:434
  19.0 3.7 %collective-permute-start.5 = (bf16[1,2,64,128]{3,2,1,0:T(8,128)(2,1)S(1)}, bf16[1,2,64,128]{3,2,1,0:T(8,128)(2,1)S(1)}, u32[]{:S(2)}, u32[]{:S(2)}) collective-permute-start(bf16[1,2,64,128]{3,2,1,0:T(8,128)(2,1)S(1)} %maximum_bitcast_fusion), channel_id=1, source_target_pairs={{0,128},{8,136},{16,144},{24,152},{32,160},{40,168},{48,176},{56,1... | collective-permute-start | bytes 98312 | tf_op jit(solution)/shard_map/ppermute | solution.py:434
  19.0 4.6 %collective-permute-start.4 = (bf16[1,2,64,128]{3,2,1,0:T(8,128)(2,1)S(1)}, bf16[1,2,64,128]{3,2,1,0:T(8,128)(2,1)S(1)}, u32[]{:S(2)}, u32[]{:S(2)}) collective-permute-start(bf16[1,2,64,128]{3,2,1,0:T(8,128)(2,1)S(1)} %maximum_bitcast_fusion), channel_id=1, source_target_pairs={{0,64},{8,72},{16,80},{24,88},{32,96},{40,104},{48,112},{56,120},{... | collective-permute-start | bytes 98312 | tf_op jit(solution)/shard_map/ppermute | solution.py:434
  19.3 1.0 copy-start.2
  21.7 24.3 %copy-start.8 = (s32[32,2]{0,1:T(2,128)S(1)}, s32[32,2]{0,1:T(2,128)}, u32[]{:S(2)}) copy-start(s32[32,2]{0,1:T(2,128)} %param.15) | copy-start | bytes 772
  21.7 24.3 %copy-start.5 = (s32[32]{0:T(128)S(1)}, s32[32]{0:T(128)}, u32[]{:S(2)}) copy-start(s32[32]{0:T(128)} %param.14) | copy-start | bytes 388
  21.7 24.3 %copy-start.6 = (s32[128]{0:T(128)S(1)}, s32[128]{0:T(128)}, u32[]{:S(2)}) copy-start(s32[128]{0:T(128)} %param.13) | copy-start | bytes 1540
  21.7 24.3 %copy-start.7 = (s32[128]{0:T(128)S(1)}, s32[128]{0:T(128)}, u32[]{:S(2)}) copy-start(s32[128]{0:T(128)} %param.12) | copy-start | bytes 1540
  23.5 17.2 %all-to-all-start = ((bf16[16,2,4,16,128]{4,3,2,1,0:T(8,128)(2,1)}), bf16[16,2,4,16,128]{4,3,2,1,0:T(8,128)(2,1)S(1)}, u32[]{:S(2)}, u32[]{:S(2)}) async-start(bf16[16,2,4,16,128]{4,3,2,1,0:T(8,128)(2,1)} %spread.1), calls=%async_computation | async-start | bytes 1048576 | tf_op jit(solution)/shard_map/all_to_all | solution.py:438
  28.8 8.7 %collective-permute-start.9 = (bf16[4,2,64,128]{3,2,1,0:T(8,128)(2,1)S(1)}, bf16[4,2,64,128]{3,2,1,0:T(8,128)(2,1)S(1)}, u32[]{:S(2)}, u32[]{:S(2)}) collective-permute-start(bf16[4,2,64,128]{3,2,1,0:T(8,128)(2,1)S(1)} %pad_maximum_fusion.1), channel_id=1, source_target_pairs={{0,48},{8,56},{16,0},{24,8},{32,16},{40,24},{48,32},{56,40},{64,11... | collective-permute-start | bytes 393224 | tf_op jit(solution)/shard_map/ppermute | solution.py:440
  31.4 6.1 %collective-permute-start.8 = (bf16[4,2,64,128]{3,2,1,0:T(8,128)(2,1)S(1)}, bf16[4,2,64,128]{3,2,1,0:T(8,128)(2,1)S(1)}, u32[]{:S(2)}, u32[]{:S(2)}) collective-permute-start(bf16[4,2,64,128]{3,2,1,0:T(8,128)(2,1)S(1)} %pad_maximum_fusion.1), channel_id=1, source_target_pairs={{0,32},{8,40},{16,48},{24,56},{32,0},{40,8},{48,16},{56,24},{64,96... | collective-permute-start | bytes 393224 | tf_op jit(solution)/shard_map/ppermute | solution.py:440
  31.9 8.7 %collective-permute-start.7 = (bf16[4,2,64,128]{3,2,1,0:T(8,128)(2,1)S(1)}, bf16[4,2,64,128]{3,2,1,0:T(8,128)(2,1)S(1)}, u32[]{:S(2)}, u32[]{:S(2)}) collective-permute-start(bf16[4,2,64,128]{3,2,1,0:T(8,128)(2,1)S(1)} %pad_maximum_fusion.1), channel_id=1, source_target_pairs={{0,16},{8,24},{16,32},{24,40},{32,48},{40,56},{48,0},{56,8},{64,80... | collective-permute-start | bytes 393224 | tf_op jit(solution)/shard_map/ppermute | solution.py:440
  36.1 0.7 copy-start.3
  40.8 6.7 %collective-permute-start.10 = (bf16[16,2,4,16,128]{4,3,2,1,0:T(8,128)(2,1)S(1)}, bf16[16,2,4,16,128]{4,3,2,1,0:T(8,128)(2,1)S(1)}, u32[]{:S(2)}, u32[]{:S(2)}) collective-permute-start(bf16[16,2,4,16,128]{4,3,2,1,0:T(8,128)(2,1)S(1)} %all-to-all-done.mine_ref), channel_id=1, source_target_pairs={{0,8},{8,0},{16,24},{24,16},{32,40},{40,32},{48,56},{56,48},{64,72... | collective-permute-start | bytes 1572872 | tf_op jit(solution)/shard_map/ppermute | solution.py:444
  46.0 8.2 %collective-permute-start.11 = (bf16[16,2,64,128]{3,2,1,0:T(8,128)(2,1)S(1)}, bf16[16,2,64,128]{3,2,1,0:T(8,128)(2,1)S(1)}, u32[]{:S(2)}, u32[]{:S(2)}) collective-permute-start(bf16[16,2,64,128]{3,2,1,0:T(8,128)(2,1)S(1)} %pad_maximum_fusion.mine_ref), channel_id=1, source_target_pairs={{0,8},{8,0},{16,24},{24,16},{32,40},{40,32},{48,56},{56,48},{64,72... | collective-permute-start | bytes 1572872 | tf_op jit(solution)/shard_map/ppermute | solution.py:443
  49.2 15.2 %copy-start.4 = (f32[512,128]{1,0:T(8,128)S(1)}, f32[512,128]{1,0:T(8,128)}, u32[]{:S(2)}) copy-start(f32[512,128]{1,0:T(8,128)} %copy-done.3) | copy-start | bytes 786436
  49.2 15.2 %all-to-all-start.1 = ((bf16[16,2,2,16,128]{4,3,2,1,0:T(8,128)(2,1)}), bf16[16,2,2,16,128]{4,3,2,1,0:T(8,128)(2,1)S(1)}, u32[]{:S(2)}, u32[]{:S(2)}) async-start(bf16[16,2,2,16,128]{4,3,2,1,0:T(8,128)(2,1)} %select_pieces.1), calls=%async_computation.1 | async-start | bytes 524288 | tf_op jit(solution)/shard_map/all_to_all | solution.py:446

commit v4 on v3

--- a/solution.py
+++ b/solution.py
@@ -18,6 +18,8 @@
 NODE_ROWS = DEPTH * NODE_LEN
 SHARED = ROOT + NODE_ROWS
 KEYS = SHARED + LEAF_LEN
+TOKENS = ROOT // (CHIPS * CORES)
+NEAR = Z
 LEAVES = 32
 SLOT_LEAF, ANCESTORS, NODE_SLOT, NODE_LENS, BLK = 0, 32, 96, 224, 352
 SPREAD = 4
@@ -132,10 +134,40 @@
         copies.append(copy)
 
 
-def leaf_kernel(leaf_ref, q_ref, sums_hbm, totals_ref, keys, values, sums, sems):
-    store_keys(keys, 0, leaf_ref[0])
-    store_values(values, 0, leaf_ref[1])
+def store_root(keys, values, first, parts):
+    count = parts.shape[0] * parts.shape[2]
+    store_keys(keys, first, parts[:, 0].reshape(count, HD))
+    store_values(values, first, parts[:, 1].reshape(count, HD))
+
+
+def near_kernel(
+    table_ref,
+    root_ref,
+    leaf_ref,
+    q_ref,
+    sums_hbm,
+    totals_ref,
+    down_ref,
+    along_ref,
+    keys,
+    values,
+    sums,
+    sems,
+):
+    blk = table_ref[BLK]
+    first_len = table_ref[NODE_LENS + node_at(table_ref, blk, 0)]
+    second_len = table_ref[NODE_LENS + node_at(table_ref, blk, 1)]
+    for ref, dim in ((down_ref, 0), (along_ref, 1)):
+        r = lax.broadcasted_iota(jnp.int32, ref.shape, dim)
+        token = (r >> 5) * PIECE + (r & (PIECE - 1))
+        length = jnp.where((r & PIECE) == 0, first_len, second_len)
+        ref[...] = jnp.where(token < length, 1.0, 0.0)
+    near = NEAR * TOKENS
+    store_root(keys, values, 0, root_ref)
+    store_keys(keys, near, leaf_ref[0])
+    store_values(values, near, leaf_ref[1])
     half = LEAF_LEN // 2
+    middle, last = near + half, near + LEAF_LEN
     row = lax.broadcasted_iota(jnp.int32, (half, half), 0)
     column = lax.broadcasted_iota(jnp.int32, (half, half), 1)
     causal = row >= column
@@ -144,9 +176,11 @@
         columns = slice(head * HD, (head + 1) * HD)
         query = scaled_query(q_ref[:, columns])
         upper, lower = query[:half], query[half:]
-        acc_upper = weigh(upper, keys[:, :half], values[:half], causal)
-        acc_lower = weigh(lower, keys[:, :half], values[:half]) + weigh(
-            lower, keys[:, half:], values[half:], causal
+        acc_upper = weigh(upper, keys[:, :near], values[:near]) + weigh(
+            upper, keys[:, near:middle], values[near:middle], causal
+        )
+        acc_lower = weigh(lower, keys[:, :middle], values[:middle]) + weigh(
+            lower, keys[:, middle:last], values[middle:last], causal
         )
         sums[:half, columns] = acc_upper[:, :HD]
         sums[half:, columns] = acc_lower[:, :HD]
@@ -156,11 +190,9 @@
         copy.wait()
 
 
-def root_kernel(mine_ref, other_ref, q_ref, sums_hbm, totals_ref, keys, values, sums, sems):
-    count = ROOT // CORES
-    for part, ref in enumerate((mine_ref, other_ref)):
-        store_keys(keys, part * count, ref[:, 0].reshape(count, HD))
-        store_values(values, part * count, ref[:, 1].reshape(count, HD))
+def far_kernel(mine_ref, other_ref, q_ref, sums_hbm, totals_ref, keys, values, sums, sems):
+    store_root(keys, values, 0, mine_ref[NEAR:])
+    store_root(keys, values, (CHIPS - NEAR) * TOKENS, other_ref)
     copies = []
     for head in range(HEADS_DEV):
         columns = slice(head * HD, (head + 1) * HD)
@@ -173,16 +205,17 @@
 
 
 def node_kernel(
-    table_ref,
     node_ref,
-    leaf_totals_ref,
-    root_totals_ref,
+    down_ref,
+    along_ref,
+    near_totals_ref,
+    far_totals_ref,
     q_ref,
     mine_ref,
     other_ref,
     leaf_ref,
-    leaf_sums_hbm,
-    root_sums_hbm,
+    near_sums_hbm,
+    far_sums_hbm,
     out_ref,
     _,
     __,
@@ -190,32 +223,23 @@
     values,
     root_vmem,
     all_keys,
-    leaf_sums,
-    root_sums,
+    near_sums,
+    far_sums,
     result,
     sems,
 ):
     arrivals = (
-        pltpu.make_async_copy(leaf_sums_hbm, leaf_sums, sems.at[0]),
-        pltpu.make_async_copy(root_sums_hbm, root_sums, sems.at[1]),
+        pltpu.make_async_copy(near_sums_hbm, near_sums, sems.at[0]),
+        pltpu.make_async_copy(far_sums_hbm, far_sums, sems.at[1]),
     )
     for arrival in arrivals:
         arrival.start()
-    blk = table_ref[BLK]
-    first_len = table_ref[NODE_LENS + node_at(table_ref, blk, 0)]
-    second_len = table_ref[NODE_LENS + node_at(table_ref, blk, 1)]
-
-    def visible(shape, dim):
-        r = lax.broadcasted_iota(jnp.int32, shape, dim)
-        token = (r >> 5) * PIECE + (r & (PIECE - 1))
-        return token < jnp.where((r & PIECE) == 0, first_len, second_len)
-
-    shown = visible((NODE_ROWS, HD), 0)
+    shown = down_ref[...] > 0.5
     node_keys = node_ref[:, 0].reshape(NODE_ROWS, HD).astype(f32)
     node_values = node_ref[:, 1].reshape(NODE_ROWS, HD).astype(f32)
     store_keys(keys, 0, jnp.where(shown, node_keys, 0.0).astype(bf16))
     values[:, 0:HD] = jnp.where(shown, node_values, 0.0).astype(bf16)
-    values[:, HD : 2 * HD] = jnp.where(shown, 1.0, 0.0).astype(bf16)
+    values[:, HD : 2 * HD] = down_ref[...].astype(bf16)
 
     outside = jnp.zeros((LEAF_LEN, HD), f32)
     copies = []
@@ -230,10 +254,10 @@
         for head, acc in zip(heads, mixed):
             columns = slice(head * HD, (head + 1) * HD)
             place = total_column(head)
-            earlier = leaf_totals_ref[...] + root_totals_ref[...]
+            earlier = near_totals_ref[...] + far_totals_ref[...]
             total = acc[:, HD:] + earlier[:, place : place + 1]
             outside = jnp.where((total >= TOTAL_MIN) & (total <= TOTAL_MAX), outside, 1.0)
-            sums = acc[:, :HD] + (leaf_sums[:, columns] + root_sums[:, columns])
+            sums = acc[:, :HD] + (near_sums[:, columns] + far_sums[:, columns])
             result[:, columns] = (sums / total).astype(bf16)
         part = slice(heads[0] * HD, (heads[-1] + 1) * HD)
         copy = pltpu.make_async_copy(
@@ -266,7 +290,7 @@
                 keys_here = all_keys[0, pl.ds(pl.multiple_of(block * NODE_ROWS, NODE_ROWS), NODE_ROWS)]
                 scores = dot_t(query, keys_here) * SCORE_SCALE
                 first = ROOT // NODE_ROWS
-                seen = jnp.where(visible((rows, NODE_ROWS), 1), 1, 0)
+                seen = jnp.where(jnp.broadcast_to(along_ref[0:1], row.shape) > 0.5, 1, 0)
                 seen = jnp.where(block < first, 1, jnp.where(block == first, seen, row >= column))
                 return jnp.where(seen > 0, scores, MASKED), seen > 0
 
@@ -339,52 +363,58 @@
 sums_out = [pltpu.HBM(sums_shape, f32), jax.ShapeDtypeStruct(totals_shape, f32)]
 
 
-def attend_leaf(leaf_kv, queries):
+def attend_near(table, root, leaf_kv, queries):
+    count = NEAR * TOKENS + LEAF_LEN
     return pl.pallas_call(
-        leaf_kernel,
-        in_specs=[vmem] * 2,
-        out_specs=[anywhere, vmem],
-        out_shape=sums_out,
+        near_kernel,
+        in_specs=[smem] + [vmem] * 3,
+        out_specs=[anywhere, vmem, vmem, vmem],
+        out_shape=sums_out
+        + [
+            jax.ShapeDtypeStruct((NODE_ROWS, HD), f32),
+            jax.ShapeDtypeStruct((8, NODE_ROWS), f32),
+        ],
         scratch_shapes=[
-            pltpu.VMEM((2 * HD, LEAF_LEN), bf16),
-            pltpu.VMEM((LEAF_LEN, 2 * HD), bf16),
+            pltpu.VMEM((2 * HD, count), bf16),
+            pltpu.VMEM((count, 2 * HD), bf16),
             pltpu.VMEM(sums_shape, f32),
             pltpu.SemaphoreType.DMA((HEADS_DEV // GROUP,)),
         ],
-        compiler_params=limit(16),
-        name="attend_leaf",
-    )(leaf_kv, queries)
-
-
-def attend_root(mine, other, queries):
+        compiler_params=limit(24),
+        name="attend_near",
+    )(table, root, leaf_kv, queries)
+
+
+def attend_far(mine, other, queries):
+    count = ROOT - NEAR * TOKENS
     return pl.pallas_call(
-        root_kernel,
+        far_kernel,
         in_specs=[vmem] * 3,
         out_specs=[anywhere, vmem],
         out_shape=sums_out,
         scratch_shapes=[
-            pltpu.VMEM((2 * HD, ROOT), bf16),
-            pltpu.VMEM((ROOT, 2 * HD), bf16),
+            pltpu.VMEM((2 * HD, count), bf16),
+            pltpu.VMEM((count, 2 * HD), bf16),
             pltpu.VMEM(sums_shape, f32),
             pltpu.SemaphoreType.DMA((HEADS_DEV // GROUP,)),
         ],
         compiler_params=limit(32),
-        name="attend_root",
+        name="attend_far",
     )(mine, other, queries)
 
 
-def attend_nodes(table, nodes, leaf_part, root_part, queries, mine, other, leaf_kv):
-    (leaf_sums, leaf_totals), (root_sums, root_totals) = leaf_part, root_part
+def attend_nodes(nodes, masks, near_part, far_part, queries, mine, other, leaf_kv):
+    (near_sums, near_totals), (far_sums, far_totals) = near_part, far_part
     return pl.pallas_call(
         node_kernel,
-        in_specs=[smem] + [vmem] * 4 + [anywhere] * 5,
+        in_specs=[vmem] * 6 + [anywhere] * 5,
         out_specs=[anywhere] * 3,
         out_shape=[
             jax.ShapeDtypeStruct((LEAF_LEN, HEADS_DEV * HD), bf16),
             pltpu.HBM(sums_shape, f32),
             pltpu.HBM(sums_shape, f32),
         ],
-        input_output_aliases={8: 1, 9: 2},
+        input_output_aliases={9: 1, 10: 2},
         scratch_shapes=[
             pltpu.VMEM((2 * HD, NODE_ROWS), bf16),
             pltpu.VMEM((NODE_ROWS, 2 * HD), bf16),
@@ -398,16 +428,16 @@
         compiler_params=limit(32),
         name="attend_nodes",
     )(
-        table,
         nodes,
-        leaf_totals,
-        root_totals,
+        *masks,
+        near_totals,
+        far_totals,
         queries,
         mine,
         other,
         leaf_kv,
-        leaf_sums,
-        root_sums,
+        near_sums,
+        far_sums,
     )[0]
 
 
@@ -437,17 +467,17 @@
     root, pieces = lax.optimization_barrier((root, pieces))
     mine = lax.all_to_all(pieces, "blk", 0, 0, tiled=True, axis_index_groups=SAME_CORE)
 
+    near_sums, near_totals, *masks = attend_near(table, root, leaf_kv, queries)
     root = jnp.concatenate([root] + [lax.ppermute(root, "blk", shifted(0, d, 0)) for d in range(1, Y)])
-    leaf_sums, leaf_totals = attend_leaf(leaf_kv, queries)
-    root, mine, leaf_totals = lax.optimization_barrier((root, mine, leaf_totals))
+    root, mine, near_totals = lax.optimization_barrier((root, mine, near_totals))
     root_other = lax.ppermute(root, "blk", shifted(0, 0, 1))
     other = lax.ppermute(mine, "blk", shifted(0, 0, 1))
     chosen = select_pieces(table, mine, other)
     nodes = lax.all_to_all(chosen, "blk", 0, 0, tiled=True, axis_index_groups=SAME_CORE)
 
-    leaf_part = leaf_sums, leaf_totals
-    root_part = attend_root(root, root_other, queries)
-    return attend_nodes(table, nodes, leaf_part, root_part, queries, root, root_other, leaf_kv)
+    near_part = near_sums, near_totals
+    far_part = attend_far(root, root_other, queries)
+    return attend_nodes(nodes, masks, near_part, far_part, queries, root, root_other, leaf_kv)
 
 
 def solution(mesh):

time: 196 us -> 195 us (level)
  no operation moved by 1% of the time
where the time goes in v4:
time: 195 us; the launch traced here: 194 us
  Pallas kernels  148 us (76%)
  starting transfers between devices  33.4 us (17%)
  waiting for transfers between devices  10.7 us (5%)
  local copies, waits for them, and re-layouts  2.13 us (1%)
    pallas_call x1, Pallas kernels, attend_nodes(): pl.pallas_call(node_kernel, in_specs=[vmem] * 6 + [anywhere] * 5, out_spe...  130 us
    pallas_call x1, Pallas kernels, attend_far(): pl.pallas_call(far_kernel, in_specs=[vmem] * 3, out_specs=[anywhere, vmem...  9.04 us
    ppermute x1, starting transfers between devices, per_device(): away = lax.ppermute(root_kv, 'tp', swap)  7.74 us
    pallas_call x1, Pallas kernels, attend_near(): pl.pallas_call(near_kernel, in_specs=[smem] + [vmem] * 3, out_specs=[anyw...  5.29 us
    all_to_all x1, starting transfers between devices, per_device(): lax.all_to_all(pieces, 'blk', 0, 0, tiled=True, axis_index_groups=SAME_CORE)  5.22 us
    ppermute x1, starting transfers between devices, per_device(): other = lax.ppermute(mine, 'blk', shifted(0, 0, 1))  5.22 us
    all_to_all x1, starting transfers between devices, per_device(): lax.all_to_all(chosen, 'blk', 0, 0, tiled=True, axis_index_groups=SAME_CORE)  4.71 us
  transfers between devices with their start and end apart: 14, of which 8 were waited for; matrix products, arithmetic and copies ran while one was open for 1% of the time, Pallas kernels for 9%

profile of v4, /device:TPU:1, one launch (start us, length us, event | category | flops | bytes accessed | tf_op | source)
XLA Modules:
  0.0 194.3 jit_solution(9552302297406543101)
XLA Ops:
  0.0 0.0 copy-start
  0.0 0.0 copy-start.1
  0.0 7.7 %collective-permute-start = (bf16[2,8,1024]{2,1,0:T(8,128)(2,1)}, bf16[2,8,1024]{2,1,0:T(8,128)(2,1)S(1)}, u32[]{:S(2)}, u32[]{:S(2)}) collective-permute-start(bf16[2,8,1024]{2,1,0:T(8,128)(2,1)} %param.10), channel_id=1, source_target_pairs={{0,4},{1,5},{2,6},{3,7},{4,0},{5,1},{6,2},{7,3},{8,12},{9,13},{10,... | collective-permute-start | bytes 98312 | tf_op jit(solution)/shard_map/ppermute | solution.py:456
  7.7 0.8 constant_dynamic-update-slice_fusion.1
  8.5 0.7 collective-permute-done
  9.3 0.1 constant_dynamic-slice_fusion.3
  9.4 2.6 %collective-permute-start.3 = (bf16[2,16,128]{2,1,0:T(8,128)(2,1)S(1)}, bf16[2,16,128]{2,1,0:T(8,128)(2,1)S(1)}, u32[]{:S(2)}, u32[]{:S(2)}) collective-permute-start(bf16[2,16,128]{2,1,0:T(8,128)(2,1)S(1)} %get-tuple-element.30), channel_id=1, source_target_pairs={{0,3},{1,0},{2,1},{3,2},{4,7},{5,4},{6,5},{7,6},{8,11},{9,8},{10,9... | collective-permute-start | bytes 24584 | tf_op jit(solution)/shard_map/ppermute | solution.py:461
  11.9 0.5 collective-permute-start.2
  12.4 0.6 collective-permute-start.1
  13.0 0.0 collective-permute-done.3
  13.0 2.9 %collective-permute-done.2 = bf16[2,16,128]{2,1,0:T(8,128)(2,1)S(1)} collective-permute-done((bf16[2,16,128]{2,1,0:T(8,128)(2,1)S(1)}, bf16[2,16,128]{2,1,0:T(8,128)(2,1)S(1)}, u32[]{:S(2)}, u32[]{:S(2)}) %collective-permute-start.2) | collective-permute-done | bytes 8224 | tf_op jit(solution)/shard_map/ppermute | solution.py:461
  15.9 0.2 collective-permute-done.1
  16.2 2.8 %collective-permute-start.6 = (bf16[1,2,64,128]{3,2,1,0:T(8,128)(2,1)S(1)}, bf16[1,2,64,128]{3,2,1,0:T(8,128)(2,1)S(1)}, u32[]{:S(2)}, u32[]{:S(2)}) collective-permute-start(bf16[1,2,64,128]{3,2,1,0:T(8,128)(2,1)S(1)} %maximum_bitcast_fusion), channel_id=1, source_target_pairs={{0,192},{8,200},{16,208},{24,216},{32,224},{40,232},{48,240},{56,2... | collective-permute-start | bytes 98312 | tf_op jit(solution)/shard_map/ppermute | solution.py:464
  19.0 0.0 collective-permute-start.5
  19.0 0.3 collective-permute-start.4
  19.3 0.0 copy-start.2
  19.3 1.0 copy-done.2
  20.3 1.4 spread.1
  21.8 0.0 collective-permute-done.6
  21.8 0.9 collective-permute-done.5
  22.7 0.9 collective-permute-done.4
  23.5 5.2 %all-to-all-start = ((bf16[16,2,4,16,128]{4,3,2,1,0:T(8,128)(2,1)}), bf16[16,2,4,16,128]{4,3,2,1,0:T(8,128)(2,1)S(1)}, u32[]{:S(2)}, u32[]{:S(2)}) async-start(bf16[16,2,4,16,128]{4,3,2,1,0:T(8,128)(2,1)} %spread.1), calls=%async_computation | async-start | bytes 1048576 | tf_op jit(solution)/shard_map/all_to_all | solution.py:468
  28.8 2.6 %collective-permute-start.9 = (bf16[4,2,64,128]{3,2,1,0:T(8,128)(2,1)S(1)}, bf16[4,2,64,128]{3,2,1,0:T(8,128)(2,1)S(1)}, u32[]{:S(2)}, u32[]{:S(2)}) collective-permute-start(bf16[4,2,64,128]{3,2,1,0:T(8,128)(2,1)S(1)} %pad_maximum_fusion.1.root_ref), channel_id=1, source_target_pairs={{0,48},{8,56},{16,0},{24,8},{32,16},{40,24},{48,32},{56,40},{64,11... | collective-permute-start | bytes 393224 | tf_op jit(solution)/shard_map/ppermute | solution.py:471
  31.4 0.6 collective-permute-start.8
  31.9 0.6 collective-permute-start.7
  32.5 0.0 copy-done.6
  32.5 0.1 reshape.6
  32.6 0.0 copy-done.3
  32.6 0.0 copy-done.4
  32.6 0.0 copy-done.5
  32.6 0.1 concatenate.15.table_ref
  32.7 0.0 copy-done
  32.7 0.0 copy-done.1
  32.7 5.3 %attend_near.1 = (f32[512,1024]{1,0:T(8,128)}, f32[512,128]{1,0:T(8,128)S(1)}, f32[512,128]{1,0:T(8,128)S(1)}, f32[8,512]{1,0:T(8,128)S(1)}) custom-call(s32[353]{0:T(512)S(1)} %concatenate.15.table_ref, bf16[4,2,64,128]{3,2,1,0:T(8,128)(2,1)S(1)} %pad_maximum_fusion.1.root_ref, bf16[2,512,128]{2,1,0:T(8,128)(2,1)S(1)} %copy-done.1, ...), custom_call_target="tpu_custom_call" | custom-call | tf_op jit(solution)/shard_map/attend_near/pallas_call | solution.py:368
  38.0 0.0 collective-permute-done.9
  38.0 0.0 collective-permute-done.8
  38.0 2.7 %collective-permute-done.7 = bf16[4,2,64,128]{3,2,1,0:T(8,128)(2,1)S(1)} collective-permute-done((bf16[4,2,64,128]{3,2,1,0:T(8,128)(2,1)S(1)}, bf16[4,2,64,128]{3,2,1,0:T(8,128)(2,1)S(1)}, u32[]{:S(2)}, u32[]{:S(2)}) %collective-permute-start.7) | collective-permute-done | bytes 131104 | tf_op jit(solution)/shard_map/ppermute | solution.py:471
  40.7 0.1 pad_maximum_fusion.mine_ref
  40.7 0.0 all-to-all-done.mine_ref
  40.8 5.2 %collective-permute-start.10 = (bf16[16,2,4,16,128]{4,3,2,1,0:T(8,128)(2,1)S(1)}, bf16[16,2,4,16,128]{4,3,2,1,0:T(8,128)(2,1)S(1)}, u32[]{:S(2)}, u32[]{:S(2)}) collective-permute-start(bf16[16,2,4,16,128]{4,3,2,1,0:T(8,128)(2,1)S(1)} %all-to-all-done.mine_ref), channel_id=1, source_target_pairs={{0,8},{8,0},{16,24},{24,16},{32,40},{40,32},{48,56},{56,48},{64,72... | collective-permute-start | bytes 1572872 | tf_op jit(solution)/shard_map/ppermute | solution.py:474
  46.0 0.0 collective-permute-start.11
  46.0 1.5 collective-permute-done.10.other_ref
  47.5 1.7 select_pieces.1
  49.2 4.7 %all-to-all-start.1 = ((bf16[16,2,2,16,128]{4,3,2,1,0:T(8,128)(2,1)}), bf16[16,2,2,16,128]{4,3,2,1,0:T(8,128)(2,1)S(1)}, u32[]{:S(2)}, u32[]{:S(2)}) async-start(bf16[16,2,2,16,128]{4,3,2,1,0:T(8,128)(2,1)} %select_pieces.1), calls=%async_computation.1 | async-start | bytes 524288 | tf_op jit(solution)/shard_map/all_to_all | solution.py:476
  53.9 0.0 collective-permute-done.11.other_ref
  53.9 9.0 %attend_far.1 = (f32[512,1024]{1,0:T(8,128)}, f32[512,128]{1,0:T(8,128)S(1)}) custom-call(bf16[16,2,64,128]{3,2,1,0:T(8,128)(2,1)S(1)} %pad_maximum_fusion.mine_ref, bf16[16,2,64,128]{3,2,1,0:T(8,128)(2,1)S(1)} %collective-permute-done.11.other_ref, bf16[512,1024]{1,0:T(8,128)(2,1)S(1)} %copy-done), custom_call_target="tpu_custom_call" | custom-call | tf_op jit(solution)/shard_map/attend_far/pallas_call | solution.py:390
  63.0 0.8 all-to-all-done.1.node_ref
  63.8 130.3 %attend_nodes.1 = (bf16[512,1024]{1,0:T(8,128)(2,1)}, f32[512,1024]{1,0:T(8,128)}, f32[512,1024]{1,0:T(8,128)}) custom-call(bf16[16,2,2,16,128]{4,3,2,1,0:T(8,128)(2,1)S(1)} %all-to-all-done.1.node_ref, f32[512,128]{1,0:T(8,128)S(1)} %get-tuple-element.21.down_ref, ...), custom_call_target="tpu_custom_call", output_to_operand_aliasing={{1}: (9, {}), {2}: (10, {})} | custom-call | tf_op jit(solution)/shard_map/attend_nodes/pallas_call | solution.py:408
  (7 shorter events, 0.0 us)
Async XLA Ops:
  0.0 32.7 %copy-start = (bf16[512,1024]{1,0:T(8,128)(2,1)S(1)}, bf16[512,1024]{1,0:T(8,128)(2,1)}, u32[]{:S(2)}) copy-start(bf16[512,1024]{1,0:T(8,128)(2,1)} %q_ref.5) | copy-start | bytes 3145732
  0.0 32.7 %copy-start.1 = (bf16[2,512,128]{2,1,0:T(8,128)(2,1)S(1)}, bf16[2,512,128]{2,1,0:T(8,128)(2,1)}, u32[]{:S(2)}) copy-start(bf16[2,512,128]{2,1,0:T(8,128)(2,1)} %leaf_ref.3) | copy-start | bytes 786436
  0.0 9.3 %collective-permute-start = (bf16[2,8,1024]{2,1,0:T(8,128)(2,1)}, bf16[2,8,1024]{2,1,0:T(8,128)(2,1)S(1)}, u32[]{:S(2)}, u32[]{:S(2)}) collective-permute-start(bf16[2,8,1024]{2,1,0:T(8,128)(2,1)} %param.10), channel_id=1, source_target_pairs={{0,4},{1,5},{2,6},{3,7},{4,0},{5,1},{6,2},{7,3},{8,12},{9,13},{10,... | collective-permute-start | bytes 98312 | tf_op jit(solution)/shard_map/ppermute | solution.py:456
  9.4 3.7 %collective-permute-start.3 = (bf16[2,16,128]{2,1,0:T(8,128)(2,1)S(1)}, bf16[2,16,128]{2,1,0:T(8,128)(2,1)S(1)}, u32[]{:S(2)}, u32[]{:S(2)}) collective-permute-start(bf16[2,16,128]{2,1,0:T(8,128)(2,1)S(1)} %get-tuple-element.30), channel_id=1, source_target_pairs={{0,3},{1,0},{2,1},{3,2},{4,7},{5,4},{6,5},{7,6},{8,11},{9,8},{10,9... | collective-permute-start | bytes 24584 | tf_op jit(solution)/shard_map/ppermute | solution.py:461
  11.9 4.0 %collective-permute-start.2 = (bf16[2,16,128]{2,1,0:T(8,128)(2,1)S(1)}, bf16[2,16,128]{2,1,0:T(8,128)(2,1)S(1)}, u32[]{:S(2)}, u32[]{:S(2)}) collective-permute-start(bf16[2,16,128]{2,1,0:T(8,128)(2,1)S(1)} %get-tuple-element.31), channel_id=1, source_target_pairs={{0,2},{1,3},{2,0},{3,1},{4,6},{5,7},{6,4},{7,5},{8,10},{9,11},{10,... | collective-permute-start | bytes 24584 | tf_op jit(solution)/shard_map/ppermute | solution.py:461
  12.4 3.7 %collective-permute-start.1 = (bf16[2,16,128]{2,1,0:T(8,128)(2,1)S(1)}, bf16[2,16,128]{2,1,0:T(8,128)(2,1)S(1)}, u32[]{:S(2)}, u32[]{:S(2)}) collective-permute-start(bf16[2,16,128]{2,1,0:T(8,128)(2,1)S(1)} %get-tuple-element.32), channel_id=1, source_target_pairs={{0,1},{1,2},{2,3},{3,0},{4,5},{5,6},{6,7},{7,4},{8,9},{9,10},{10,1... | collective-permute-start | bytes 24584 | tf_op jit(solution)/shard_map/ppermute | solution.py:461
  16.2 5.6 %collective-permute-start.6 = (bf16[1,2,64,128]{3,2,1,0:T(8,128)(2,1)S(1)}, bf16[1,2,64,128]{3,2,1,0:T(8,128)(2,1)S(1)}, u32[]{:S(2)}, u32[]{:S(2)}) collective-permute-start(bf16[1,2,64,128]{3,2,1,0:T(8,128)(2,1)S(1)} %maximum_bitcast_fusion), channel_id=1, source_target_pairs={{0,192},{8,200},{16,208},{24,216},{32,224},{40,232},{48,240},{56,2... | collective-permute-start | bytes 98312 | tf_op jit(solution)/shard_map/ppermute | solution.py:464
  19.0 3.7 %collective-permute-start.5 = (bf16[1,2,64,128]{3,2,1,0:T(8,128)(2,1)S(1)}, bf16[1,2,64,128]{3,2,1,0:T(8,128)(2,1)S(1)}, u32[]{:S(2)}, u32[]{:S(2)}) collective-permute-start(bf16[1,2,64,128]{3,2,1,0:T(8,128)(2,1)S(1)} %maximum_bitcast_fusion), channel_id=1, source_target_pairs={{0,128},{8,136},{16,144},{24,152},{32,160},{40,168},{48,176},{56,1... | collective-permute-start | bytes 98312 | tf_op jit(solution)/shard_map/ppermute | solution.py:464
  19.0 4.6 %collective-permute-start.4 = (bf16[1,2,64,128]{3,2,1,0:T(8,128)(2,1)S(1)}, bf16[1,2,64,128]{3,2,1,0:T(8,128)(2,1)S(1)}, u32[]{:S(2)}, u32[]{:S(2)}) collective-permute-start(bf16[1,2,64,128]{3,2,1,0:T(8,128)(2,1)S(1)} %maximum_bitcast_fusion), channel_id=1, source_target_pairs={{0,64},{8,72},{16,80},{24,88},{32,96},{40,104},{48,112},{56,120},{... | collective-permute-start | bytes 98312 | tf_op jit(solution)/shard_map/ppermute | solution.py:464
  19.3 1.0 copy-start.2
  20.3 12.2 %copy-start.6 = (s32[32,2]{0,1:T(2,128)S(1)}, s32[32,2]{0,1:T(2,128)}, u32[]{:S(2)}) copy-start(s32[32,2]{0,1:T(2,128)} %param.15) | copy-start | bytes 772
  20.3 12.3 %copy-start.3 = (s32[32]{0:T(128)S(1)}, s32[32]{0:T(128)}, u32[]{:S(2)}) copy-start(s32[32]{0:T(128)} %param.14) | copy-start | bytes 388
  20.3 12.3 %copy-start.4 = (s32[128]{0:T(128)S(1)}, s32[128]{0:T(128)}, u32[]{:S(2)}) copy-start(s32[128]{0:T(128)} %param.13) | copy-start | bytes 1540
  20.3 12.3 %copy-start.5 = (s32[128]{0:T(128)S(1)}, s32[128]{0:T(128)}, u32[]{:S(2)}) copy-start(s32[128]{0:T(128)} %param.12) | copy-start | bytes 1540
  23.5 17.2 %all-to-all-start = ((bf16[16,2,4,16,128]{4,3,2,1,0:T(8,128)(2,1)}), bf16[16,2,4,16,128]{4,3,2,1,0:T(8,128)(2,1)S(1)}, u32[]{:S(2)}, u32[]{:S(2)}) async-start(bf16[16,2,4,16,128]{4,3,2,1,0:T(8,128)(2,1)} %spread.1), calls=%async_computation | async-start | bytes 1048576 | tf_op jit(solution)/shard_map/all_to_all | solution.py:468
  28.8 9.2 %collective-permute-start.9 = (bf16[4,2,64,128]{3,2,1,0:T(8,128)(2,1)S(1)}, bf16[4,2,64,128]{3,2,1,0:T(8,128)(2,1)S(1)}, u32[]{:S(2)}, u32[]{:S(2)}) collective-permute-start(bf16[4,2,64,128]{3,2,1,0:T(8,128)(2,1)S(1)} %pad_maximum_fusion.1.root_ref), channel_id=1, source_target_pairs={{0,48},{8,56},{16,0},{24,8},{32,16},{40,24},{48,32},{56,40},{64,11... | collective-permute-start | bytes 393224 | tf_op jit(solution)/shard_map/ppermute | solution.py:471
  31.4 6.6 %collective-permute-start.8 = (bf16[4,2,64,128]{3,2,1,0:T(8,128)(2,1)S(1)}, bf16[4,2,64,128]{3,2,1,0:T(8,128)(2,1)S(1)}, u32[]{:S(2)}, u32[]{:S(2)}) collective-permute-start(bf16[4,2,64,128]{3,2,1,0:T(8,128)(2,1)S(1)} %pad_maximum_fusion.1.root_ref), channel_id=1, source_target_pairs={{0,32},{8,40},{16,48},{24,56},{32,0},{40,8},{48,16},{56,24},{64,96... | collective-permute-start | bytes 393224 | tf_op jit(solution)/shard_map/ppermute | solution.py:471
  31.9 8.7 %collective-permute-start.7 = (bf16[4,2,64,128]{3,2,1,0:T(8,128)(2,1)S(1)}, bf16[4,2,64,128]{3,2,1,0:T(8,128)(2,1)S(1)}, u32[]{:S(2)}, u32[]{:S(2)}) collective-permute-start(bf16[4,2,64,128]{3,2,1,0:T(8,128)(2,1)S(1)} %pad_maximum_fusion.1.root_ref), channel_id=1, source_target_pairs={{0,16},{8,24},{16,32},{24,40},{32,48},{40,56},{48,0},{56,8},{64,80... | collective-permute-start | bytes 393224 | tf_op jit(solution)/shard_map/ppermute | solution.py:471
  40.8 6.8 %collective-permute-start.10 = (bf16[16,2,4,16,128]{4,3,2,1,0:T(8,128)(2,1)S(1)}, bf16[16,2,4,16,128]{4,3,2,1,0:T(8,128)(2,1)S(1)}, u32[]{:S(2)}, u32[]{:S(2)}) collective-permute-start(bf16[16,2,4,16,128]{4,3,2,1,0:T(8,128)(2,1)S(1)} %all-to-all-done.mine_ref), channel_id=1, source_target_pairs={{0,8},{8,0},{16,24},{24,16},{32,40},{40,32},{48,56},{56,48},{64,72... | collective-permute-start | bytes 1572872 | tf_op jit(solution)/shard_map/ppermute | solution.py:474
  46.0 7.9 %collective-permute-start.11 = (bf16[16,2,64,128]{3,2,1,0:T(8,128)(2,1)S(1)}, bf16[16,2,64,128]{3,2,1,0:T(8,128)(2,1)S(1)}, u32[]{:S(2)}, u32[]{:S(2)}) collective-permute-start(bf16[16,2,64,128]{3,2,1,0:T(8,128)(2,1)S(1)} %pad_maximum_fusion.mine_ref), channel_id=1, source_target_pairs={{0,8},{8,0},{16,24},{24,16},{32,40},{40,32},{48,56},{56,48},{64,72... | collective-permute-start | bytes 1572872 | tf_op jit(solution)/shard_map/ppermute | solution.py:473
  49.2 14.6 %all-to-all-start.1 = ((bf16[16,2,2,16,128]{4,3,2,1,0:T(8,128)(2,1)}), bf16[16,2,2,16,128]{4,3,2,1,0:T(8,128)(2,1)S(1)}, u32[]{:S(2)}, u32[]{:S(2)}) async-start(bf16[16,2,2,16,128]{4,3,2,1,0:T(8,128)(2,1)} %select_pieces.1), calls=%async_computation.1 | async-start | bytes 524288 | tf_op jit(solution)/shard_map/all_to_all | solution.py:476

commit v5 on v4

--- a/solution.py
+++ b/solution.py
@@ -25,6 +25,8 @@
 SPREAD = 4
 GROUP = 4
 NODE_GROUPS = ((0, 1, 2, 3, 4, 5), (6, 7))
+EARLY_HEADS = 5
+FAR_EARLY_HEADS = 2
 SCORE_SCALE = HD**-0.5
 LOG_SCALE = SCORE_SCALE * 1.4426950408889634
 MASKED = -1e30
@@ -190,16 +192,39 @@
         copy.wait()
 
 
-def far_kernel(mine_ref, other_ref, q_ref, sums_hbm, totals_ref, keys, values, sums, sems):
+def far_kernel(
+    mine_ref,
+    other_ref,
+    q_ref,
+    near_totals_ref,
+    near_sums_hbm,
+    sums_hbm,
+    totals_ref,
+    keys,
+    values,
+    sums,
+    sems,
+):
+    arrival = pltpu.make_async_copy(near_sums_hbm, sums, sems.at[HEADS_DEV // GROUP])
+    arrival.start()
     store_root(keys, values, 0, mine_ref[NEAR:])
     store_root(keys, values, (CHIPS - NEAR) * TOKENS, other_ref)
     copies = []
+    held = []
     for head in range(HEADS_DEV):
         columns = slice(head * HD, (head + 1) * HD)
-        acc = weigh(scaled_query(q_ref[:, columns]), keys[...], values[...])
-        sums[:, columns] = acc[:, :HD]
-        store_total(totals_ref, head, acc[:, HD:])
-        store_group(copies, sums, sums_hbm, sems, head)
+        held.append((head, weigh(scaled_query(q_ref[:, columns]), keys[...], values[...])))
+        if head + 1 < FAR_EARLY_HEADS:
+            continue
+        if head + 1 == FAR_EARLY_HEADS:
+            arrival.wait()
+        for place, acc in held:
+            columns = slice(place * HD, (place + 1) * HD)
+            sums[:, columns] += acc[:, :HD]
+            store_total(totals_ref, place, acc[:, HD:])
+            store_group(copies, sums, sums_hbm, sems, place)
+        held = []
+    totals_ref[...] += near_totals_ref[...]
     for copy in copies:
         copy.wait()
 
@@ -208,32 +233,24 @@
     node_ref,
     down_ref,
     along_ref,
-    near_totals_ref,
-    far_totals_ref,
+    totals_ref,
     q_ref,
     mine_ref,
     other_ref,
     leaf_ref,
-    near_sums_hbm,
-    far_sums_hbm,
+    sums_hbm,
     out_ref,
     _,
-    __,
     keys,
     values,
     root_vmem,
     all_keys,
-    near_sums,
-    far_sums,
+    earlier_sums,
     result,
     sems,
 ):
-    arrivals = (
-        pltpu.make_async_copy(near_sums_hbm, near_sums, sems.at[0]),
-        pltpu.make_async_copy(far_sums_hbm, far_sums, sems.at[1]),
-    )
-    for arrival in arrivals:
-        arrival.start()
+    arrival = pltpu.make_async_copy(sums_hbm, earlier_sums, sems.at[0])
+    arrival.start()
     shown = down_ref[...] > 0.5
     node_keys = node_ref[:, 0].reshape(NODE_ROWS, HD).astype(f32)
     node_values = node_ref[:, 1].reshape(NODE_ROWS, HD).astype(f32)
@@ -243,25 +260,26 @@
 
     outside = jnp.zeros((LEAF_LEN, HD), f32)
     copies = []
+    held = []
     for heads in NODE_GROUPS:
-        mixed = [
-            weigh(scaled_query(q_ref[:, head * HD : (head + 1) * HD]), keys[...], values[...])
-            for head in heads
-        ]
-        if not copies:
-            for arrival in arrivals:
+        for head in heads:
+            columns = slice(head * HD, (head + 1) * HD)
+            held.append((head, weigh(scaled_query(q_ref[:, columns]), keys[...], values[...])))
+            if head + 1 < EARLY_HEADS:
+                continue
+            if head + 1 == EARLY_HEADS:
                 arrival.wait()
-        for head, acc in zip(heads, mixed):
-            columns = slice(head * HD, (head + 1) * HD)
-            place = total_column(head)
-            earlier = near_totals_ref[...] + far_totals_ref[...]
-            total = acc[:, HD:] + earlier[:, place : place + 1]
-            outside = jnp.where((total >= TOTAL_MIN) & (total <= TOTAL_MAX), outside, 1.0)
-            sums = acc[:, :HD] + (near_sums[:, columns] + far_sums[:, columns])
-            result[:, columns] = (sums / total).astype(bf16)
+            for place, acc in held:
+                columns = slice(place * HD, (place + 1) * HD)
+                first = total_column(place)
+                total = acc[:, HD:] + totals_ref[:, first : first + 1]
+                outside = jnp.where((total >= TOTAL_MIN) & (total <= TOTAL_MAX), outside, 1.0)
+                sums = acc[:, :HD] + earlier_sums[:, columns]
+                result[:, columns] = (sums / total).astype(bf16)
+            held = []
         part = slice(heads[0] * HD, (heads[-1] + 1) * HD)
         copy = pltpu.make_async_copy(
-            result.at[:, part], out_ref.at[:, part], sems.at[2 + len(copies)]
+            result.at[:, part], out_ref.at[:, part], sems.at[1 + len(copies)]
         )
         copy.start()
         copies.append(copy)
@@ -385,59 +403,55 @@
     )(table, root, leaf_kv, queries)
 
 
-def attend_far(mine, other, queries):
+def attend_far(mine, other, queries, totals, sums):
     count = ROOT - NEAR * TOKENS
     return pl.pallas_call(
         far_kernel,
-        in_specs=[vmem] * 3,
+        in_specs=[vmem] * 4 + [anywhere],
         out_specs=[anywhere, vmem],
         out_shape=sums_out,
+        input_output_aliases={4: 0},
         scratch_shapes=[
             pltpu.VMEM((2 * HD, count), bf16),
             pltpu.VMEM((count, 2 * HD), bf16),
             pltpu.VMEM(sums_shape, f32),
-            pltpu.SemaphoreType.DMA((HEADS_DEV // GROUP,)),
+            pltpu.SemaphoreType.DMA((HEADS_DEV // GROUP + 1,)),
         ],
         compiler_params=limit(32),
         name="attend_far",
-    )(mine, other, queries)
-
-
-def attend_nodes(nodes, masks, near_part, far_part, queries, mine, other, leaf_kv):
-    (near_sums, near_totals), (far_sums, far_totals) = near_part, far_part
+    )(mine, other, queries, totals, sums)
+
+
+def attend_nodes(nodes, masks, totals, sums, queries, mine, other, leaf_kv):
     return pl.pallas_call(
         node_kernel,
-        in_specs=[vmem] * 6 + [anywhere] * 5,
-        out_specs=[anywhere] * 3,
+        in_specs=[vmem] * 5 + [anywhere] * 4,
+        out_specs=[anywhere] * 2,
         out_shape=[
             jax.ShapeDtypeStruct((LEAF_LEN, HEADS_DEV * HD), bf16),
             pltpu.HBM(sums_shape, f32),
-            pltpu.HBM(sums_shape, f32),
         ],
-        input_output_aliases={9: 1, 10: 2},
+        input_output_aliases={8: 1},
         scratch_shapes=[
             pltpu.VMEM((2 * HD, NODE_ROWS), bf16),
             pltpu.VMEM((NODE_ROWS, 2 * HD), bf16),
             pltpu.VMEM((CORES,) + mine.shape, bf16),
             pltpu.VMEM((2, KEYS, HD), bf16),
             pltpu.VMEM(sums_shape, f32),
-            pltpu.VMEM(sums_shape, f32),
             pltpu.VMEM((LEAF_LEN, HEADS_DEV * HD), bf16),
-            pltpu.SemaphoreType.DMA((2 + len(NODE_GROUPS),)),
+            pltpu.SemaphoreType.DMA((1 + len(NODE_GROUPS),)),
         ],
         compiler_params=limit(32),
         name="attend_nodes",
     )(
         nodes,
         *masks,
-        near_totals,
-        far_totals,
+        totals,
         queries,
         mine,
         other,
         leaf_kv,
-        near_sums,
-        far_sums,
+        sums,
     )[0]
 
 
@@ -475,9 +489,8 @@
     chosen = select_pieces(table, mine, other)
     nodes = lax.all_to_all(chosen, "blk", 0, 0, tiled=True, axis_index_groups=SAME_CORE)
 
-    near_part = near_sums, near_totals
-    far_part = attend_far(root, root_other, queries)
-    return attend_nodes(nodes, masks, near_part, far_part, queries, root, root_other, leaf_kv)
+    sums, totals = attend_far(root, root_other, queries, near_totals, near_sums)
+    return attend_nodes(nodes, masks, totals, sums, queries, root, root_other, leaf_kv)
 
 
 def solution(mesh):

time: 195 us -> 194 us (level)
  no operation moved by 1% of the time
where the time goes in v5:
time: 194 us
  Pallas kernels  147 us (76%)
  starting transfers between devices  33.4 us (17%)
  waiting for transfers between devices  10.2 us (5%)
  local copies, waits for them, and re-layouts  2.13 us (1%)
    pallas_call x1, Pallas kernels, attend_nodes(): pl.pallas_call(node_kernel, in_specs=[vmem] * 5 + [anywhere] * 4, out_spe...  130 us
    pallas_call x1, Pallas kernels, attend_far(): pl.pallas_call(far_kernel, in_specs=[vmem] * 4 + [anywhere], out_specs=[a...  9.45 us
    ppermute x1, starting transfers between devices, per_device(): away = lax.ppermute(root_kv, 'tp', swap)  7.74 us
    pallas_call x1, Pallas kernels, attend_near(): pl.pallas_call(near_kernel, in_specs=[smem] + [vmem] * 3, out_specs=[anyw...  5.29 us
    all_to_all x1, starting transfers between devices, per_device(): lax.all_to_all(pieces, 'blk', 0, 0, tiled=True, axis_index_groups=SAME_CORE)  5.22 us
    ppermute x1, starting transfers between devices, per_device(): other = lax.ppermute(mine, 'blk', shifted(0, 0, 1))  5.22 us
    all_to_all x1, starting transfers between devices, per_device(): lax.all_to_all(chosen, 'blk', 0, 0, tiled=True, axis_index_groups=SAME_CORE)  4.71 us
  transfers between devices with their start and end apart: 14, of which 8 were waited for; matrix products, arithmetic and copies ran while one was open for 1% of the time, Pallas kernels for 9%

profile of v5, /device:TPU:1, one launch (start us, length us, event | category | flops | bytes accessed | tf_op | source)
XLA Modules:
  0.0 193.6 jit_solution(8743513877760091223)
XLA Ops:
  0.0 0.0 copy-start
  0.0 0.0 copy-start.1
  0.0 7.7 %collective-permute-start = (bf16[2,8,1024]{2,1,0:T(8,128)(2,1)}, bf16[2,8,1024]{2,1,0:T(8,128)(2,1)S(1)}, u32[]{:S(2)}, u32[]{:S(2)}) collective-permute-start(bf16[2,8,1024]{2,1,0:T(8,128)(2,1)} %param.10), channel_id=1, source_target_pairs={{0,4},{1,5},{2,6},{3,7},{4,0},{5,1},{6,2},{7,3},{8,12},{9,13},{10,... | collective-permute-start | bytes 98312 | tf_op jit(solution)/shard_map/ppermute | solution.py:470
  7.7 0.8 constant_dynamic-update-slice_fusion.1
  8.5 0.7 collective-permute-done
  9.3 0.1 constant_dynamic-slice_fusion.3
  9.4 2.6 %collective-permute-start.3 = (bf16[2,16,128]{2,1,0:T(8,128)(2,1)S(1)}, bf16[2,16,128]{2,1,0:T(8,128)(2,1)S(1)}, u32[]{:S(2)}, u32[]{:S(2)}) collective-permute-start(bf16[2,16,128]{2,1,0:T(8,128)(2,1)S(1)} %get-tuple-element.30), channel_id=1, source_target_pairs={{0,3},{1,0},{2,1},{3,2},{4,7},{5,4},{6,5},{7,6},{8,11},{9,8},{10,9... | collective-permute-start | bytes 24584 | tf_op jit(solution)/shard_map/ppermute | solution.py:475
  11.9 0.5 collective-permute-start.2
  12.4 0.6 collective-permute-start.1
  13.0 0.0 collective-permute-done.3
  13.0 2.9 %collective-permute-done.2 = bf16[2,16,128]{2,1,0:T(8,128)(2,1)S(1)} collective-permute-done((bf16[2,16,128]{2,1,0:T(8,128)(2,1)S(1)}, bf16[2,16,128]{2,1,0:T(8,128)(2,1)S(1)}, u32[]{:S(2)}, u32[]{:S(2)}) %collective-permute-start.2) | collective-permute-done | bytes 8224 | tf_op jit(solution)/shard_map/ppermute | solution.py:475
  15.9 0.2 collective-permute-done.1
  16.2 2.8 %collective-permute-start.6 = (bf16[1,2,64,128]{3,2,1,0:T(8,128)(2,1)S(1)}, bf16[1,2,64,128]{3,2,1,0:T(8,128)(2,1)S(1)}, u32[]{:S(2)}, u32[]{:S(2)}) collective-permute-start(bf16[1,2,64,128]{3,2,1,0:T(8,128)(2,1)S(1)} %maximum_bitcast_fusion), channel_id=1, source_target_pairs={{0,192},{8,200},{16,208},{24,216},{32,224},{40,232},{48,240},{56,2... | collective-permute-start | bytes 98312 | tf_op jit(solution)/shard_map/ppermute | solution.py:478
  19.0 0.0 collective-permute-start.5
  19.0 0.3 collective-permute-start.4
  19.3 0.0 copy-start.2
  19.3 1.0 copy-done.2
  20.3 1.4 spread.1
  21.8 0.0 collective-permute-done.6
  21.8 0.9 collective-permute-done.5
  22.7 0.9 collective-permute-done.4
  23.5 5.2 %all-to-all-start = ((bf16[16,2,4,16,128]{4,3,2,1,0:T(8,128)(2,1)}), bf16[16,2,4,16,128]{4,3,2,1,0:T(8,128)(2,1)S(1)}, u32[]{:S(2)}, u32[]{:S(2)}) async-start(bf16[16,2,4,16,128]{4,3,2,1,0:T(8,128)(2,1)} %spread.1), calls=%async_computation | async-start | bytes 1048576 | tf_op jit(solution)/shard_map/all_to_all | solution.py:482
  28.8 2.6 %collective-permute-start.9 = (bf16[4,2,64,128]{3,2,1,0:T(8,128)(2,1)S(1)}, bf16[4,2,64,128]{3,2,1,0:T(8,128)(2,1)S(1)}, u32[]{:S(2)}, u32[]{:S(2)}) collective-permute-start(bf16[4,2,64,128]{3,2,1,0:T(8,128)(2,1)S(1)} %pad_maximum_fusion.1.root_ref), channel_id=1, source_target_pairs={{0,48},{8,56},{16,0},{24,8},{32,16},{40,24},{48,32},{56,40},{64,11... | collective-permute-start | bytes 393224 | tf_op jit(solution)/shard_map/ppermute | solution.py:485
  31.4 0.6 collective-permute-start.8
  31.9 0.6 collective-permute-start.7
  32.5 0.0 copy-done.6
  32.5 0.1 reshape.6
  32.6 0.0 copy-done.3
  32.6 0.0 copy-done.4
  32.6 0.0 copy-done.5
  32.6 0.1 concatenate.15.table_ref
  32.7 0.0 copy-done
  32.7 0.0 copy-done.1
  32.7 5.3 %attend_near.1 = (f32[512,1024]{1,0:T(8,128)}, f32[512,128]{1,0:T(8,128)S(1)}, f32[512,128]{1,0:T(8,128)S(1)}, f32[8,512]{1,0:T(8,128)S(1)}) custom-call(s32[353]{0:T(512)S(1)} %concatenate.15.table_ref, bf16[4,2,64,128]{3,2,1,0:T(8,128)(2,1)S(1)} %pad_maximum_fusion.1.root_ref, bf16[2,512,128]{2,1,0:T(8,128)(2,1)S(1)} %copy-done.1, ...), custom_call_target="tpu_custom_call" | custom-call | tf_op jit(solution)/shard_map/attend_near/pallas_call | solution.py:386
  38.0 0.0 collective-permute-done.9
  38.0 0.0 collective-permute-done.8
  38.0 2.7 %collective-permute-done.7 = bf16[4,2,64,128]{3,2,1,0:T(8,128)(2,1)S(1)} collective-permute-done((bf16[4,2,64,128]{3,2,1,0:T(8,128)(2,1)S(1)}, bf16[4,2,64,128]{3,2,1,0:T(8,128)(2,1)S(1)}, u32[]{:S(2)}, u32[]{:S(2)}) %collective-permute-start.7) | collective-permute-done | bytes 131104 | tf_op jit(solution)/shard_map/ppermute | solution.py:485
  40.7 0.1 pad_maximum_fusion.mine_ref
  40.7 0.0 all-to-all-done.mine_ref
  40.8 5.2 %collective-permute-start.10 = (bf16[16,2,4,16,128]{4,3,2,1,0:T(8,128)(2,1)S(1)}, bf16[16,2,4,16,128]{4,3,2,1,0:T(8,128)(2,1)S(1)}, u32[]{:S(2)}, u32[]{:S(2)}) collective-permute-start(bf16[16,2,4,16,128]{4,3,2,1,0:T(8,128)(2,1)S(1)} %all-to-all-done.mine_ref), channel_id=1, source_target_pairs={{0,8},{8,0},{16,24},{24,16},{32,40},{40,32},{48,56},{56,48},{64,72... | collective-permute-start | bytes 1572872 | tf_op jit(solution)/shard_map/ppermute | solution.py:488
  46.0 0.0 collective-permute-start.11
  46.0 1.5 collective-permute-done.10.other_ref
  47.5 1.7 select_pieces.1
  49.2 4.7 %all-to-all-start.1 = ((bf16[16,2,2,16,128]{4,3,2,1,0:T(8,128)(2,1)}), bf16[16,2,2,16,128]{4,3,2,1,0:T(8,128)(2,1)S(1)}, u32[]{:S(2)}, u32[]{:S(2)}) async-start(bf16[16,2,2,16,128]{4,3,2,1,0:T(8,128)(2,1)} %select_pieces.1), calls=%async_computation.1 | async-start | bytes 524288 | tf_op jit(solution)/shard_map/all_to_all | solution.py:490
  53.9 0.0 collective-permute-done.11.other_ref
  53.9 9.4 %attend_far.1 = (f32[512,1024]{1,0:T(8,128)}, f32[512,128]{1,0:T(8,128)S(1)}) custom-call(bf16[16,2,64,128]{3,2,1,0:T(8,128)(2,1)S(1)} %pad_maximum_fusion.mine_ref, bf16[16,2,64,128]{3,2,1,0:T(8,128)(2,1)S(1)} %collective-permute-done.11.other_ref, bf16[512,1024]{1,0:T(8,128)(2,1)S(1)} %copy-done, ...), custom_call_target="tpu_custom_call", output_to_operand_aliasing={{0}: (4, {})} | custom-call | tf_op jit(solution)/shard_map/attend_far/pallas_call | solution.py:408
  63.4 0.4 all-to-all-done.1.node_ref
  63.8 129.6 %attend_nodes.1 = (bf16[512,1024]{1,0:T(8,128)(2,1)}, f32[512,1024]{1,0:T(8,128)}) custom-call(bf16[16,2,2,16,128]{4,3,2,1,0:T(8,128)(2,1)S(1)} %all-to-all-done.1.node_ref, f32[512,128]{1,0:T(8,128)S(1)} %get-tuple-element.21.down_ref, f32[8,512]{1,0:T(8,128)S(1)} %get-tuple-element.22.along_ref, ...), custom_call_target="tpu_custom_call", output_to_operand_aliasing={{1}: (8, {})} | custom-call | tf_op jit(solution)/shard_map/attend_nodes/pallas_call | solution.py:426
  (7 shorter events, 0.0 us)
Async XLA Ops:
  0.0 32.7 %copy-start = (bf16[512,1024]{1,0:T(8,128)(2,1)S(1)}, bf16[512,1024]{1,0:T(8,128)(2,1)}, u32[]{:S(2)}) copy-start(bf16[512,1024]{1,0:T(8,128)(2,1)} %q_ref.5) | copy-start | bytes 3145732
  0.0 32.7 %copy-start.1 = (bf16[2,512,128]{2,1,0:T(8,128)(2,1)S(1)}, bf16[2,512,128]{2,1,0:T(8,128)(2,1)}, u32[]{:S(2)}) copy-start(bf16[2,512,128]{2,1,0:T(8,128)(2,1)} %leaf_ref.3) | copy-start | bytes 786436
  0.0 9.3 %collective-permute-start = (bf16[2,8,1024]{2,1,0:T(8,128)(2,1)}, bf16[2,8,1024]{2,1,0:T(8,128)(2,1)S(1)}, u32[]{:S(2)}, u32[]{:S(2)}) collective-permute-start(bf16[2,8,1024]{2,1,0:T(8,128)(2,1)} %param.10), channel_id=1, source_target_pairs={{0,4},{1,5},{2,6},{3,7},{4,0},{5,1},{6,2},{7,3},{8,12},{9,13},{10,... | collective-permute-start | bytes 98312 | tf_op jit(solution)/shard_map/ppermute | solution.py:470
  9.4 3.7 %collective-permute-start.3 = (bf16[2,16,128]{2,1,0:T(8,128)(2,1)S(1)}, bf16[2,16,128]{2,1,0:T(8,128)(2,1)S(1)}, u32[]{:S(2)}, u32[]{:S(2)}) collective-permute-start(bf16[2,16,128]{2,1,0:T(8,128)(2,1)S(1)} %get-tuple-element.30), channel_id=1, source_target_pairs={{0,3},{1,0},{2,1},{3,2},{4,7},{5,4},{6,5},{7,6},{8,11},{9,8},{10,9... | collective-permute-start | bytes 24584 | tf_op jit(solution)/shard_map/ppermute | solution.py:475
  11.9 4.0 %collective-permute-start.2 = (bf16[2,16,128]{2,1,0:T(8,128)(2,1)S(1)}, bf16[2,16,128]{2,1,0:T(8,128)(2,1)S(1)}, u32[]{:S(2)}, u32[]{:S(2)}) collective-permute-start(bf16[2,16,128]{2,1,0:T(8,128)(2,1)S(1)} %get-tuple-element.31), channel_id=1, source_target_pairs={{0,2},{1,3},{2,0},{3,1},{4,6},{5,7},{6,4},{7,5},{8,10},{9,11},{10,... | collective-permute-start | bytes 24584 | tf_op jit(solution)/shard_map/ppermute | solution.py:475
  12.4 3.7 %collective-permute-start.1 = (bf16[2,16,128]{2,1,0:T(8,128)(2,1)S(1)}, bf16[2,16,128]{2,1,0:T(8,128)(2,1)S(1)}, u32[]{:S(2)}, u32[]{:S(2)}) collective-permute-start(bf16[2,16,128]{2,1,0:T(8,128)(2,1)S(1)} %get-tuple-element.32), channel_id=1, source_target_pairs={{0,1},{1,2},{2,3},{3,0},{4,5},{5,6},{6,7},{7,4},{8,9},{9,10},{10,1... | collective-permute-start | bytes 24584 | tf_op jit(solution)/shard_map/ppermute | solution.py:475
  16.2 5.6 %collective-permute-start.6 = (bf16[1,2,64,128]{3,2,1,0:T(8,128)(2,1)S(1)}, bf16[1,2,64,128]{3,2,1,0:T(8,128)(2,1)S(1)}, u32[]{:S(2)}, u32[]{:S(2)}) collective-permute-start(bf16[1,2,64,128]{3,2,1,0:T(8,128)(2,1)S(1)} %maximum_bitcast_fusion), channel_id=1, source_target_pairs={{0,192},{8,200},{16,208},{24,216},{32,224},{40,232},{48,240},{56,2... | collective-permute-start | bytes 98312 | tf_op jit(solution)/shard_map/ppermute | solution.py:478
  19.0 3.7 %collective-permute-start.5 = (bf16[1,2,64,128]{3,2,1,0:T(8,128)(2,1)S(1)}, bf16[1,2,64,128]{3,2,1,0:T(8,128)(2,1)S(1)}, u32[]{:S(2)}, u32[]{:S(2)}) collective-permute-start(bf16[1,2,64,128]{3,2,1,0:T(8,128)(2,1)S(1)} %maximum_bitcast_fusion), channel_id=1, source_target_pairs={{0,128},{8,136},{16,144},{24,152},{32,160},{40,168},{48,176},{56,1... | collective-permute-start | bytes 98312 | tf_op jit(solution)/shard_map/ppermute | solution.py:478
  19.0 4.6 %collective-permute-start.4 = (bf16[1,2,64,128]{3,2,1,0:T(8,128)(2,1)S(1)}, bf16[1,2,64,128]{3,2,1,0:T(8,128)(2,1)S(1)}, u32[]{:S(2)}, u32[]{:S(2)}) collective-permute-start(bf16[1,2,64,128]{3,2,1,0:T(8,128)(2,1)S(1)} %maximum_bitcast_fusion), channel_id=1, source_target_pairs={{0,64},{8,72},{16,80},{24,88},{32,96},{40,104},{48,112},{56,120},{... | collective-permute-start | bytes 98312 | tf_op jit(solution)/shard_map/ppermute | solution.py:478
  19.3 1.0 copy-start.2
  20.3 12.2 %copy-start.6 = (s32[32,2]{0,1:T(2,128)S(1)}, s32[32,2]{0,1:T(2,128)}, u32[]{:S(2)}) copy-start(s32[32,2]{0,1:T(2,128)} %param.15) | copy-start | bytes 772
  20.3 12.3 %copy-start.3 = (s32[32]{0:T(128)S(1)}, s32[32]{0:T(128)}, u32[]{:S(2)}) copy-start(s32[32]{0:T(128)} %param.14) | copy-start | bytes 388
  20.3 12.3 %copy-start.4 = (s32[128]{0:T(128)S(1)}, s32[128]{0:T(128)}, u32[]{:S(2)}) copy-start(s32[128]{0:T(128)} %param.13) | copy-start | bytes 1540
  20.3 12.3 %copy-start.5 = (s32[128]{0:T(128)S(1)}, s32[128]{0:T(128)}, u32[]{:S(2)}) copy-start(s32[128]{0:T(128)} %param.12) | copy-start | bytes 1540
  23.5 17.2 %all-to-all-start = ((bf16[16,2,4,16,128]{4,3,2,1,0:T(8,128)(2,1)}), bf16[16,2,4,16,128]{4,3,2,1,0:T(8,128)(2,1)S(1)}, u32[]{:S(2)}, u32[]{:S(2)}) async-start(bf16[16,2,4,16,128]{4,3,2,1,0:T(8,128)(2,1)} %spread.1), calls=%async_computation | async-start | bytes 1048576 | tf_op jit(solution)/shard_map/all_to_all | solution.py:482
  28.8 9.2 %collective-permute-start.9 = (bf16[4,2,64,128]{3,2,1,0:T(8,128)(2,1)S(1)}, bf16[4,2,64,128]{3,2,1,0:T(8,128)(2,1)S(1)}, u32[]{:S(2)}, u32[]{:S(2)}) collective-permute-start(bf16[4,2,64,128]{3,2,1,0:T(8,128)(2,1)S(1)} %pad_maximum_fusion.1.root_ref), channel_id=1, source_target_pairs={{0,48},{8,56},{16,0},{24,8},{32,16},{40,24},{48,32},{56,40},{64,11... | collective-permute-start | bytes 393224 | tf_op jit(solution)/shard_map/ppermute | solution.py:485
  31.4 6.6 %collective-permute-start.8 = (bf16[4,2,64,128]{3,2,1,0:T(8,128)(2,1)S(1)}, bf16[4,2,64,128]{3,2,1,0:T(8,128)(2,1)S(1)}, u32[]{:S(2)}, u32[]{:S(2)}) collective-permute-start(bf16[4,2,64,128]{3,2,1,0:T(8,128)(2,1)S(1)} %pad_maximum_fusion.1.root_ref), channel_id=1, source_target_pairs={{0,32},{8,40},{16,48},{24,56},{32,0},{40,8},{48,16},{56,24},{64,96... | collective-permute-start | bytes 393224 | tf_op jit(solution)/shard_map/ppermute | solution.py:485
  31.9 8.7 %collective-permute-start.7 = (bf16[4,2,64,128]{3,2,1,0:T(8,128)(2,1)S(1)}, bf16[4,2,64,128]{3,2,1,0:T(8,128)(2,1)S(1)}, u32[]{:S(2)}, u32[]{:S(2)}) collective-permute-start(bf16[4,2,64,128]{3,2,1,0:T(8,128)(2,1)S(1)} %pad_maximum_fusion.1.root_ref), channel_id=1, source_target_pairs={{0,16},{8,24},{16,32},{24,40},{32,48},{40,56},{48,0},{56,8},{64,80... | collective-permute-start | bytes 393224 | tf_op jit(solution)/shard_map/ppermute | solution.py:485
  40.8 6.8 %collective-permute-start.10 = (bf16[16,2,4,16,128]{4,3,2,1,0:T(8,128)(2,1)S(1)}, bf16[16,2,4,16,128]{4,3,2,1,0:T(8,128)(2,1)S(1)}, u32[]{:S(2)}, u32[]{:S(2)}) collective-permute-start(bf16[16,2,4,16,128]{4,3,2,1,0:T(8,128)(2,1)S(1)} %all-to-all-done.mine_ref), channel_id=1, source_target_pairs={{0,8},{8,0},{16,24},{24,16},{32,40},{40,32},{48,56},{56,48},{64,72... | collective-permute-start | bytes 1572872 | tf_op jit(solution)/shard_map/ppermute | solution.py:488
  46.0 7.9 %collective-permute-start.11 = (bf16[16,2,64,128]{3,2,1,0:T(8,128)(2,1)S(1)}, bf16[16,2,64,128]{3,2,1,0:T(8,128)(2,1)S(1)}, u32[]{:S(2)}, u32[]{:S(2)}) collective-permute-start(bf16[16,2,64,128]{3,2,1,0:T(8,128)(2,1)S(1)} %pad_maximum_fusion.mine_ref), channel_id=1, source_target_pairs={{0,8},{8,0},{16,24},{24,16},{32,40},{40,32},{48,56},{56,48},{64,72... | collective-permute-start | bytes 1572872 | tf_op jit(solution)/shard_map/ppermute | solution.py:487
  49.2 14.6 %all-to-all-start.1 = ((bf16[16,2,2,16,128]{4,3,2,1,0:T(8,128)(2,1)}), bf16[16,2,2,16,128]{4,3,2,1,0:T(8,128)(2,1)S(1)}, u32[]{:S(2)}, u32[]{:S(2)}) async-start(bf16[16,2,2,16,128]{4,3,2,1,0:T(8,128)(2,1)} %select_pieces.1), calls=%async_computation.1 | async-start | bytes 524288 | tf_op jit(solution)/shard_map/all_to_all | solution.py:490

commit v6 on v5

--- a/solution.py
+++ b/solution.py
@@ -22,7 +22,7 @@
 NEAR = Z
 LEAVES = 32
 SLOT_LEAF, ANCESTORS, NODE_SLOT, NODE_LENS, BLK = 0, 32, 96, 224, 352
-SPREAD = 4
+SPREAD = 8
 GROUP = 4
 NODE_GROUPS = ((0, 1, 2, 3, 4, 5), (6, 7))
 EARLY_HEADS = 5

time: 194 us -> 194 us (level)
  transfers between devices with their start and end apart: 14 -> 14, of which waited for: 8 -> 9; matrix products, arithmetic and copies ran while one was open for 1% -> 1% of each run, Pallas kernels for 9% -> 9%
where the time goes in v6:
time: 194 us
  Pallas kernels  147 us (76%)
  starting transfers between devices  34.2 us (18%)
  waiting for transfers between devices  10 us (5%)
  local copies, waits for them, and re-layouts  2.13 us (1%)
    pallas_call x1, Pallas kernels, attend_nodes(): pl.pallas_call(node_kernel, in_specs=[vmem] * 5 + [anywhere] * 4, out_spe...  130 us
    pallas_call x1, Pallas kernels, attend_far(): pl.pallas_call(far_kernel, in_specs=[vmem] * 4 + [anywhere], out_specs=[a...  9.45 us
    ppermute x1, starting transfers between devices, per_device(): away = lax.ppermute(root_kv, 'tp', swap)  7.74 us
    ppermute x1, starting transfers between devices, per_device(): other = lax.ppermute(mine, 'blk', shifted(0, 0, 1))  6.56 us
    pallas_call x1, Pallas kernels, attend_near(): pl.pallas_call(near_kernel, in_specs=[smem] + [vmem] * 3, out_specs=[anyw...  5.29 us
    all_to_all x1, starting transfers between devices, per_device(): lax.all_to_all(chosen, 'blk', 0, 0, tiled=True, axis_index_groups=SAME_CORE)  4.71 us
    all_to_all x1, starting transfers between devices, per_device(): lax.all_to_all(pieces, 'blk', 0, 0, tiled=True, axis_index_groups=SAME_CORE)  4.67 us
  transfers between devices with their start and end apart: 14, of which 9 were waited for; matrix products, arithmetic and copies ran while one was open for 1% of the time, Pallas kernels for 9%

profile of v6, /device:TPU:1, one launch (start us, length us, event | category | flops | bytes accessed | tf_op | source)
XLA Modules:
  0.0 193.6 jit_solution(16985468092694949691)
XLA Ops:
  0.0 0.0 copy-start
  0.0 0.0 copy-start.1
  0.0 7.7 %collective-permute-start = (bf16[2,8,1024]{2,1,0:T(8,128)(2,1)}, bf16[2,8,1024]{2,1,0:T(8,128)(2,1)S(1)}, u32[]{:S(2)}, u32[]{:S(2)}) collective-permute-start(bf16[2,8,1024]{2,1,0:T(8,128)(2,1)} %param.10), channel_id=1, source_target_pairs={{0,4},{1,5},{2,6},{3,7},{4,0},{5,1},{6,2},{7,3},{8,12},{9,13},{10,... | collective-permute-start | bytes 98312 | tf_op jit(solution)/shard_map/ppermute | solution.py:470
  7.7 0.8 constant_dynamic-update-slice_fusion.1
  8.5 0.7 collective-permute-done
  9.3 0.1 constant_dynamic-slice_fusion.3
  9.4 2.6 %collective-permute-start.3 = (bf16[2,16,128]{2,1,0:T(8,128)(2,1)S(1)}, bf16[2,16,128]{2,1,0:T(8,128)(2,1)S(1)}, u32[]{:S(2)}, u32[]{:S(2)}) collective-permute-start(bf16[2,16,128]{2,1,0:T(8,128)(2,1)S(1)} %get-tuple-element.30), channel_id=1, source_target_pairs={{0,3},{1,0},{2,1},{3,2},{4,7},{5,4},{6,5},{7,6},{8,11},{9,8},{10,9... | collective-permute-start | bytes 24584 | tf_op jit(solution)/shard_map/ppermute | solution.py:475
  11.9 0.5 collective-permute-start.2
  12.4 0.6 collective-permute-start.1
  13.0 0.0 collective-permute-done.3
  13.0 2.9 %collective-permute-done.2 = bf16[2,16,128]{2,1,0:T(8,128)(2,1)S(1)} collective-permute-done((bf16[2,16,128]{2,1,0:T(8,128)(2,1)S(1)}, bf16[2,16,128]{2,1,0:T(8,128)(2,1)S(1)}, u32[]{:S(2)}, u32[]{:S(2)}) %collective-permute-start.2) | collective-permute-done | bytes 8224 | tf_op jit(solution)/shard_map/ppermute | solution.py:475
  15.9 0.2 collective-permute-done.1
  16.2 2.8 %collective-permute-start.6 = (bf16[1,2,64,128]{3,2,1,0:T(8,128)(2,1)S(1)}, bf16[1,2,64,128]{3,2,1,0:T(8,128)(2,1)S(1)}, u32[]{:S(2)}, u32[]{:S(2)}) collective-permute-start(bf16[1,2,64,128]{3,2,1,0:T(8,128)(2,1)S(1)} %maximum_bitcast_fusion), channel_id=1, source_target_pairs={{0,192},{8,200},{16,208},{24,216},{32,224},{40,232},{48,240},{56,2... | collective-permute-start | bytes 98312 | tf_op jit(solution)/shard_map/ppermute | solution.py:478
  19.0 0.0 collective-permute-start.5
  19.0 0.3 collective-permute-start.4
  19.3 0.0 copy-start.2
  19.3 1.0 copy-done.2
  20.3 0.9 spread.1
  21.2 0.0 collective-permute-done.6
  21.2 1.5 collective-permute-done.5
  22.7 0.9 collective-permute-done.4
  23.5 4.7 %all-to-all-start = ((bf16[16,2,4,16,128]{4,3,2,1,0:T(8,128)(2,1)}), bf16[16,2,4,16,128]{4,3,2,1,0:T(8,128)(2,1)S(1)}, u32[]{:S(2)}, u32[]{:S(2)}) async-start(bf16[16,2,4,16,128]{4,3,2,1,0:T(8,128)(2,1)} %spread.1), calls=%async_computation | async-start | bytes 1048576 | tf_op jit(solution)/shard_map/all_to_all | solution.py:482
  28.2 2.6 %collective-permute-start.9 = (bf16[4,2,64,128]{3,2,1,0:T(8,128)(2,1)S(1)}, bf16[4,2,64,128]{3,2,1,0:T(8,128)(2,1)S(1)}, u32[]{:S(2)}, u32[]{:S(2)}) collective-permute-start(bf16[4,2,64,128]{3,2,1,0:T(8,128)(2,1)S(1)} %pad_maximum_fusion.1.root_ref), channel_id=1, source_target_pairs={{0,48},{8,56},{16,0},{24,8},{32,16},{40,24},{48,32},{56,40},{64,11... | collective-permute-start | bytes 393224 | tf_op jit(solution)/shard_map/ppermute | solution.py:485
  30.8 0.6 collective-permute-start.8
  31.4 0.6 collective-permute-start.7
  32.0 0.0 copy-done.6
  32.0 0.1 reshape.6
  32.0 0.0 copy-done.3
  32.0 0.0 copy-done.4
  32.0 0.0 copy-done.5
  32.0 0.1 concatenate.15.table_ref
  32.1 0.0 copy-done
  32.1 0.0 copy-done.1
  32.1 5.3 %attend_near.1 = (f32[512,1024]{1,0:T(8,128)}, f32[512,128]{1,0:T(8,128)S(1)}, f32[512,128]{1,0:T(8,128)S(1)}, f32[8,512]{1,0:T(8,128)S(1)}) custom-call(s32[353]{0:T(512)S(1)} %concatenate.15.table_ref, bf16[4,2,64,128]{3,2,1,0:T(8,128)(2,1)S(1)} %pad_maximum_fusion.1.root_ref, bf16[2,512,128]{2,1,0:T(8,128)(2,1)S(1)} %copy-done.1, ...), custom_call_target="tpu_custom_call" | custom-call | tf_op jit(solution)/shard_map/attend_near/pallas_call | solution.py:386
  37.4 0.0 collective-permute-done.9
  37.4 0.0 collective-permute-done.8
  37.5 1.5 collective-permute-done.7
  39.0 0.1 pad_maximum_fusion.mine_ref
  39.0 0.4 all-to-all-done.mine_ref
  39.4 6.6 %collective-permute-start.10 = (bf16[16,2,4,16,128]{4,3,2,1,0:T(8,128)(2,1)S(1)}, bf16[16,2,4,16,128]{4,3,2,1,0:T(8,128)(2,1)S(1)}, u32[]{:S(2)}, u32[]{:S(2)}) collective-permute-start(bf16[16,2,4,16,128]{4,3,2,1,0:T(8,128)(2,1)S(1)} %all-to-all-done.mine_ref), channel_id=1, source_target_pairs={{0,8},{8,0},{16,24},{24,16},{32,40},{40,32},{48,56},{56,48},{64,72... | collective-permute-start | bytes 1572872 | tf_op jit(solution)/shard_map/ppermute | solution.py:488
  46.0 0.0 collective-permute-start.11
  46.0 1.5 collective-permute-done.10.other_ref
  47.5 1.7 select_pieces.1
  49.2 4.7 %all-to-all-start.1 = ((bf16[16,2,2,16,128]{4,3,2,1,0:T(8,128)(2,1)}), bf16[16,2,2,16,128]{4,3,2,1,0:T(8,128)(2,1)S(1)}, u32[]{:S(2)}, u32[]{:S(2)}) async-start(bf16[16,2,2,16,128]{4,3,2,1,0:T(8,128)(2,1)} %select_pieces.1), calls=%async_computation.1 | async-start | bytes 524288 | tf_op jit(solution)/shard_map/all_to_all | solution.py:490
  53.9 0.0 collective-permute-done.11.other_ref
  53.9 9.4 %attend_far.1 = (f32[512,1024]{1,0:T(8,128)}, f32[512,128]{1,0:T(8,128)S(1)}) custom-call(bf16[16,2,64,128]{3,2,1,0:T(8,128)(2,1)S(1)} %pad_maximum_fusion.mine_ref, bf16[16,2,64,128]{3,2,1,0:T(8,128)(2,1)S(1)} %collective-permute-done.11.other_ref, bf16[512,1024]{1,0:T(8,128)(2,1)S(1)} %copy-done, ...), custom_call_target="tpu_custom_call", output_to_operand_aliasing={{0}: (4, {})} | custom-call | tf_op jit(solution)/shard_map/attend_far/pallas_call | solution.py:408
  63.4 0.4 all-to-all-done.1.node_ref
  63.8 129.6 %attend_nodes.1 = (bf16[512,1024]{1,0:T(8,128)(2,1)}, f32[512,1024]{1,0:T(8,128)}) custom-call(bf16[16,2,2,16,128]{4,3,2,1,0:T(8,128)(2,1)S(1)} %all-to-all-done.1.node_ref, f32[512,128]{1,0:T(8,128)S(1)} %get-tuple-element.21.down_ref, f32[8,512]{1,0:T(8,128)S(1)} %get-tuple-element.22.along_ref, ...), custom_call_target="tpu_custom_call", output_to_operand_aliasing={{1}: (8, {})} | custom-call | tf_op jit(solution)/shard_map/attend_nodes/pallas_call | solution.py:426
  (7 shorter events, 0.0 us)
Async XLA Ops:
  0.0 32.1 %copy-start = (bf16[512,1024]{1,0:T(8,128)(2,1)S(1)}, bf16[512,1024]{1,0:T(8,128)(2,1)}, u32[]{:S(2)}) copy-start(bf16[512,1024]{1,0:T(8,128)(2,1)} %q_ref.5) | copy-start | bytes 3145732
  0.0 32.1 %copy-start.1 = (bf16[2,512,128]{2,1,0:T(8,128)(2,1)S(1)}, bf16[2,512,128]{2,1,0:T(8,128)(2,1)}, u32[]{:S(2)}) copy-start(bf16[2,512,128]{2,1,0:T(8,128)(2,1)} %leaf_ref.3) | copy-start | bytes 786436
  0.0 9.3 %collective-permute-start = (bf16[2,8,1024]{2,1,0:T(8,128)(2,1)}, bf16[2,8,1024]{2,1,0:T(8,128)(2,1)S(1)}, u32[]{:S(2)}, u32[]{:S(2)}) collective-permute-start(bf16[2,8,1024]{2,1,0:T(8,128)(2,1)} %param.10), channel_id=1, source_target_pairs={{0,4},{1,5},{2,6},{3,7},{4,0},{5,1},{6,2},{7,3},{8,12},{9,13},{10,... | collective-permute-start | bytes 98312 | tf_op jit(solution)/shard_map/ppermute | solution.py:470
  9.4 3.7 %collective-permute-start.3 = (bf16[2,16,128]{2,1,0:T(8,128)(2,1)S(1)}, bf16[2,16,128]{2,1,0:T(8,128)(2,1)S(1)}, u32[]{:S(2)}, u32[]{:S(2)}) collective-permute-start(bf16[2,16,128]{2,1,0:T(8,128)(2,1)S(1)} %get-tuple-element.30), channel_id=1, source_target_pairs={{0,3},{1,0},{2,1},{3,2},{4,7},{5,4},{6,5},{7,6},{8,11},{9,8},{10,9... | collective-permute-start | bytes 24584 | tf_op jit(solution)/shard_map/ppermute | solution.py:475
  11.9 4.0 %collective-permute-start.2 = (bf16[2,16,128]{2,1,0:T(8,128)(2,1)S(1)}, bf16[2,16,128]{2,1,0:T(8,128)(2,1)S(1)}, u32[]{:S(2)}, u32[]{:S(2)}) collective-permute-start(bf16[2,16,128]{2,1,0:T(8,128)(2,1)S(1)} %get-tuple-element.31), channel_id=1, source_target_pairs={{0,2},{1,3},{2,0},{3,1},{4,6},{5,7},{6,4},{7,5},{8,10},{9,11},{10,... | collective-permute-start | bytes 24584 | tf_op jit(solution)/shard_map/ppermute | solution.py:475
  12.4 3.7 %collective-permute-start.1 = (bf16[2,16,128]{2,1,0:T(8,128)(2,1)S(1)}, bf16[2,16,128]{2,1,0:T(8,128)(2,1)S(1)}, u32[]{:S(2)}, u32[]{:S(2)}) collective-permute-start(bf16[2,16,128]{2,1,0:T(8,128)(2,1)S(1)} %get-tuple-element.32), channel_id=1, source_target_pairs={{0,1},{1,2},{2,3},{3,0},{4,5},{5,6},{6,7},{7,4},{8,9},{9,10},{10,1... | collective-permute-start | bytes 24584 | tf_op jit(solution)/shard_map/ppermute | solution.py:475
  16.2 5.0 %collective-permute-start.6 = (bf16[1,2,64,128]{3,2,1,0:T(8,128)(2,1)S(1)}, bf16[1,2,64,128]{3,2,1,0:T(8,128)(2,1)S(1)}, u32[]{:S(2)}, u32[]{:S(2)}) collective-permute-start(bf16[1,2,64,128]{3,2,1,0:T(8,128)(2,1)S(1)} %maximum_bitcast_fusion), channel_id=1, source_target_pairs={{0,192},{8,200},{16,208},{24,216},{32,224},{40,232},{48,240},{56,2... | collective-permute-start | bytes 98312 | tf_op jit(solution)/shard_map/ppermute | solution.py:478
  19.0 3.7 %collective-permute-start.5 = (bf16[1,2,64,128]{3,2,1,0:T(8,128)(2,1)S(1)}, bf16[1,2,64,128]{3,2,1,0:T(8,128)(2,1)S(1)}, u32[]{:S(2)}, u32[]{:S(2)}) collective-permute-start(bf16[1,2,64,128]{3,2,1,0:T(8,128)(2,1)S(1)} %maximum_bitcast_fusion), channel_id=1, source_target_pairs={{0,128},{8,136},{16,144},{24,152},{32,160},{40,168},{48,176},{56,1... | collective-permute-start | bytes 98312 | tf_op jit(solution)/shard_map/ppermute | solution.py:478
  19.0 4.6 %collective-permute-start.4 = (bf16[1,2,64,128]{3,2,1,0:T(8,128)(2,1)S(1)}, bf16[1,2,64,128]{3,2,1,0:T(8,128)(2,1)S(1)}, u32[]{:S(2)}, u32[]{:S(2)}) collective-permute-start(bf16[1,2,64,128]{3,2,1,0:T(8,128)(2,1)S(1)} %maximum_bitcast_fusion), channel_id=1, source_target_pairs={{0,64},{8,72},{16,80},{24,88},{32,96},{40,104},{48,112},{56,120},{... | collective-permute-start | bytes 98312 | tf_op jit(solution)/shard_map/ppermute | solution.py:478
  19.3 1.0 copy-start.2
  20.3 11.6 %copy-start.6 = (s32[32,2]{0,1:T(2,128)S(1)}, s32[32,2]{0,1:T(2,128)}, u32[]{:S(2)}) copy-start(s32[32,2]{0,1:T(2,128)} %param.15) | copy-start | bytes 772
  20.3 11.7 %copy-start.3 = (s32[32]{0:T(128)S(1)}, s32[32]{0:T(128)}, u32[]{:S(2)}) copy-start(s32[32]{0:T(128)} %param.14) | copy-start | bytes 388
  20.3 11.7 %copy-start.4 = (s32[128]{0:T(128)S(1)}, s32[128]{0:T(128)}, u32[]{:S(2)}) copy-start(s32[128]{0:T(128)} %param.13) | copy-start | bytes 1540
  20.3 11.7 %copy-start.5 = (s32[128]{0:T(128)S(1)}, s32[128]{0:T(128)}, u32[]{:S(2)}) copy-start(s32[128]{0:T(128)} %param.12) | copy-start | bytes 1540
  23.5 15.9 %all-to-all-start = ((bf16[16,2,4,16,128]{4,3,2,1,0:T(8,128)(2,1)}), bf16[16,2,4,16,128]{4,3,2,1,0:T(8,128)(2,1)S(1)}, u32[]{:S(2)}, u32[]{:S(2)}) async-start(bf16[16,2,4,16,128]{4,3,2,1,0:T(8,128)(2,1)} %spread.1), calls=%async_computation | async-start | bytes 1048576 | tf_op jit(solution)/shard_map/all_to_all | solution.py:482
  28.2 9.2 %collective-permute-start.9 = (bf16[4,2,64,128]{3,2,1,0:T(8,128)(2,1)S(1)}, bf16[4,2,64,128]{3,2,1,0:T(8,128)(2,1)S(1)}, u32[]{:S(2)}, u32[]{:S(2)}) collective-permute-start(bf16[4,2,64,128]{3,2,1,0:T(8,128)(2,1)S(1)} %pad_maximum_fusion.1.root_ref), channel_id=1, source_target_pairs={{0,48},{8,56},{16,0},{24,8},{32,16},{40,24},{48,32},{56,40},{64,11... | collective-permute-start | bytes 393224 | tf_op jit(solution)/shard_map/ppermute | solution.py:485
  30.8 6.6 %collective-permute-start.8 = (bf16[4,2,64,128]{3,2,1,0:T(8,128)(2,1)S(1)}, bf16[4,2,64,128]{3,2,1,0:T(8,128)(2,1)S(1)}, u32[]{:S(2)}, u32[]{:S(2)}) collective-permute-start(bf16[4,2,64,128]{3,2,1,0:T(8,128)(2,1)S(1)} %pad_maximum_fusion.1.root_ref), channel_id=1, source_target_pairs={{0,32},{8,40},{16,48},{24,56},{32,0},{40,8},{48,16},{56,24},{64,96... | collective-permute-start | bytes 393224 | tf_op jit(solution)/shard_map/ppermute | solution.py:485
  31.4 7.6 %collective-permute-start.7 = (bf16[4,2,64,128]{3,2,1,0:T(8,128)(2,1)S(1)}, bf16[4,2,64,128]{3,2,1,0:T(8,128)(2,1)S(1)}, u32[]{:S(2)}, u32[]{:S(2)}) collective-permute-start(bf16[4,2,64,128]{3,2,1,0:T(8,128)(2,1)S(1)} %pad_maximum_fusion.1.root_ref), channel_id=1, source_target_pairs={{0,16},{8,24},{16,32},{24,40},{32,48},{40,56},{48,0},{56,8},{64,80... | collective-permute-start | bytes 393224 | tf_op jit(solution)/shard_map/ppermute | solution.py:485
  39.4 8.1 %collective-permute-start.10 = (bf16[16,2,4,16,128]{4,3,2,1,0:T(8,128)(2,1)S(1)}, bf16[16,2,4,16,128]{4,3,2,1,0:T(8,128)(2,1)S(1)}, u32[]{:S(2)}, u32[]{:S(2)}) collective-permute-start(bf16[16,2,4,16,128]{4,3,2,1,0:T(8,128)(2,1)S(1)} %all-to-all-done.mine_ref), channel_id=1, source_target_pairs={{0,8},{8,0},{16,24},{24,16},{32,40},{40,32},{48,56},{56,48},{64,72... | collective-permute-start | bytes 1572872 | tf_op jit(solution)/shard_map/ppermute | solution.py:488
  46.0 7.9 %collective-permute-start.11 = (bf16[16,2,64,128]{3,2,1,0:T(8,128)(2,1)S(1)}, bf16[16,2,64,128]{3,2,1,0:T(8,128)(2,1)S(1)}, u32[]{:S(2)}, u32[]{:S(2)}) collective-permute-start(bf16[16,2,64,128]{3,2,1,0:T(8,128)(2,1)S(1)} %pad_maximum_fusion.mine_ref), channel_id=1, source_target_pairs={{0,8},{8,0},{16,24},{24,16},{32,40},{40,32},{48,56},{56,48},{64,72... | collective-permute-start | bytes 1572872 | tf_op jit(solution)/shard_map/ppermute | solution.py:487
  49.2 14.6 %all-to-all-start.1 = ((bf16[16,2,2,16,128]{4,3,2,1,0:T(8,128)(2,1)}), bf16[16,2,2,16,128]{4,3,2,1,0:T(8,128)(2,1)S(1)}, u32[]{:S(2)}, u32[]{:S(2)}) async-start(bf16[16,2,2,16,128]{4,3,2,1,0:T(8,128)(2,1)} %select_pieces.1), calls=%async_computation.1 | async-start | bytes 524288 | tf_op jit(solution)/shard_map/all_to_all | solution.py:490
